TPU v7x, 128 devices: a whole 4x4x4 slice. The times are simulated.
128 devices in a mesh: seq: 8 (over x_hi, z), res: 16 (over y, x_lo, core).
Axes of the slice: x: 4 (x_hi: 2, x_lo: 2; x = x_hi * 2 + x_lo), y: 4, z: 4, core: 2. Of those that a mesh axis runs over, the one named last changes fastest.
Arguments:
- multiple_alignment_rep: bfloat16 [256, 512, 256], P('seq', 'res'), may hold values from -6 to 6
- pair_rep: bfloat16 [512, 512, 128], P('res'), may hold values from -6 to 6
- aligned_member_valid: int32 [256], replicated, may hold values from 0 to 1
- chain_position_valid: int32 [512], replicated, may hold values from 0 to 1
- horizontal_entry_matrices: bfloat16 [256, 1024], replicated, may hold values from -4 to 4
- horizontal_exit_matrix: bfloat16 [256, 256], replicated, may hold values from -0.375 to 0.375
- bias_proj: bfloat16 [128, 8], replicated, may hold values from -0.5 to 0.5
- vertical_entry_matrices: bfloat16 [256, 1024], replicated, may hold values from -4 to 4
- vertical_exit_matrix: bfloat16 [256, 256], replicated, may hold values from -0.375 to 0.375
- dyadic_projection_matrices: bfloat16 [256, 64], replicated, may hold values from -0.375 to 0.375
- outer_out: bfloat16 [1024, 128], replicated, may hold values from -2.5 to 2.5
- pair_grad: bfloat16 [512, 512, 128], P('res'), may hold values from -6 to 6
Outputs:
- alignment_refreshed: bfloat16 [256, 512, 256], P('seq', 'res')
- couple_delta: bfloat16 [512, 512, 128], P('res')
- refreshed_alignment_cotangent: bfloat16 [256, 512, 256], P('seq', 'res')
All inputs are finite; a program needn't handle non-finite values.
Results may differ from a plain program's by a relative error of at most 0.03.
Values may be sent and summed in bfloat16 or wider, within the bound.
No kernel may reach another device: no remote copies, remote signals or barrier semaphores. Data moves between devices by JAX's collectives and lax.ppermute only.
A program may use at most 256 MiB of HBM per device.

v0:
```python
import jax
import jax.numpy as jnp
from jax import lax
from jax.experimental import pallas as pl
from jax.experimental.pallas import tpu as pltpu
from jax.sharding import PartitionSpec as P

FACTOR_WIDTH = 32
H = 8
HEAD_SIZE = 32
LOG2E = 1.4426950408889634
MASKED = -1000000000.0 * LOG2E
BF16 = jnp.bfloat16
F32 = jnp.float32
NT = (((1,), (1,)), ((), ()))
ROW_UNROLL = 1
COL_STEP = 64
PAIR_UNROLL = 2

VMEM = pl.BlockSpec(memory_space=pltpu.VMEM)
SMEM = pl.BlockSpec(memory_space=pltpu.SMEM)
ORDER = pl.BlockSpec(memory_space=pl.ANY)
ROOM = pltpu.CompilerParams(vmem_limit_bytes=56 * 1024 * 1024)


def lasting(microseconds):
    return pl.CostEstimate(
        flops=0, bytes_accessed=int(microseconds * 3.69e6), transcendentals=0
    )


def nn(left, right):
    return jnp.dot(left, right, preferred_element_type=F32)


def nt(left, right):
    return lax.dot_general(left, right, NT, preferred_element_type=F32)


def standardize(values):
    center = values - jnp.mean(values, -1, keepdims=True)
    spread = jnp.mean(center * center, -1, keepdims=True)
    return center * lax.rsqrt(spread + 1e-05)


def put(ref, rows, values):
    for half in range(2):
        ref[half, rows, :] = values[:, 128 * half : 128 * half + 128]


def take(ref, rows):
    return jnp.concatenate([ref[0, rows, :], ref[1, rows, :]], 1)


def column_of(row):
    return jnp.broadcast_to(row.astype(F32), (8, row.shape[1])).T[:, :1]


def seq_index():
    return lax.axis_index("x_hi"), lax.axis_index("z")


def res_index():
    return lax.axis_index("x_lo"), lax.axis_index("y")


def scale_of(member):
    return 1.0 / jnp.sum(member.astype(F32), keepdims=True)


def bias_kernel(pair_ref, proj_ref, valid_ref, out_ref, turn_s):
    at = pl.program_id(0)
    rows, residues, depth = pair_ref.shape
    line = lax.broadcasted_iota(jnp.int32, (depth, depth), 0)
    lane = lax.broadcasted_iota(jnp.int32, (depth, depth), 1)
    centering = (jnp.where(line == lane, 1.0, 0.0) - 1.0 / depth).astype(BF16)
    live = valid_ref[...] > 0
    proj = proj_ref[...]
    blank = jnp.zeros_like(proj)
    mean = jnp.full_like(proj, 1.0 / depth)
    sides = jnp.concatenate(
        [jnp.concatenate([proj, blank], 1), jnp.concatenate([blank, mean], 1)], 0
    ).astype(BF16)
    center = nn(pair_ref[...].reshape(rows * residues, depth), centering)
    both = jnp.concatenate([center.astype(BF16), (center * center).astype(BF16)], 1)
    for one in range(rows):
        sums = nt(sides, both[one * residues : one * residues + residues])
        bias = sums[:H] * lax.rsqrt(sums[H:] + 1e-05) * LOG2E
        bias = jnp.where(live, bias, MASKED)
        here = pl.ds(pl.multiple_of((at * rows + one) * H, H), H)
        for part in range(residues // 128):
            turn_s[part, here, :] = bias[:, 128 * part : 128 * part + 128]

    @pl.when(at == pl.num_programs(0) - 1)
    def _():
        total = out_ref.shape[0] // H
        for head in range(H):
            for part in range(residues // 128):
                out_ref[total * head : total * head + total, 128 * part : 128 * part + 128] = (
                    turn_s[part, pl.ds(head, total, stride=H), :].astype(BF16)
                )


def pair_bias(pair, proj, valid):
    rows, residues, depth = pair.shape
    step = 4
    return pl.pallas_call(
        bias_kernel,
        grid=(rows // step,),
        in_specs=[
            pl.BlockSpec((step, residues, depth), lambda g: (g, 0, 0)),
            pl.BlockSpec((H, depth), lambda g: (0, 0)),
            pl.BlockSpec((1, residues), lambda g: (0, 0)),
        ],
        out_specs=pl.BlockSpec((rows * H, residues), lambda g: (0, 0)),
        out_shape=jax.ShapeDtypeStruct((rows * H, residues), BF16),
        scratch_shapes=[pltpu.VMEM((residues // 128, rows * H, 128), F32)],
        compiler_params=ROOM,
        cost_estimate=lasting(9),
        name="pair_bias",
    )(pair, proj, valid)


def scores_of(query, keys, side):
    lanes = slice(128 * side, 128 * side + 128)
    lane = lax.broadcasted_iota(jnp.int32, (1, 128), 1) // HEAD_SIZE
    part = query[:, lanes]
    spread = [jnp.where(lane == head, part, 0.0).astype(BF16) for head in range(4)]
    return nt(jnp.concatenate(spread, 0), keys[:, lanes])


def weigh(scores, values, side):
    rows = scores.shape[0] // 4
    lane = lax.broadcasted_iota(jnp.int32, (1, 128), 1) // HEAD_SIZE
    weights = jnp.exp2(scores - jnp.max(scores, -1, keepdims=True))
    scale = 1.0 / jnp.sum(weights, -1, keepdims=True)
    summed = nn(weights.astype(BF16), values[:, 128 * side : 128 * side + 128])
    output = summed[:rows] * scale[:rows]
    for head in range(1, 4):
        here = slice(rows * head, rows * head + rows)
        output = jnp.where(lane == head, summed[here] * scale[here], output)
    return output


def entry_kernel(x_ref, other_ref, valid_ref, w_ref, q_ref, k_ref, v_ref, g_ref, live_s):
    blocks, seqs, rows, depth = x_ref.shape
    core = lax.axis_index("core")
    live_s[...] = jnp.broadcast_to(column_of(valid_ref[...]), live_s.shape)
    for s in range(seqs):
        for other in range(2):
            source = other_ref if other else x_ref
            x = source[:, s].reshape(blocks * rows, depth)
            normed = standardize(x.astype(F32)).astype(BF16)
            pair = nn(normed, w_ref[:, depth : 3 * depth])
            side = 1 - core if other else core
            for at in range(blocks):
                here = slice(rows * at, rows * at + rows)
                to = pl.ds(pl.multiple_of((2 * at + side) * rows, rows), rows)
                k_ref[s, to, :] = (pair[here, :depth] * live_s[to, :1]).astype(BF16)
                v_ref[s, to, :] = pair[here, depth:].astype(BF16)
            if not other:
                query = nn(normed, w_ref[:, :depth]) * (HEAD_SIZE**-0.5 * LOG2E)
                q_ref[s] = query.astype(BF16)
                g_ref[s] = jax.nn.sigmoid(nn(normed, w_ref[:, 3 * depth :])).astype(BF16)


def row_entry(x, other, valid, w):
    blocks, seqs, rows, depth = x.shape
    here = jax.ShapeDtypeStruct((seqs, blocks * rows, depth), BF16)
    full = jax.ShapeDtypeStruct((seqs, 2 * blocks * rows, depth), BF16)
    return pl.pallas_call(
        entry_kernel,
        in_specs=[VMEM] * 4,
        out_specs=[VMEM] * 4,
        out_shape=[here, full, full, here],
        scratch_shapes=[pltpu.VMEM((2 * blocks * rows, 128), F32)],
        compiler_params=ROOM,
        cost_estimate=lasting(5),
        name="row_entry",
    )(x, other, valid, w)


def place(index, pieces, store):
    across, along = index
    for block, piece in enumerate(pieces):
        store((across ^ (block // 4)) * 4 + ((along + block) & 3), piece)


def place_halves(index, pieces, size, store):
    across, along = index
    pieces = list(pieces)
    for block in range(8):
        parts = 2 if block % 4 == 2 else 1
        for part in range(parts):
            at = (across ^ (block // 4)) * 4 + ((along + block) & 3)
            store(at, size // parts * part, size // parts, pieces.pop(0))


def row_kernel(q_ref, k_ref, v_ref, g_ref, x_ref, wo_ref, *refs):
    pieces, (out_ref, bias_s) = refs[:8], refs[8:]
    blocks, seqs, rows, depth = x_ref.shape

    def store(block, piece):
        bias_s[(block % 4) * 2 + block // 4] = piece[...]

    place(res_index(), pieces, store)
    upper = lax.broadcasted_iota(jnp.int32, (rows // 8, 8, depth), 1) < 4

    def block(at, carry):
        here = pl.ds(pl.multiple_of(at * rows, rows), rows)
        scores = {}
        for side in range(2):
            offset = bias_s[at, 4 * rows * side : 4 * rows * side + 4 * rows, :].astype(F32)
            for s in range(seqs):
                scores[s, side] = scores_of(q_ref[s, here, :], k_ref.at[s], side) + offset
        done = []
        for s in range(seqs):
            output = jnp.concatenate(
                [weigh(scores[s, side], v_ref.at[s], side) for side in range(2)], 1
            )
            gated = (g_ref[s, here, :].astype(F32) * output).astype(BF16)
            after = x_ref[at, s].astype(F32) + nn(gated, wo_ref[...])
            done.append(after.reshape(rows // 8, 8, depth))
        even, odd = [], []
        for first, second in zip(done[::2], done[1::2]):
            even.append(jnp.where(upper, first, pltpu.roll(second, 4, 1)))
            odd.append(jnp.where(upper, pltpu.roll(first, 4, 1), second))
        even = jnp.concatenate(even, 1).astype(BF16)
        odd = jnp.concatenate(odd, 1).astype(BF16)
        for pair in range(rows // 8):
            out_ref[2 * pair, at] = even[pair]
            out_ref[2 * pair + 1, at] = odd[pair]
        return carry

    lax.fori_loop(0, blocks, block, 0, unroll=ROW_UNROLL)


def row_attention(q, k, v, g, x, wo, bias):
    blocks, seqs, rows, depth = x.shape
    return pl.pallas_call(
        row_kernel,
        in_specs=[VMEM] * (6 + len(bias)),
        out_specs=VMEM,
        out_shape=jax.ShapeDtypeStruct((rows // 4, blocks, 4 * seqs, depth), BF16),
        scratch_shapes=[pltpu.VMEM((blocks,) + bias[0].shape, BF16)],
        compiler_params=ROOM,
        cost_estimate=lasting(14),
        name="row_attention",
    )(q, k, v, g, x, wo, *bias)


def col_kernel(
    y_ref, valid_ref, chain_ref, w_ref, wo_ref, dyadic_ref, _,
    out_ref, b_ref, y_s, q_s, k_s, v_s, g_s, o_s,
):
    tokens, depth = y_s.shape[1], 2 * y_s.shape[2]
    parts = q_s.shape[0]
    seqs = tokens // parts
    live = valid_ref[...].astype(F32)
    live_column = column_of(live)
    offset = jnp.where(live > 0, 0.0, MASKED)
    x_hi, z = seq_index()
    x_lo, y_at = res_index()
    first = ((y_at * 2 + x_lo) * 2 + lax.axis_index("core")) * 32 + (x_hi * 4 + z) * parts
    put(y_s, slice(None), y_ref[...].reshape(tokens, depth).astype(F32))
    for at in range(parts):
        y = take(y_s, pl.ds(at, seqs, stride=parts))
        mixed = nn(standardize(y).astype(BF16), w_ref[...])
        q_s[at] = mixed[:, :depth] * (HEAD_SIZE**-0.5 * LOG2E)
        k_s[at] = (mixed[:, depth : 2 * depth] * live_column).astype(BF16)
        v_s[at] = mixed[:, 2 * depth : 3 * depth].astype(BF16)
        g_s[at] = jax.nn.sigmoid(mixed[:, 3 * depth :])
    step = COL_STEP

    def block(part, carry):
        here = pl.ds(pl.multiple_of(part * step, step), step)
        scores = [
            [scores_of(q_s[at, here, :], k_s[at], side) + offset for side in range(2)]
            for at in range(parts)
        ]
        for at in range(parts):
            output = jnp.concatenate(
                [weigh(scores[at][side], v_s[at], side) for side in range(2)], 1
            )
            o_s[at, here, :] = (g_s[at, here, :] * output).astype(BF16)
        return carry

    lax.fori_loop(0, seqs // step, block, 0)
    for at in range(parts):
        y = take(y_s, pl.ds(at, seqs, stride=parts))
        done = (y + nn(o_s[at], wo_ref[...])).astype(BF16)
        groups = out_ref.shape[0]
        here = slice(seqs // groups * at, seqs // groups * at + seqs // groups)
        out_ref[:, here, :] = done.reshape(groups, seqs // groups, depth)
        normed = standardize(done.astype(F32)).astype(BF16)
        factors = nt(dyadic_ref[...], normed) * (live * chain_ref[first + at].astype(F32))
        for group in range(groups):
            to = slice(128 + 32 * at, 160 + 32 * at)
            out_ref[group, to, :] = factors[:32].astype(BF16)
        b_ref[pl.ds(32 * at, 32), :] = factors[32:].astype(BF16)


def col_attention(y, valid, chain, w, wo, dyadic_t, groups, after):
    sources, eight, depth = y.shape
    tokens = sources * eight
    seqs = tokens // 4
    return pl.pallas_call(
        col_kernel,
        in_specs=[VMEM] * 2 + [SMEM] + [VMEM] * 3 + [ORDER],
        out_specs=[VMEM] * 2,
        out_shape=[
            jax.ShapeDtypeStruct((groups, 2 * 4 * FACTOR_WIDTH, seqs), BF16),
            jax.ShapeDtypeStruct((4 * FACTOR_WIDTH, seqs), BF16),
        ],
        scratch_shapes=[
            pltpu.VMEM((2, tokens, depth // 2), F32),
            pltpu.VMEM((4, seqs, depth), F32),
            pltpu.VMEM((4, seqs, depth), BF16),
            pltpu.VMEM((4, seqs, depth), BF16),
            pltpu.VMEM((4, seqs, depth), F32),
            pltpu.VMEM((4, seqs, depth), BF16),
        ],
        compiler_params=ROOM,
        cost_estimate=lasting(8),
        name="col_attention",
    )(y, valid, chain, w, wo, dyadic_t, after)


def assemble_kernel(*refs):
    pieces, (out_ref, d_s) = refs[:10], refs[10:]
    step = out_ref.shape[0]
    at = pl.program_id(0)

    def store(block, start, size, piece):
        d_s[block, start : start + size] = piece[...]

    @pl.when(at == 0)
    def _():
        place_halves(seq_index(), pieces, d_s.shape[1], store)

    upper = lax.broadcasted_iota(jnp.int32, (8, 8, 128), 1) < 4

    def line(one, carry):
        even, odd = [], []
        for pair in range(4):
            first = d_s[2 * pair, at * step + one].astype(F32).reshape(8, 8, 128)
            second = d_s[2 * pair + 1, at * step + one].astype(F32).reshape(8, 8, 128)
            even.append(jnp.where(upper, first, pltpu.roll(second, 4, 1)))
            odd.append(jnp.where(upper, pltpu.roll(first, 4, 1), second))
        both = jnp.stack([jnp.stack(even, 1), jnp.stack(odd, 1)], 1)
        out_ref[one] = both.reshape(512, 128).astype(BF16)
        return carry

    lax.fori_loop(0, step, line, 0, unroll=2)


def assemble(pieces):
    rows, columns, depth = pieces[0].shape
    step = 8
    return pl.pallas_call(
        assemble_kernel,
        grid=(rows // step,),
        in_specs=[VMEM] * len(pieces),
        out_specs=pl.BlockSpec((step, 8 * columns, depth), lambda g: (g, 0, 0)),
        out_shape=jax.ShapeDtypeStruct((rows, 8 * columns, depth), BF16),
        scratch_shapes=[pltpu.VMEM((8, rows, columns, depth), BF16)],
        compiler_params=ROOM,
        cost_estimate=lasting(5),
        name="assemble",
    )(*pieces)


def spread_kernel(g_ref, w_ref, member_ref, _, out_ref):
    width = FACTOR_WIDTH
    scale = scale_of(member_ref[...])
    blank = jnp.zeros((64, 128), BF16)

    def pair(at, carry):
        parts = []
        for one in range(2):
            given = g_ref[2 * at + one]
            parts.append(jnp.concatenate([given, blank], 1))
            parts.append(jnp.concatenate([blank, given], 1))
        both = (nt(w_ref[...], jnp.concatenate(parts, 0)) * scale).astype(BF16)
        for one in range(2):
            here = pl.ds(pl.multiple_of((2 * at + one) * width, width), width)
            out_ref[here, :] = jnp.concatenate(
                [
                    both[width * e : width * e + width, 128 * one : 128 * one + 128]
                    for e in range(16)
                ],
                1,
            )
        return carry

    lax.fori_loop(0, g_ref.shape[0] // 2, pair, 0)


def spread_of(given, w, member, after):
    rows, columns, _ = given.shape
    return pl.pallas_call(
        spread_kernel,
        in_specs=[VMEM] * 3 + [ORDER],
        out_specs=VMEM,
        out_shape=jax.ShapeDtypeStruct((rows * FACTOR_WIDTH, columns * FACTOR_WIDTH), BF16),
        compiler_params=ROOM,
        cost_estimate=lasting(8),
        name="spread",
    )(given, w, member, after)


def couple_kernel(both_ref, w_ref, member_ref, b_ref, out_ref, a_ref, bd_ref, o_s, b_s):
    width = FACTOR_WIDTH
    rows, columns = o_s.shape
    put(b_s, slice(None), b_ref[...].reshape(columns, b_ref.shape[2]).astype(F32))
    count = columns // width
    for at in range(width):
        here = slice(at * count, at * count + count)
        bd_ref[here, :] = take(b_s, pl.ds(at, count, stride=width)).astype(BF16)
    a_ref[...] = both_ref[:, 128:].reshape(a_ref.shape)
    for at in range(columns // 256):
        here = slice(256 * at, 256 * at + 256)
        o_s[:, here] = nt(a_ref[...], bd_ref[here, :]).astype(BF16)
    scale = scale_of(member_ref[...])
    w = w_ref[...].astype(F32).T.astype(BF16)
    low = lax.broadcasted_iota(jnp.int32, (128, 128), 1) < 64

    def pair(at, carry):
        outer = o_s[pl.ds(pl.multiple_of(at * 2 * width, 2 * width), 2 * width), :]
        stacks = []
        for one in range(2):
            part = outer[width * one : width * one + width]
            stacks.append(
                jnp.concatenate([part[:, 128 * e : 128 * e + 128] for e in range(16)], 0)
            )
        both = nn(w, jnp.concatenate(stacks, 1))
        top = jnp.where(low, both[:128, :128], pltpu.roll(both[:128, 128:], 64, 1))
        bottom = jnp.where(low, pltpu.roll(both[128:, :128], 64, 1), both[128:, 128:])
        delta = ((top + bottom) * scale).T
        out_ref[pl.ds(at * 2, 2)] = delta.reshape(2, 64, 128).astype(BF16)
        return carry

    lax.fori_loop(0, rows // (2 * width), pair, 0, unroll=PAIR_UNROLL)


def couple(both, w, member, b_all):
    seqs = both.shape[2]
    rows, columns = both.shape[0] * 128, b_all.shape[0] * 128
    return pl.pallas_call(
        couple_kernel,
        in_specs=[VMEM] * 4,
        out_specs=[VMEM] * 3,
        out_shape=[
            jax.ShapeDtypeStruct((rows // FACTOR_WIDTH, columns // FACTOR_WIDTH, 128), BF16),
            jax.ShapeDtypeStruct((rows, seqs), BF16),
            jax.ShapeDtypeStruct((columns, seqs), BF16),
        ],
        scratch_shapes=[
            pltpu.VMEM((rows, columns), BF16),
            pltpu.VMEM((2, columns, seqs // 2), F32),
        ],
        compiler_params=ROOM,
        cost_estimate=lasting(9),
        name="couple",
    )(both, w, member, b_all)


def grad_a_kernel(bd_ref, s_ref, *refs):
    out_ref = refs[-1]
    for at in range(4):
        here = slice(256 * at, 256 * at + 256)
        out_ref[:, here] = nn(s_ref[here, :], bd_ref[...]).T.astype(BF16)


def grad_a_of(bd, spread, after):
    return pl.pallas_call(
        grad_a_kernel,
        in_specs=[VMEM] * 2 + [ORDER] * len(after),
        out_specs=VMEM,
        out_shape=jax.ShapeDtypeStruct((bd.shape[1], spread.shape[0]), BF16),
        compiler_params=ROOM,
        cost_estimate=lasting(4),
        name="grad_a",
    )(bd, spread, *after)


def grad_b_kernel(a_ref, s_ref, *refs):
    out_ref, turned_s = refs[-2:]
    width = FACTOR_WIDTH
    columns = out_ref.shape[0] // width
    left = a_ref[...].astype(F32).T.astype(BF16)
    for at in range(columns * width // 256):
        here = slice(256 * at, 256 * at + 256)
        put(turned_s, here, nn(left, s_ref[:, here]).T)
    for at in range(columns):
        to = slice(at * width, at * width + width)
        out_ref[to, :] = take(turned_s, pl.ds(at, width, stride=columns)).astype(BF16)


def grad_b_of(a_all, spread, after):
    seqs, columns = a_all.shape[1], spread.shape[1]
    return pl.pallas_call(
        grad_b_kernel,
        in_specs=[VMEM] * 2 + [ORDER] * len(after),
        out_specs=VMEM,
        out_shape=jax.ShapeDtypeStruct((columns, seqs), BF16),
        scratch_shapes=[pltpu.VMEM((2, columns, seqs // 2), F32)],
        compiler_params=ROOM,
        cost_estimate=lasting(5),
        name="grad_b",
    )(a_all, spread, *after)


def pack_kernel(ga_ref, gb_ref, out_ref):
    groups, members, _ = out_ref.shape
    wide = ga_ref.shape[1]
    total = gb_ref[0].astype(F32)
    for at in range(1, gb_ref.shape[0]):
        total = total + gb_ref[at].astype(F32)
    out_ref[:, :, :wide] = ga_ref[...].reshape(groups, members, wide)
    out_ref[:, :, wide:] = total.T.reshape(groups, members, total.shape[0]).astype(BF16)


def pack_grads(ga, gb, groups):
    seqs, wide = ga.shape
    return pl.pallas_call(
        pack_kernel,
        in_specs=[VMEM] * 2,
        out_specs=VMEM,
        out_shape=jax.ShapeDtypeStruct((groups, seqs // groups, wide + gb.shape[1]), BF16),
        compiler_params=ROOM,
        cost_estimate=lasting(3),
        name="pack_grads",
    )(ga, gb)


def home_kernel(gf_ref, w_ref, x_ref, member_ref, chain_ref, x_out_ref, ct_ref, x_s, ct_s):
    width = FACTOR_WIDTH
    groups, rows, depth = x_ref.shape
    parts = 4
    seqs = rows // 2 // parts
    residues = groups * parts
    wide = residues * width
    x_hi, z = seq_index()
    x_lo, y = res_index()
    first = ((y * 2 + x_lo) * 2 + lax.axis_index("core")) * residues
    member = member_ref[pl.ds(x_hi * 4 + z, 1), :]
    member = jnp.broadcast_to(member.astype(F32), (8, member.shape[1])).T[:seqs, :1]
    total = gf_ref[0, :, :wide].astype(F32)
    for at in range(1, groups):
        total = total + gf_ref[at, :, :wide].astype(F32)
    lane = lax.broadcasted_iota(jnp.int32, (1, 128), 1) // width
    lines = []
    for group in range(groups):
        live = jnp.zeros((1, 128), F32)
        for at in range(parts):
            here = chain_ref[first + group * parts + at].astype(F32)
            live = jnp.where(lane == at, here, live)
        live = live * member
        left = total[:, 128 * group : 128 * group + 128] * live
        right = gf_ref[group, :, wide:].astype(F32) * live
        lines.append(jnp.concatenate([left, right], 1))
    given = jnp.concatenate(lines, 0)
    lane = lax.broadcasted_iota(jnp.int32, (1, depth), 1) // width % parts
    back = jnp.concatenate([w_ref[:width, :]] * parts + [w_ref[width:, :]] * parts, 0)
    for at in range(parts):
        upstream = nn(jnp.where(lane == at, given, 0.0).astype(BF16), back)
        x = x_ref[:, seqs * at : seqs * at + seqs]
        x = x.reshape(groups * seqs, depth).astype(F32)
        center = x - jnp.mean(x, -1, keepdims=True)
        inverse = lax.rsqrt(jnp.mean(center * center, -1, keepdims=True) + 1e-05)
        scaled = center * inverse
        cotangent = inverse * (
            upstream
            - jnp.mean(upstream, -1, keepdims=True)
            - scaled * jnp.mean(upstream * scaled, -1, keepdims=True)
        )
        for group in range(groups):
            here = pl.ds(group * parts + at, seqs, stride=residues)
            put(x_s, here, x[group * seqs : group * seqs + seqs])
            put(ct_s, here, cotangent[group * seqs : group * seqs + seqs])
    x_out_ref[...] = take(x_s, slice(None)).reshape(seqs, residues, depth).astype(BF16)
    ct_ref[...] = take(ct_s, slice(None)).reshape(seqs, residues, depth).astype(BF16)


def finish_home(gf, w, both, member, chain):
    groups, rows, depth = both.shape
    seqs, residues = rows // 8, groups * 4
    shape = (seqs, residues, depth)
    return pl.pallas_call(
        home_kernel,
        in_specs=[VMEM] * 4 + [SMEM],
        out_specs=[VMEM] * 2,
        out_shape=[jax.ShapeDtypeStruct(shape, BF16)] * 2,
        scratch_shapes=[pltpu.VMEM((2, seqs * residues, depth // 2), F32)] * 2,
        compiler_params=ROOM,
        cost_estimate=lasting(6),
        name="finish_home",
    )(gf, w, both, member, chain)


def hold_kernel(*refs):
    pass


def hold(arrays, after):
    count = len(arrays)
    return pl.pallas_call(
        hold_kernel,
        in_specs=[ORDER] * (count + 1),
        out_specs=[ORDER] * count,
        out_shape=[jax.ShapeDtypeStruct(one.shape, one.dtype) for one in arrays],
        input_output_aliases={at: at for at in range(count)},
        cost_estimate=lasting(0.1),
        name="hold",
    )(*arrays, after)


def turn_by(steps):
    return [(at, (at + steps) % 4) for at in range(4)]


SWAP = [(0, 1), (1, 0)]


def ring(x, along, across, after=None):
    partner = lax.ppermute(x, across, SWAP)
    below = lax.ppermute(x, along, turn_by(1))
    above = lax.ppermute(x, along, turn_by(3))
    far = lax.ppermute(x, along, turn_by(2))
    if after is not None:
        partner, far = hold([partner, far], after)
    partner_below = lax.ppermute(partner, along, turn_by(1))
    partner_above = lax.ppermute(partner, along, turn_by(3))
    partner_far = lax.ppermute(far, across, SWAP)
    return [x, above, far, below, partner, partner_above, partner_far, partner_below]


def ring_halves(x, along, across):
    half = x.shape[0] // 2
    partner = lax.ppermute(x, across, SWAP)
    below = lax.ppermute(x, along, turn_by(1))
    above = lax.ppermute(x, along, turn_by(3))
    far_low = lax.ppermute(below[:half], along, turn_by(1))
    far_high = lax.ppermute(above[half:], along, turn_by(3))
    partner_below = lax.ppermute(partner, along, turn_by(1))
    partner_above = lax.ppermute(partner, along, turn_by(3))
    partner_low = lax.ppermute(far_low, across, SWAP)
    partner_high = lax.ppermute(far_high, across, SWAP)
    return [
        x, above, far_low, far_high, below,
        partner, partner_above, partner_low, partner_high, partner_below,
    ]


def per_device(
    multiple_alignment_rep,
    pair_rep,
    aligned_member_valid,
    chain_position_valid,
    horizontal_entry_matrices,
    horizontal_exit_matrix,
    bias_proj,
    vertical_entry_matrices,
    vertical_exit_matrix,
    dyadic_projection_matrices,
    outer_out,
    pair_grad,
):
    seqs_here, res_here, depth = multiple_alignment_rep.shape
    residues = pair_rep.shape[1]
    pair_width = outer_out.shape[1]
    q_size, b_size, r_size = 8, 8, 16
    width = FACTOR_WIDTH
    q_at = lax.axis_index("x_hi") * 4 + lax.axis_index("z")
    member = aligned_member_valid.reshape(1, -1)
    chain_row = chain_position_valid.reshape(1, residues)

    dyadic_t = dyadic_projection_matrices.T
    cube = outer_out.reshape(width, width // 2, 2, pair_width)
    w_outer = cube.transpose(1, 0, 2, 3).reshape(16 * width, 2 * pair_width)
    grad_here = lax.dynamic_index_in_dim(
        pair_grad.reshape(res_here, r_size, q_size, 4, pair_width), q_at, 2, keepdims=False
    ).reshape(res_here, r_size * 4, pair_width)

    bias = pair_bias(pair_rep, bias_proj.astype(F32).T, chain_row)
    x_rows = lax.all_to_all(
        multiple_alignment_rep.reshape(b_size, seqs_here // b_size, res_here, depth),
        ("y", "x_lo"), 0, 0, tiled=True,
    )
    (x_rows,) = hold([x_rows], bias)
    x_other = lax.ppermute(x_rows, "core", SWAP)
    q, k, v, g = row_entry(x_rows, x_other, chain_row, horizontal_entry_matrices)
    bias_pieces = ring(bias, "y", "x_lo", after=q)
    after_row = row_attention(q, k, v, g, x_rows, horizontal_exit_matrix, bias_pieces)

    spread = spread_of(grad_here, w_outer, member, after_row)
    columns = lax.all_to_all(
        after_row.reshape(q_size * b_size, 16, depth),
        ("x_hi", "z", "y", "x_lo"), 0, 0, tiled=True,
    )
    going, factor_b = col_attention(
        columns, member, chain_position_valid,
        vertical_entry_matrices, vertical_exit_matrix, dyadic_t, q_size, spread,
    )
    b_all = lax.all_gather(factor_b, ("y", "x_lo", "core"), axis=0)
    back = lax.all_to_all(going, ("x_hi", "z"), 0, 0, tiled=True)

    delta, a_all, bd = couple(back, w_outer, member, b_all)
    deltas = ring_halves(delta, "z", "x_hi")
    gb = grad_b_of(a_all, spread, [delta])
    gb = lax.all_to_all(
        gb.reshape(r_size, 4 * width, -1), ("y", "x_lo", "core"), 0, 0, tiled=True
    )
    ga = grad_a_of(bd, spread, [deltas[1], deltas[4], deltas[5]])
    couple_delta = assemble(deltas)
    factors = lax.all_to_all(pack_grads(ga, gb, q_size), ("x_hi", "z"), 0, 0, tiled=True)
    alignment_refreshed, cotangent = finish_home(
        factors, dyadic_t, back, member.reshape(q_size, seqs_here), chain_position_valid
    )
    return (alignment_refreshed, couple_delta, cotangent)


def solution(mesh):
    torus = jax.sharding.Mesh(
        mesh.devices.reshape(2, 4, 4, 2, 2), ("x_hi", "z", "y", "x_lo", "core")
    )
    seq, res = ("x_hi", "z"), ("y", "x_lo", "core")
    placed = (
        P(seq, res, None),
        P(res, None, None),
        P(),
        P(),
        P(),
        P(),
        P(),
        P(),
        P(),
        P(),
        P(),
        P(res, None, None),
    )
    return jax.shard_map(
        per_device,
        mesh=torus,
        in_specs=placed,
        out_specs=(P(seq, res, None), P(res, None, None), P(seq, res, None)),
        check_vma=False,
    )
```

profile of v0, /device:TPU:0, one launch (start us, length us, event | category | flops | bytes accessed | tf_op | source)
XLA Modules:
  0.0 230.8 jit_solution(9249738756658055834)
XLA Ops:
  7.2 5.5 %all-to-all-start = ((bf16[8,4,32,256]{3,2,1,0:T(8,128)(2,1)}), bf16[8,4,32,256]{3,2,1,0:T(8,128)(2,1)S(1)}, u32[]{:S(2)}, u32[]{:S(2)}) async-start(bf16[8,4,32,256]{3,2,1,0:T(8,128)(2,1)} %bitcast.27), calls=%async_computation | async-start | bytes 1048576 | tf_op jit(solution)/shard_map/all_to_all | solution.py:687
  13.9 8.5 %pair_bias.1.refs_1_.refs_0_ = bf16[256,512]{1,0:T(8,128)(2,1)} custom-call(bf16[32,512,128]{2,1,0:T(8,128)(2,1)} %pair_ref.1, f32[8,128]{1,0:T(8,128)} %convert_bitcast_fusion.proj_ref, s32[1,512]{1,0:T(1,128)} %bitcast.32), custom_call_target="tpu_custom_call" | custom-call | bytes 33210000 | tf_op jit(solution)/shard_map/pair_bias/pallas_call | solution.py:107
  25.2 3.0 %collective-permute-start.3 = (bf16[256,512]{1,0:T(8,128)(2,1)}, bf16[256,512]{1,0:T(8,128)(2,1)S(1)}, u32[]{:S(2)}, u32[]{:S(2)}) collective-permute-start(bf16[256,512]{1,0:T(8,128)(2,1)} %pair_bias.1.refs_1_.refs_0_), channel_id=1, source_target_pairs={{0,8},{4,12},{8,0},{12,4},{1,9},{5,13},{9,1},{13,5},{2,10},{6,14},... | collective-permute-start | bytes 786440 | tf_op jit(solution)/shard_map/ppermute | solution.py:630
  31.0 4.9 %row_entry.1 = (bf16[4,256,256]{2,1,0:T(8,128)(2,1)}, bf16[4,512,256]{2,1,0:T(8,128)(2,1)}, bf16[4,512,256]{2,1,0:T(8,128)(2,1)}, bf16[4,256,256]{2,1,0:T(8,128)(2,1)}) custom-call(bf16[8,4,32,256]{3,2,1,0:T(8,128)(2,1)} %hold.2.x_ref, bf16[8,4,32,256]{3,2,1,0:T(8,128)(2,1)} %copy-done.12, s32[1,512]{1,0:T(1,128)} %bitcast.33, bf16[256,1024]{1,0:T(8,128)(2,1)} %w_ref.2), custom_call_target="tpu_custom_call" | custom-call | bytes 18450000 | tf_op jit(solution)/shard_map/row_entry/pallas_call | solution.py:171
  41.8 4.9 %collective-permute-done.5.refs_5_ = bf16[256,512]{1,0:T(8,128)(2,1)S(1)} collective-permute-done((bf16[256,512]{1,0:T(8,128)(2,1)}, bf16[256,512]{1,0:T(8,128)(2,1)S(1)}, u32[]{:S(2)}, u32[]{:S(2)}) %collective-permute-start.5) | collective-permute-done | bytes 262176 | tf_op jit(solution)/shard_map/ppermute | solution.py:634
  48.8 14.4 %row_attention.1._ = bf16[8,8,16,256]{3,2,1,0:T(8,128)(2,1)} custom-call(bf16[4,256,256]{2,1,0:T(8,128)(2,1)} %get-tuple-element.16.refs_2_.q_ref, bf16[4,512,256]{2,1,0:T(8,128)(2,1)} %get-tuple-element.17.k_ref, bf16[4,512,256]{2,1,0:T(8,128)(2,1)} %get-tuple-element.18.v_ref, bf16[4,256,256]{2,1,0:T(8,128)(2,1)} %get-tuple-element.19.g_ref, ...), custom_call_target="tpu_custom_call" | custom-call | bytes 51660000 | tf_op jit(solution)/shard_map/row_attention/pallas_call | solution.py:240
  63.2 9.4 %all-to-all-start.1 = ((bf16[64,16,256]{2,1,0:T(8,128)(2,1)}), bf16[64,16,256]{2,1,0:T(8,128)(2,1)S(1)}, u32[]{:S(2)}, u32[]{:S(2)}) async-start(bf16[64,16,256]{2,1,0:T(8,128)(2,1)} %bitcast.20), calls=%async_computation.1 | async-start | bytes 1048576 | tf_op jit(solution)/shard_map/all_to_all | solution.py:698
  75.7 7.6 %spread.1._.s_ref = bf16[1024,2048]{1,0:T(8,128)(2,1)} custom-call(bf16[32,64,128]{2,1,0:T(8,128)(2,1)} %bitcast.24, bf16[512,256]{1,0:T(8,128)(2,1)} %bitcast.22, s32[1,256]{1,0:T(1,128)} %bitcast.34, bf16[8,8,16,256]{3,2,1,0:T(8,128)(2,1)} %row_attention.1._), custom_call_target="tpu_custom_call" | custom-call | bytes 29520000 | tf_op jit(solution)/shard_map/spread/pallas_call | solution.py:401
  85.7 8.0 %col_attention.1 = (bf16[8,256,256]{2,1,0:T(8,128)(2,1)}, bf16[128,256]{1,0:T(8,128)(2,1)}) custom-call(bf16[64,16,256]{2,1,0:T(8,128)(2,1)} %copy-done.7, s32[1,256]{1,0:T(1,128)} %bitcast.35, s32[512]{0:T(512)} %chain_ref.3, bf16[256,1024]{1,0:T(8,128)(2,1)} %w_ref.3, bf16[256,256]{1,0:T(8,128)(2,1)} %wo_ref.3, bf16[64,256]{1,0:T(8,128)(2,1)} %bitcast.29, ...), custom_call_target="tpu_custom_call" | custom-call | bytes 29520000 | tf_op jit(solution)/shard_map/col_attention/pallas_call | solution.py:307
  93.8 23.6 %all_to_all.25.both_ref.x_ref = bf16[8,256,256]{2,1,0:T(8,128)(2,1)} all-to-all(bf16[8,256,256]{2,1,0:T(8,128)(2,1)} %get-tuple-element.22), channel_id=1, replica_groups=mesh['x_hi'=2,'z'=4,'y'=4,'x_lo'=2,'core'=2] {'x_hi','z'}, dimensions={0} | all-to-all | bytes 2097152 | tf_op jit(solution)/shard_map/all_to_all | solution.py:707
  117.4 8.9 %all-gather.3.cloned.1.call-done = bf16[2048,256]{1,0:T(8,128)(2,1)} async-done(((bf16[128,256]{1,0:T(8,128)(2,1)}), bf16[2048,256]{1,0:T(8,128)(2,1)}) %all-gather.3.cloned.1.call-update) | async-done | bytes 1048592 | tf_op jit(solution)/shard_map/all_gather | solution.py:706
  126.3 9.1 %couple.1 = (bf16[32,64,128]{2,1,0:T(8,128)(2,1)}, bf16[1024,256]{1,0:T(8,128)(2,1)}, bf16[2048,256]{1,0:T(8,128)(2,1)}) custom-call(bf16[8,256,256]{2,1,0:T(8,128)(2,1)} %all_to_all.25.both_ref.x_ref, bf16[512,256]{1,0:T(8,128)(2,1)} %bitcast.23, s32[1,256]{1,0:T(1,128)} %bitcast.36, bf16[16,128,256]{2,1,0:T(8,128)(2,1)} %bitcast.25), custom_call_target="tpu_custom_call" | custom-call | bytes 33210000 | tf_op jit(solution)/shard_map/couple/pallas_call | solution.py:449
  135.4 5.9 %grad_b.1 = bf16[2048,256]{1,0:T(8,128)(2,1)} custom-call(bf16[1024,256]{1,0:T(8,128)(2,1)} %get-tuple-element.26.a_ref, bf16[1024,2048]{1,0:T(8,128)(2,1)} %spread.1._.s_ref, bf16[32,64,128]{2,1,0:T(8,128)(2,1)} %get-tuple-element.25.refs_0_), custom_call_target="tpu_custom_call" | custom-call | bytes 18450000 | tf_op jit(solution)/shard_map/grad_b/pallas_call | solution.py:502
  141.3 4.5 %all-to-all-start.3 = ((bf16[16,128,256]{2,1,0:T(8,128)(2,1)}), bf16[16,128,256]{2,1,0:T(8,128)(2,1)S(1)}, u32[]{:S(2)}, u32[]{:S(2)}) async-start(bf16[16,128,256]{2,1,0:T(8,128)(2,1)} %bitcast.21), calls=%async_computation.3 | async-start | bytes 2097152 | tf_op jit(solution)/shard_map/all_to_all | solution.py:712
  151.8 9.5 %collective-permute-done.9.refs_1_.refs_4_ = bf16[32,64,128]{2,1,0:T(8,128)(2,1)S(1)} collective-permute-done((bf16[32,64,128]{2,1,0:T(8,128)(2,1)S(1)}, bf16[32,64,128]{2,1,0:T(8,128)(2,1)S(1)}, u32[]{:S(2)}, u32[]{:S(2)}) %collective-permute-start.9) | collective-permute-done | bytes 524320 | tf_op jit(solution)/shard_map/ppermute | solution.py:642
  162.4 10.4 %collective-permute-done.10.refs_2_.refs_5_ = bf16[32,64,128]{2,1,0:T(8,128)(2,1)S(1)} collective-permute-done((bf16[32,64,128]{2,1,0:T(8,128)(2,1)S(1)}, bf16[32,64,128]{2,1,0:T(8,128)(2,1)S(1)}, u32[]{:S(2)}, u32[]{:S(2)}) %collective-permute-start.10) | collective-permute-done | bytes 524320 | tf_op jit(solution)/shard_map/ppermute | solution.py:641
  176.5 3.2 %collective-permute-start.12 = (bf16[16,64,128]{2,1,0:T(8,128)(2,1)}, bf16[16,64,128]{2,1,0:T(8,128)(2,1)S(1)}, u32[]{:S(2)}, u32[]{:S(2)}) collective-permute-start(bf16[16,64,128]{2,1,0:T(8,128)(2,1)} %slice.9), channel_id=1, source_target_pairs={{0,48},{16,0},{32,16},{48,32},{1,49},{17,1},{33,17},{49,33},{2,50}... | collective-permute-start | bytes 786440 | tf_op jit(solution)/shard_map/ppermute | solution.py:645
  179.7 4.7 %grad_a.1.ga_ref = bf16[256,1024]{1,0:T(8,128)(2,1)} custom-call(bf16[2048,256]{1,0:T(8,128)(2,1)} %get-tuple-element.24.bd_ref, bf16[1024,2048]{1,0:T(8,128)(2,1)} %spread.1._.s_ref, bf16[32,64,128]{2,1,0:T(8,128)(2,1)} %copy-done.3, bf16[32,64,128]{2,1,0:T(8,128)(2,1)} %copy-done.2, bf16[32,64,128]{2,1,0:T(8,128)(2,1)} %copy-done.5), custom_call_target="tpu_custom_call" | custom-call | bytes 14760000 | tf_op jit(solution)/shard_map/grad_a/pallas_call | solution.py:476
  187.8 3.5 %all-to-all-start.4 = ((bf16[8,32,1152]{2,1,0:T(8,128)(2,1)}), bf16[8,32,1152]{2,1,0:T(8,128)(2,1)S(1)}, u32[]{:S(2)}, u32[]{:S(2)}) async-start(bf16[8,32,1152]{2,1,0:T(8,128)(2,1)} %pack_grads.1), calls=%async_computation.4 | async-start | bytes 1179648 | tf_op jit(solution)/shard_map/all_to_all | solution.py:717
  191.4 3.5 %collective-permute-start.14 = (bf16[16,64,128]{2,1,0:T(8,128)(2,1)S(1)}, bf16[16,64,128]{2,1,0:T(8,128)(2,1)S(1)}, u32[]{:S(2)}, u32[]{:S(2)}) collective-permute-start(bf16[16,64,128]{2,1,0:T(8,128)(2,1)S(1)} %collective-permute-done.11.refs_2_), channel_id=1, source_target_pairs={{0,64},{64,0},{1,65},{65,1},{2,66},{66,2},{3,67},{67,3},{4,68},{68... | collective-permute-start | bytes 786440 | tf_op jit(solution)/shard_map/ppermute | solution.py:648
  195.9 12.6 %collective-permute-done.14.refs_7_ = bf16[16,64,128]{2,1,0:T(8,128)(2,1)S(1)} collective-permute-done((bf16[16,64,128]{2,1,0:T(8,128)(2,1)S(1)}, bf16[16,64,128]{2,1,0:T(8,128)(2,1)S(1)}, u32[]{:S(2)}, u32[]{:S(2)}) %collective-permute-start.14) | collective-permute-done | bytes 262176 | tf_op jit(solution)/shard_map/ppermute | solution.py:648
  208.5 3.7 %collective-permute-done.15.refs_8_ = bf16[16,64,128]{2,1,0:T(8,128)(2,1)S(1)} collective-permute-done((bf16[16,64,128]{2,1,0:T(8,128)(2,1)S(1)}, bf16[16,64,128]{2,1,0:T(8,128)(2,1)S(1)}, u32[]{:S(2)}, u32[]{:S(2)}) %collective-permute-start.15) | collective-permute-done | bytes 262176 | tf_op jit(solution)/shard_map/ppermute | solution.py:649
  212.9 5.2 %assemble.1 = bf16[32,512,128]{2,1,0:T(8,128)(2,1)} custom-call(bf16[32,64,128]{2,1,0:T(8,128)(2,1)} %get-tuple-element.25.refs_0_, bf16[32,64,128]{2,1,0:T(8,128)(2,1)} %copy-done.3, bf16[16,64,128]{2,1,0:T(8,128)(2,1)} %copy-done.13, bf16[16,64,128]{2,1,0:T(8,128)(2,1)} %copy-done.15, bf16[32,64,128]{2,1,0:T(8,128)(2,1)} %copy-done.2, ...), custom_call_target="tpu_custom_call" | custom-call | bytes 18450000 | tf_op jit(solution)/shard_map/assemble/pallas_call | solution.py:360
  219.0 5.0 %finish_home.1 = (bf16[32,32,256]{2,1,0:T(8,128)(2,1)}, bf16[32,32,256]{2,1,0:T(8,128)(2,1)}) custom-call(bf16[8,32,1152]{2,1,0:T(8,128)(2,1)} %copy-done.4, bf16[64,256]{1,0:T(8,128)(2,1)} %bitcast.30, bf16[8,256,256]{2,1,0:T(8,128)(2,1)} %all_to_all.25.both_ref.x_ref, s32[8,32]{1,0:T(8,128)} %reshape_reshape.3.member_ref, s32[512]{0:T(512)} %chain_ref.3), custom_call_target="tpu_custom_call" | custom-call | bytes 22140000 | tf_op jit(solution)/shard_map/finish_home/pallas_call | solution.py:590
  (90 shorter events, 37.0 us)
Async XLA Ops:
  7.2 15.6 %all-to-all-start = ((bf16[8,4,32,256]{3,2,1,0:T(8,128)(2,1)}), bf16[8,4,32,256]{3,2,1,0:T(8,128)(2,1)S(1)}, u32[]{:S(2)}, u32[]{:S(2)}) async-start(bf16[8,4,32,256]{3,2,1,0:T(8,128)(2,1)} %bitcast.27), calls=%async_computation | async-start | bytes 1048576 | tf_op jit(solution)/shard_map/all_to_all | solution.py:687
  23.5 6.7 %collective-permute-start = (bf16[8,4,32,256]{3,2,1,0:T(8,128)(2,1)}, bf16[8,4,32,256]{3,2,1,0:T(8,128)(2,1)S(1)}, u32[]{:S(2)}, u32[]{:S(2)}) collective-permute-start(bf16[8,4,32,256]{3,2,1,0:T(8,128)(2,1)} %hold.2.x_ref), channel_id=1, source_target_pairs={{0,1},{1,0},{2,3},{3,2},{4,5},{5,4},{6,7},{7,6},{8,9},{9,8},{10,11... | collective-permute-start | bytes 1572872 | tf_op jit(solution)/shard_map/ppermute | solution.py:692
  23.5 12.4 %collective-permute-start.2 = (bf16[256,512]{1,0:T(8,128)(2,1)}, bf16[256,512]{1,0:T(8,128)(2,1)S(1)}, u32[]{:S(2)}, u32[]{:S(2)}) collective-permute-start(bf16[256,512]{1,0:T(8,128)(2,1)} %pair_bias.1.refs_1_.refs_0_), channel_id=1, source_target_pairs={{0,2},{2,0},{1,3},{3,1},{4,6},{6,4},{5,7},{7,5},{8,10},{10,8},{9,1... | collective-permute-start | bytes 786440 | tf_op jit(solution)/shard_map/ppermute | solution.py:627
  25.2 10.9 %collective-permute-start.3 = (bf16[256,512]{1,0:T(8,128)(2,1)}, bf16[256,512]{1,0:T(8,128)(2,1)S(1)}, u32[]{:S(2)}, u32[]{:S(2)}) collective-permute-start(bf16[256,512]{1,0:T(8,128)(2,1)} %pair_bias.1.refs_1_.refs_0_), channel_id=1, source_target_pairs={{0,8},{4,12},{8,0},{12,4},{1,9},{5,13},{9,1},{13,5},{2,10},{6,14},... | collective-permute-start | bytes 786440 | tf_op jit(solution)/shard_map/ppermute | solution.py:630
  28.2 13.5 %collective-permute-start.1 = (bf16[256,512]{1,0:T(8,128)(2,1)}, bf16[256,512]{1,0:T(8,128)(2,1)S(1)}, u32[]{:S(2)}, u32[]{:S(2)}) collective-permute-start(bf16[256,512]{1,0:T(8,128)(2,1)} %pair_bias.1.refs_1_.refs_0_), channel_id=1, source_target_pairs={{0,12},{4,0},{8,4},{12,8},{1,13},{5,1},{9,5},{13,9},{2,14},{6,2},{... | collective-permute-start | bytes 786440 | tf_op jit(solution)/shard_map/ppermute | solution.py:629
  29.4 12.4 %collective-permute-start.4 = (bf16[256,512]{1,0:T(8,128)(2,1)}, bf16[256,512]{1,0:T(8,128)(2,1)S(1)}, u32[]{:S(2)}, u32[]{:S(2)}) collective-permute-start(bf16[256,512]{1,0:T(8,128)(2,1)} %pair_bias.1.refs_1_.refs_0_), channel_id=1, source_target_pairs={{0,4},{4,8},{8,12},{12,0},{1,5},{5,9},{9,13},{13,1},{2,6},{6,10},{... | collective-permute-start | bytes 786440 | tf_op jit(solution)/shard_map/ppermute | solution.py:628
  36.8 35.8 %copy-start.22 = (bf16[1024,128]{1,0:T(8,128)(2,1)S(1)}, bf16[1024,128]{1,0:T(8,128)(2,1)}, u32[]{:S(2)}) copy-start(bf16[1024,128]{1,0:T(8,128)(2,1)} %param.22) | copy-start | bytes 786436
  36.8 9.8 %collective-permute-start.5 = (bf16[256,512]{1,0:T(8,128)(2,1)}, bf16[256,512]{1,0:T(8,128)(2,1)S(1)}, u32[]{:S(2)}, u32[]{:S(2)}) collective-permute-start(bf16[256,512]{1,0:T(8,128)(2,1)} %get-tuple-element.21.refs_4_), channel_id=1, source_target_pairs={{0,12},{4,0},{8,4},{12,8},{1,13},{5,1},{9,5},{13,9},{2,14},{6,2},{... | collective-permute-start | bytes 786440 | tf_op jit(solution)/shard_map/ppermute | solution.py:634
  39.5 7.1 %collective-permute-start.6 = (bf16[256,512]{1,0:T(8,128)(2,1)}, bf16[256,512]{1,0:T(8,128)(2,1)S(1)}, u32[]{:S(2)}, u32[]{:S(2)}) collective-permute-start(bf16[256,512]{1,0:T(8,128)(2,1)} %get-tuple-element.20.refs_2_), channel_id=1, source_target_pairs={{0,2},{2,0},{1,3},{3,1},{4,6},{6,4},{5,7},{7,5},{8,10},{10,8},{9,1... | collective-permute-start | bytes 786440 | tf_op jit(solution)/shard_map/ppermute | solution.py:635
  40.1 8.0 %collective-permute-start.7 = (bf16[256,512]{1,0:T(8,128)(2,1)}, bf16[256,512]{1,0:T(8,128)(2,1)S(1)}, u32[]{:S(2)}, u32[]{:S(2)}) collective-permute-start(bf16[256,512]{1,0:T(8,128)(2,1)} %get-tuple-element.21.refs_4_), channel_id=1, source_target_pairs={{0,4},{4,8},{8,12},{12,0},{1,5},{5,9},{9,13},{13,1},{2,6},{6,10},{... | collective-permute-start | bytes 786440 | tf_op jit(solution)/shard_map/ppermute | solution.py:633
  63.2 21.7 %all-to-all-start.1 = ((bf16[64,16,256]{2,1,0:T(8,128)(2,1)}), bf16[64,16,256]{2,1,0:T(8,128)(2,1)S(1)}, u32[]{:S(2)}, u32[]{:S(2)}) async-start(bf16[64,16,256]{2,1,0:T(8,128)(2,1)} %bitcast.20), calls=%async_computation.1 | async-start | bytes 1048576 | tf_op jit(solution)/shard_map/all_to_all | solution.py:698
  72.6 53.7 %all-gather.3.cloned.1.call-start = ((), (), s32[]{:S(2)}) async-start(), calls=%async_computation.5 | async-start | bytes 1114112 | tf_op jit(solution)/shard_map/all_gather | solution.py:706
  141.3 43.2 %all-to-all-start.3 = ((bf16[16,128,256]{2,1,0:T(8,128)(2,1)}), bf16[16,128,256]{2,1,0:T(8,128)(2,1)S(1)}, u32[]{:S(2)}, u32[]{:S(2)}) async-start(bf16[16,128,256]{2,1,0:T(8,128)(2,1)} %bitcast.21), calls=%async_computation.3 | async-start | bytes 2097152 | tf_op jit(solution)/shard_map/all_to_all | solution.py:712
  145.8 15.5 %collective-permute-start.9 = (bf16[32,64,128]{2,1,0:T(8,128)(2,1)S(1)}, bf16[32,64,128]{2,1,0:T(8,128)(2,1)S(1)}, u32[]{:S(2)}, u32[]{:S(2)}) collective-permute-start(bf16[32,64,128]{2,1,0:T(8,128)(2,1)S(1)} %copy-done.6), channel_id=1, source_target_pairs={{0,16},{16,32},{32,48},{48,0},{1,17},{17,33},{33,49},{49,1},{2,18}... | collective-permute-start | bytes 1572872 | tf_op jit(solution)/shard_map/ppermute | solution.py:642
  147.3 25.4 %collective-permute-start.10 = (bf16[32,64,128]{2,1,0:T(8,128)(2,1)S(1)}, bf16[32,64,128]{2,1,0:T(8,128)(2,1)S(1)}, u32[]{:S(2)}, u32[]{:S(2)}) collective-permute-start(bf16[32,64,128]{2,1,0:T(8,128)(2,1)S(1)} %copy-done.6), channel_id=1, source_target_pairs={{0,64},{64,0},{1,65},{65,1},{2,66},{66,2},{3,67},{67,3},{4,68},{68... | collective-permute-start | bytes 1572872 | tf_op jit(solution)/shard_map/ppermute | solution.py:641
  150.1 25.7 %collective-permute-start.8 = (bf16[32,64,128]{2,1,0:T(8,128)(2,1)S(1)}, bf16[32,64,128]{2,1,0:T(8,128)(2,1)S(1)}, u32[]{:S(2)}, u32[]{:S(2)}) collective-permute-start(bf16[32,64,128]{2,1,0:T(8,128)(2,1)S(1)} %copy-done.6), channel_id=1, source_target_pairs={{0,48},{16,0},{32,16},{48,32},{1,49},{17,1},{33,17},{49,33},{2,50}... | collective-permute-start | bytes 1572872 | tf_op jit(solution)/shard_map/ppermute | solution.py:643
  162.1 29.3 %collective-permute-start.11 = (bf16[16,64,128]{2,1,0:T(8,128)(2,1)}, bf16[16,64,128]{2,1,0:T(8,128)(2,1)S(1)}, u32[]{:S(2)}, u32[]{:S(2)}) collective-permute-start(bf16[16,64,128]{2,1,0:T(8,128)(2,1)} %slice.8), channel_id=1, source_target_pairs={{0,16},{16,32},{32,48},{48,0},{1,17},{17,33},{33,49},{49,1},{2,18}... | collective-permute-start | bytes 786440 | tf_op jit(solution)/shard_map/ppermute | solution.py:644
  172.8 23.1 %collective-permute-start.13 = (bf16[32,64,128]{2,1,0:T(8,128)(2,1)S(1)}, bf16[32,64,128]{2,1,0:T(8,128)(2,1)S(1)}, u32[]{:S(2)}, u32[]{:S(2)}) collective-permute-start(bf16[32,64,128]{2,1,0:T(8,128)(2,1)S(1)} %collective-permute-done.10.refs_2_.refs_5_), channel_id=1, source_target_pairs={{0,48},{16,0},{32,16},{48,32},{1,49},{17,1},{33,17},{49,33},{2,50}... | collective-permute-start | bytes 1572872 | tf_op jit(solution)/shard_map/ppermute | solution.py:647
  175.7 20.2 %collective-permute-start.16 = (bf16[32,64,128]{2,1,0:T(8,128)(2,1)S(1)}, bf16[32,64,128]{2,1,0:T(8,128)(2,1)S(1)}, u32[]{:S(2)}, u32[]{:S(2)}) collective-permute-start(bf16[32,64,128]{2,1,0:T(8,128)(2,1)S(1)} %collective-permute-done.10.refs_2_.refs_5_), channel_id=1, source_target_pairs={{0,16},{16,32},{32,48},{48,0},{1,17},{17,33},{33,49},{49,1},{2,18}... | collective-permute-start | bytes 1572872 | tf_op jit(solution)/shard_map/ppermute | solution.py:646
  176.5 18.6 %collective-permute-start.12 = (bf16[16,64,128]{2,1,0:T(8,128)(2,1)}, bf16[16,64,128]{2,1,0:T(8,128)(2,1)S(1)}, u32[]{:S(2)}, u32[]{:S(2)}) collective-permute-start(bf16[16,64,128]{2,1,0:T(8,128)(2,1)} %slice.9), channel_id=1, source_target_pairs={{0,48},{16,0},{32,16},{48,32},{1,49},{17,1},{33,17},{49,33},{2,50}... | collective-permute-start | bytes 786440 | tf_op jit(solution)/shard_map/ppermute | solution.py:645
  187.8 30.4 %all-to-all-start.4 = ((bf16[8,32,1152]{2,1,0:T(8,128)(2,1)}), bf16[8,32,1152]{2,1,0:T(8,128)(2,1)S(1)}, u32[]{:S(2)}, u32[]{:S(2)}) async-start(bf16[8,32,1152]{2,1,0:T(8,128)(2,1)} %pack_grads.1), calls=%async_computation.4 | async-start | bytes 1179648 | tf_op jit(solution)/shard_map/all_to_all | solution.py:717
  191.4 20.9 %copy-start.13 = (bf16[16,64,128]{2,1,0:T(8,128)(2,1)}, bf16[16,64,128]{2,1,0:T(8,128)(2,1)S(1)}, u32[]{:S(2)}) copy-start(bf16[16,64,128]{2,1,0:T(8,128)(2,1)S(1)} %collective-permute-done.11.refs_2_) | copy-start | bytes 786436
  191.4 17.2 %collective-permute-start.14 = (bf16[16,64,128]{2,1,0:T(8,128)(2,1)S(1)}, bf16[16,64,128]{2,1,0:T(8,128)(2,1)S(1)}, u32[]{:S(2)}, u32[]{:S(2)}) collective-permute-start(bf16[16,64,128]{2,1,0:T(8,128)(2,1)S(1)} %collective-permute-done.11.refs_2_), channel_id=1, source_target_pairs={{0,64},{64,0},{1,65},{65,1},{2,66},{66,2},{3,67},{67,3},{4,68},{68... | collective-permute-start | bytes 786440 | tf_op jit(solution)/shard_map/ppermute | solution.py:648
  195.1 17.1 %collective-permute-start.15 = (bf16[16,64,128]{2,1,0:T(8,128)(2,1)S(1)}, bf16[16,64,128]{2,1,0:T(8,128)(2,1)S(1)}, u32[]{:S(2)}, u32[]{:S(2)}) collective-permute-start(bf16[16,64,128]{2,1,0:T(8,128)(2,1)S(1)} %collective-permute-done.12.refs_3_), channel_id=1, source_target_pairs={{0,64},{64,0},{1,65},{65,1},{2,66},{66,2},{3,67},{67,3},{4,68},{68... | collective-permute-start | bytes 786440 | tf_op jit(solution)/shard_map/ppermute | solution.py:649
  (22 other events, 131.3 us)
Sparse Core Ops, SparseCore 0:
  93.9 32.3 all-gather.2
where the time goes:
time: 232 us; the launch traced here: 231 us
  Pallas kernels  75.7 us (33%)
  waiting for transfers between devices  55.6 us (24%)
  starting transfers between devices  49 us (21%)
  blocking collectives  23.6 us (10%)
  between operations  14.2 us (6%)
  local copies, waits for them, and re-layouts  11.5 us (5%)
    all_to_all x1, blocking collectives, per_device(): back = lax.all_to_all(going, ('x_hi', 'z'), 0, 0, tiled=True)  23.6 us
    pallas_call x1, Pallas kernels, row_attention(): pl.pallas_call(row_kernel, in_specs=[VMEM] * (6 + len(bias)), out_specs=V...  14.4 us
    ppermute x1, waiting for transfers between devices, ring_halves(): partner_low = lax.ppermute(far_low, across, SWAP)  12.6 us
    ppermute x1, waiting for transfers between devices, ring_halves(): partner = lax.ppermute(x, across, SWAP)  10.4 us
    ppermute x1, waiting for transfers between devices, ring_halves(): below = lax.ppermute(x, along, turn_by(1))  9.55 us
    all_to_all x1, starting transfers between devices, per_device(): lax.all_to_all(after_row.reshape(q_size * b_size, 16, depth), ('x_hi', 'z...  9.41 us
    pallas_call x1, Pallas kernels, couple(): pl.pallas_call(couple_kernel, in_specs=[VMEM] * 4, out_specs=[VMEM] * 3,...  9.07 us
    all_gather x1, waiting for transfers between devices, per_device(): b_all = lax.all_gather(factor_b, ('y', 'x_lo', 'core'), axis=0)  8.89 us
  transfers between devices with their start and end apart: 22, of which 12 were waited for; matrix products, arithmetic and copies ran while one was open for 3% of the time, Pallas kernels for 14%

commit v1 on v0

--- a/solution.py
+++ b/solution.py
@@ -1,3 +1,5 @@
+import functools
+
 import jax
 import jax.numpy as jnp
 from jax import lax
@@ -75,7 +77,7 @@
     lane = lax.broadcasted_iota(jnp.int32, (depth, depth), 1)
     centering = (jnp.where(line == lane, 1.0, 0.0) - 1.0 / depth).astype(BF16)
     live = valid_ref[...] > 0
-    proj = proj_ref[...]
+    proj = proj_ref[...].astype(F32).T
     blank = jnp.zeros_like(proj)
     mean = jnp.full_like(proj, 1.0 / depth)
     sides = jnp.concatenate(
@@ -109,7 +111,7 @@
         grid=(rows // step,),
         in_specs=[
             pl.BlockSpec((step, residues, depth), lambda g: (g, 0, 0)),
-            pl.BlockSpec((H, depth), lambda g: (0, 0)),
+            pl.BlockSpec((depth, H), lambda g: (0, 0)),
             pl.BlockSpec((1, residues), lambda g: (0, 0)),
         ],
         out_specs=pl.BlockSpec((rows * H, residues), lambda g: (0, 0)),
@@ -129,22 +131,23 @@
     return nt(jnp.concatenate(spread, 0), keys[:, lanes])
 
 
-def weigh(scores, values, side):
+def weigh(scores, values):
     rows = scores.shape[0] // 4
     lane = lax.broadcasted_iota(jnp.int32, (1, 128), 1) // HEAD_SIZE
-    weights = jnp.exp2(scores - jnp.max(scores, -1, keepdims=True))
-    scale = 1.0 / jnp.sum(weights, -1, keepdims=True)
-    summed = nn(weights.astype(BF16), values[:, 128 * side : 128 * side + 128])
-    output = summed[:rows] * scale[:rows]
+    weights = jnp.exp2(scores - jnp.max(scores, -1, keepdims=True)).astype(BF16)
+    both = nn(weights, values)
+    summed, total = both[:rows, :128], both[:rows, 128:]
     for head in range(1, 4):
         here = slice(rows * head, rows * head + rows)
-        output = jnp.where(lane == head, summed[here] * scale[here], output)
-    return output
+        summed = jnp.where(lane == head, both[here, :128], summed)
+        total = jnp.where(lane == head, both[here, 128:], total)
+    return summed / total
 
 
 def entry_kernel(x_ref, other_ref, valid_ref, w_ref, q_ref, k_ref, v_ref, g_ref, live_s):
     blocks, seqs, rows, depth = x_ref.shape
     core = lax.axis_index("core")
+    v_ref[:, :, :, 128:] = jnp.ones(v_ref.shape[:3] + (128,), BF16)
     live_s[...] = jnp.broadcast_to(column_of(valid_ref[...]), live_s.shape)
     for s in range(seqs):
         for other in range(2):
@@ -157,7 +160,9 @@
                 here = slice(rows * at, rows * at + rows)
                 to = pl.ds(pl.multiple_of((2 * at + side) * rows, rows), rows)
                 k_ref[s, to, :] = (pair[here, :depth] * live_s[to, :1]).astype(BF16)
-                v_ref[s, to, :] = pair[here, depth:].astype(BF16)
+                for part in range(2):
+                    lanes = slice(depth + 128 * part, depth + 128 * part + 128)
+                    v_ref[s, part, to, :128] = pair[here, lanes].astype(BF16)
             if not other:
                 query = nn(normed, w_ref[:, :depth]) * (HEAD_SIZE**-0.5 * LOG2E)
                 q_ref[s] = query.astype(BF16)
@@ -168,11 +173,12 @@
     blocks, seqs, rows, depth = x.shape
     here = jax.ShapeDtypeStruct((seqs, blocks * rows, depth), BF16)
     full = jax.ShapeDtypeStruct((seqs, 2 * blocks * rows, depth), BF16)
+    sides = jax.ShapeDtypeStruct((seqs, 2, 2 * blocks * rows, 256), BF16)
     return pl.pallas_call(
         entry_kernel,
         in_specs=[VMEM] * 4,
         out_specs=[VMEM] * 4,
-        out_shape=[here, full, full, here],
+        out_shape=[here, full, sides, here],
         scratch_shapes=[pltpu.VMEM((2 * blocks * rows, 128), F32)],
         compiler_params=ROOM,
         cost_estimate=lasting(5),
@@ -196,27 +202,34 @@
             store(at, size // parts * part, size // parts, pieces.pop(0))
 
 
-def row_kernel(q_ref, k_ref, v_ref, g_ref, x_ref, wo_ref, *refs):
-    pieces, (out_ref, bias_s) = refs[:8], refs[8:]
+def row_kernel(steps, q_ref, k_ref, v_ref, g_ref, x_ref, wo_ref, *refs):
+    count = len(steps)
+    pieces, (out_ref, bias_s) = refs[:count], refs[-2:]
     blocks, seqs, rows, depth = x_ref.shape
-
-    def store(block, piece):
-        bias_s[(block % 4) * 2 + block // 4] = piece[...]
-
-    place(res_index(), pieces, store)
+    for at, piece in enumerate(pieces):
+        bias_s[at] = piece[...]
+    for before in refs[count:-2]:
+        out_ref[...] = before[...]
+    x_lo, y = res_index()
+
     upper = lax.broadcasted_iota(jnp.int32, (rows // 8, 8, depth), 1) < 4
 
-    def block(at, carry):
+    def block(step, carry):
+        across, ahead = jnp.int32(0), jnp.int32(0)
+        for one, (far_across, far_ahead) in enumerate(steps):
+            across = jnp.where(step == one, far_across, across)
+            ahead = jnp.where(step == one, far_ahead, ahead)
+        at = ((y + ahead) & 3) * 2 + (x_lo ^ across)
         here = pl.ds(pl.multiple_of(at * rows, rows), rows)
         scores = {}
         for side in range(2):
-            offset = bias_s[at, 4 * rows * side : 4 * rows * side + 4 * rows, :].astype(F32)
+            offset = bias_s[step, 4 * rows * side : 4 * rows * side + 4 * rows, :].astype(F32)
             for s in range(seqs):
                 scores[s, side] = scores_of(q_ref[s, here, :], k_ref.at[s], side) + offset
         done = []
         for s in range(seqs):
             output = jnp.concatenate(
-                [weigh(scores[s, side], v_ref.at[s], side) for side in range(2)], 1
+                [weigh(scores[s, side], v_ref[s, side]) for side in range(2)], 1
             )
             gated = (g_ref[s, here, :].astype(F32) * output).astype(BF16)
             after = x_ref[at, s].astype(F32) + nn(gated, wo_ref[...])
@@ -232,21 +245,21 @@
             out_ref[2 * pair + 1, at] = odd[pair]
         return carry
 
-    lax.fori_loop(0, blocks, block, 0, unroll=ROW_UNROLL)
-
-
-def row_attention(q, k, v, g, x, wo, bias):
+    lax.fori_loop(0, count, block, 0, unroll=ROW_UNROLL)
+
+
+def row_attention(steps, q, k, v, g, x, wo, bias, before=()):
     blocks, seqs, rows, depth = x.shape
     return pl.pallas_call(
-        row_kernel,
-        in_specs=[VMEM] * (6 + len(bias)),
+        functools.partial(row_kernel, steps),
+        in_specs=[VMEM] * (6 + len(bias) + len(before)),
         out_specs=VMEM,
         out_shape=jax.ShapeDtypeStruct((rows // 4, blocks, 4 * seqs, depth), BF16),
-        scratch_shapes=[pltpu.VMEM((blocks,) + bias[0].shape, BF16)],
-        compiler_params=ROOM,
-        cost_estimate=lasting(14),
+        scratch_shapes=[pltpu.VMEM((len(bias),) + bias[0].shape, BF16)],
+        compiler_params=ROOM,
+        cost_estimate=lasting(8),
         name="row_attention",
-    )(q, k, v, g, x, wo, *bias)
+    )(q, k, v, g, x, wo, *bias, *before)
 
 
 def col_kernel(
@@ -268,9 +281,12 @@
         mixed = nn(standardize(y).astype(BF16), w_ref[...])
         q_s[at] = mixed[:, :depth] * (HEAD_SIZE**-0.5 * LOG2E)
         k_s[at] = (mixed[:, depth : 2 * depth] * live_column).astype(BF16)
-        v_s[at] = mixed[:, 2 * depth : 3 * depth].astype(BF16)
+        for part in range(2):
+            lanes = slice(2 * depth + 128 * part, 2 * depth + 128 * part + 128)
+            v_s[at, part, :, :128] = mixed[:, lanes].astype(BF16)
         g_s[at] = jax.nn.sigmoid(mixed[:, 3 * depth :])
     step = COL_STEP
+    v_s[:, :, :, 128:] = jnp.ones(v_s.shape[:3] + (128,), BF16)
 
     def block(part, carry):
         here = pl.ds(pl.multiple_of(part * step, step), step)
@@ -280,7 +296,7 @@
         ]
         for at in range(parts):
             output = jnp.concatenate(
-                [weigh(scores[at][side], v_s[at], side) for side in range(2)], 1
+                [weigh(scores[at][side], v_s[at, side]) for side in range(2)], 1
             )
             o_s[at, here, :] = (g_s[at, here, :] * output).astype(BF16)
         return carry
@@ -316,7 +332,7 @@
             pltpu.VMEM((2, tokens, depth // 2), F32),
             pltpu.VMEM((4, seqs, depth), F32),
             pltpu.VMEM((4, seqs, depth), BF16),
-            pltpu.VMEM((4, seqs, depth), BF16),
+            pltpu.VMEM((4, 2, seqs, 256), BF16),
             pltpu.VMEM((4, seqs, depth), F32),
             pltpu.VMEM((4, seqs, depth), BF16),
         ],
@@ -409,10 +425,19 @@
     )(given, w, member, after)
 
 
-def couple_kernel(both_ref, w_ref, member_ref, b_ref, out_ref, a_ref, bd_ref, o_s, b_s):
+def couple_kernel(both_ref, w_ref, member_ref, *refs):
+    b_pieces, (out_ref, a_ref, bd_ref, o_s, b_s) = refs[:-5], refs[-5:]
     width = FACTOR_WIDTH
     rows, columns = o_s.shape
-    put(b_s, slice(None), b_ref[...].reshape(columns, b_ref.shape[2]).astype(F32))
+    core = lax.axis_index("core")
+    x_lo, y = res_index()
+    near, far = (0, 1, 3, 4), (2, 5, 6, 7)
+    for other in range(2):
+        for part, piece in zip((near, far), b_pieces[2 * other : 2 * other + 2]):
+            for at, block in enumerate(part):
+                to = ((y + block) & 3) * 2 + (x_lo ^ (block // 4))
+                to = pl.multiple_of((to * 2 + (core ^ other)) * 128, 128)
+                put(b_s, pl.ds(to, 128), piece[128 * at : 128 * at + 128, :].astype(F32))
     count = columns // width
     for at in range(width):
         here = slice(at * count, at * count + count)
@@ -443,12 +468,12 @@
     lax.fori_loop(0, rows // (2 * width), pair, 0, unroll=PAIR_UNROLL)
 
 
-def couple(both, w, member, b_all):
+def couple(both, w, member, b_pieces):
     seqs = both.shape[2]
-    rows, columns = both.shape[0] * 128, b_all.shape[0] * 128
+    rows, columns = both.shape[0] * 128, 4 * b_pieces[0].shape[0]
     return pl.pallas_call(
         couple_kernel,
-        in_specs=[VMEM] * 4,
+        in_specs=[VMEM] * 7,
         out_specs=[VMEM] * 3,
         out_shape=[
             jax.ShapeDtypeStruct((rows // FACTOR_WIDTH, columns // FACTOR_WIDTH, 128), BF16),
@@ -462,53 +487,58 @@
         compiler_params=ROOM,
         cost_estimate=lasting(9),
         name="couple",
-    )(both, w, member, b_all)
-
-
-def grad_a_kernel(bd_ref, s_ref, *refs):
-    out_ref = refs[-1]
-    for at in range(4):
-        here = slice(256 * at, 256 * at + 256)
-        out_ref[:, here] = nn(s_ref[here, :], bd_ref[...]).T.astype(BF16)
-
-
-def grad_a_of(bd, spread, after):
-    return pl.pallas_call(
-        grad_a_kernel,
-        in_specs=[VMEM] * 2 + [ORDER] * len(after),
-        out_specs=VMEM,
-        out_shape=jax.ShapeDtypeStruct((bd.shape[1], spread.shape[0]), BF16),
-        compiler_params=ROOM,
-        cost_estimate=lasting(4),
-        name="grad_a",
-    )(bd, spread, *after)
-
-
-def grad_b_kernel(a_ref, s_ref, *refs):
-    out_ref, turned_s = refs[-2:]
+    )(both, w, member, *b_pieces)
+
+
+def grads_kernel(a_ref, bd_ref, s_ref, _, ga_ref, own_ref, other_ref, turned_s):
     width = FACTOR_WIDTH
-    columns = out_ref.shape[0] // width
+    blocks = own_ref.shape[0]
+    columns = turned_s.shape[1] // width
+    core = lax.axis_index("core")
     left = a_ref[...].astype(F32).T.astype(BF16)
     for at in range(columns * width // 256):
         here = slice(256 * at, 256 * at + 256)
         put(turned_s, here, nn(left, s_ref[:, here]).T)
-    for at in range(columns):
-        to = slice(at * width, at * width + width)
-        out_ref[to, :] = take(turned_s, pl.ds(at, width, stride=columns)).astype(BF16)
-
-
-def grad_b_of(a_all, spread, after):
+    for other, out_ref in ((1, other_ref), (0, own_ref)):
+        for block in range(blocks):
+            for part in range(4):
+                column = (2 * block + (core ^ other)) * 4 + part
+                lines = take(turned_s, pl.ds(column, width, stride=columns))
+                out_ref[block, width * part : width * part + width, :] = lines.astype(BF16)
+    for at in range(4):
+        here = slice(256 * at, 256 * at + 256)
+        ga_ref[:, here] = nn(s_ref[here, :], bd_ref[...]).T.astype(BF16)
+
+
+def factor_grads(a_all, bd, spread, after):
     seqs, columns = a_all.shape[1], spread.shape[1]
-    return pl.pallas_call(
-        grad_b_kernel,
+    shape = jax.ShapeDtypeStruct((columns // 256, 128, seqs), BF16)
+    return pl.pallas_call(
+        grads_kernel,
+        in_specs=[VMEM] * 3 + [ORDER],
+        out_specs=[VMEM] * 3,
+        out_shape=[jax.ShapeDtypeStruct((seqs, spread.shape[0]), BF16), shape, shape],
+        scratch_shapes=[pltpu.VMEM((2, columns, seqs // 2), F32)],
+        compiler_params=ROOM,
+        cost_estimate=lasting(10),
+        name="factor_grads",
+    )(a_all, bd, spread, after)
+
+
+def fold_kernel(own_ref, other_ref, *refs):
+    refs[-1][...] = (own_ref[...].astype(F32) + other_ref[...].astype(F32)).astype(BF16)
+
+
+def fold(own, other, after):
+    return pl.pallas_call(
+        fold_kernel,
         in_specs=[VMEM] * 2 + [ORDER] * len(after),
         out_specs=VMEM,
-        out_shape=jax.ShapeDtypeStruct((columns, seqs), BF16),
-        scratch_shapes=[pltpu.VMEM((2, columns, seqs // 2), F32)],
-        compiler_params=ROOM,
-        cost_estimate=lasting(5),
-        name="grad_b",
-    )(a_all, spread, *after)
+        out_shape=jax.ShapeDtypeStruct(own.shape, BF16),
+        compiler_params=ROOM,
+        cost_estimate=lasting(1),
+        name="fold",
+    )(own, other, *after)
 
 
 def pack_kernel(ga_ref, gb_ref, out_ref):
@@ -683,7 +713,7 @@
         pair_grad.reshape(res_here, r_size, q_size, 4, pair_width), q_at, 2, keepdims=False
     ).reshape(res_here, r_size * 4, pair_width)
 
-    bias = pair_bias(pair_rep, bias_proj.astype(F32).T, chain_row)
+    bias = pair_bias(pair_rep, bias_proj, chain_row)
     x_rows = lax.all_to_all(
         multiple_alignment_rep.reshape(b_size, seqs_here // b_size, res_here, depth),
         ("y", "x_lo"), 0, 0, tiled=True,
@@ -692,7 +722,15 @@
     x_other = lax.ppermute(x_rows, "core", SWAP)
     q, k, v, g = row_entry(x_rows, x_other, chain_row, horizontal_entry_matrices)
     bias_pieces = ring(bias, "y", "x_lo", after=q)
-    after_row = row_attention(q, k, v, g, x_rows, horizontal_exit_matrix, bias_pieces)
+    near, far = (0, 1, 3, 4), (2, 5, 6, 7)
+    after_row = ()
+    for part in (near, far):
+        after_row = row_attention(
+            [(at // 4, at % 4) for at in part], q, k, v, g, x_rows, horizontal_exit_matrix,
+            [bias_pieces[at] for at in part], after_row,
+        )
+        after_row = [after_row]
+    (after_row,) = after_row
 
     spread = spread_of(grad_here, w_outer, member, after_row)
     columns = lax.all_to_all(
@@ -703,16 +741,17 @@
         columns, member, chain_position_valid,
         vertical_entry_matrices, vertical_exit_matrix, dyadic_t, q_size, spread,
     )
-    b_all = lax.all_gather(factor_b, ("y", "x_lo", "core"), axis=0)
+    b_ring = ring(factor_b, "y", "x_lo")
+    b_pieces = [jnp.concatenate([b_ring[at] for at in part], 0) for part in (near, far)]
+    b_pieces += [lax.ppermute(piece, "core", SWAP) for piece in b_pieces]
     back = lax.all_to_all(going, ("x_hi", "z"), 0, 0, tiled=True)
 
-    delta, a_all, bd = couple(back, w_outer, member, b_all)
+    delta, a_all, bd = couple(back, w_outer, member, b_pieces)
     deltas = ring_halves(delta, "z", "x_hi")
-    gb = grad_b_of(a_all, spread, [delta])
-    gb = lax.all_to_all(
-        gb.reshape(r_size, 4 * width, -1), ("y", "x_lo", "core"), 0, 0, tiled=True
-    )
-    ga = grad_a_of(bd, spread, [deltas[1], deltas[4], deltas[5]])
+    ga, gb, gb_other = factor_grads(a_all, bd, spread, delta)
+    gb_other = lax.ppermute(gb_other, "core", SWAP)
+    gb = fold(gb, gb_other, [deltas[1], deltas[4], deltas[5]])
+    gb = lax.all_to_all(gb, ("y", "x_lo"), 0, 0, tiled=True)
     couple_delta = assemble(deltas)
     factors = lax.all_to_all(pack_grads(ga, gb, q_size), ("x_hi", "z"), 0, 0, tiled=True)
     alignment_refreshed, cotangent = finish_home(

time: 232 us -> 207 us (0.89)
  blocking collectives: 23.6 us -> 0 us
  starting transfers between devices: 49 us -> 68.4 us
  waiting for transfers between devices: 55.6 us -> 40.5 us
  between operations: 14.2 us -> 0.98 us
  local copies, waits for them, and re-layouts: 11.5 us -> 17.7 us
  Pallas kernels: 75.7 us -> 78.3 us
    all_to_all x1 -> x0, blocking collectives: 23.6 us -> none  [per_device(): back = lax.all_to_all(going, ('x_hi', 'z'), 0, 0, tiled=True)]
    all_gather x1 -> x0, waiting for transfers between devices: 8.89 us -> none  [per_device(): b_all = lax.all_gather(factor_b, ('y', 'x_lo', 'core'), axis=0)]
    ppermute x1, waiting for transfers between devices: 9.55 us -> 2.67 us  [ring_halves(): below = lax.ppermute(x, along, turn_by(1))]
    ppermute x1, waiting for transfers between devices: 12.6 us -> 5.89 us  [ring_halves(): partner_low = lax.ppermute(far_low, across, SWAP)]
    unnamed x49 -> x68, local copies, waits for them, and re-layouts: 7.04 us -> 12.8 us
    ppermute x1 -> x2, waiting for transfers between devices: 0.01 us -> 5.73 us  [ring(): partner_far = lax.ppermute(far, across, SWAP)]
    all_to_all x1 -> x2, starting transfers between devices: 4.48 us -> 10.1 us  [the longest x1 6.59 us: per_device(): back = lax.all_to_all(going, ('x_hi', 'z'), 0, 0, tiled=True)]
    ppermute x1, waiting for transfers between devices: 0.25 us -> 4.65 us  [ring_halves(): far_high = lax.ppermute(above[half:], along, turn_by(3))]
  transfers between devices with their start and end apart: 22 -> 32, of which waited for: 12 -> 12; matrix products, arithmetic and copies ran while one was open for 3% -> 4% of each run, Pallas kernels for 14% -> 19%
where the time goes in v1:
time: 207 us; the launch traced here: 206 us
  Pallas kernels  78.3 us (38%)
  starting transfers between devices  68.4 us (33%)
  waiting for transfers between devices  40.5 us (20%)
  local copies, waits for them, and re-layouts  17.7 us (9%)
    pallas_call x2, Pallas kernels, row_attention(): pl.pallas_call(functools.partial(row_kernel, steps), in_specs=[VMEM] * (6...  19.2 us
    unnamed x68, local copies, waits for them, and re-layouts  12.8 us
    ppermute x1, waiting for transfers between devices, ring_halves(): partner = lax.ppermute(x, across, SWAP)  9.19 us
    pallas_call x1, Pallas kernels, couple(): pl.pallas_call(couple_kernel, in_specs=[VMEM] * 7, out_specs=[VMEM] * 3,...  8.94 us
    all_to_all x1, starting transfers between devices, per_device(): lax.all_to_all(after_row.reshape(q_size * b_size, 16, depth), ('x_hi', 'z...  8.74 us
    pallas_call x1, Pallas kernels, pair_bias(): pl.pallas_call(bias_kernel, grid=(rows // step,), in_specs=[pl.BlockSpec(...  8.48 us
    pallas_call x1, Pallas kernels, spread_of(): pl.pallas_call(spread_kernel, in_specs=[VMEM] * 3 + [ORDER], out_specs=VM...  7.64 us
    pallas_call x1, Pallas kernels, col_attention(): pl.pallas_call(col_kernel, in_specs=[VMEM] * 2 + [SMEM] + [VMEM] * 3 + [O...  7.63 us
  transfers between devices with their start and end apart: 32, of which 12 were waited for; matrix products, arithmetic and copies ran while one was open for 4% of the time, Pallas kernels for 19%

profile of v1, /device:TPU:0, one launch (start us, length us, event | category | flops | bytes accessed | tf_op | source)
XLA Modules:
  0.0 205.9 jit_solution(5248657242870432672)
XLA Ops:
  0.6 5.5 %all-to-all-start = ((bf16[8,4,32,256]{3,2,1,0:T(8,128)(2,1)}), bf16[8,4,32,256]{3,2,1,0:T(8,128)(2,1)S(1)}, u32[]{:S(2)}, u32[]{:S(2)}) async-start(bf16[8,4,32,256]{3,2,1,0:T(8,128)(2,1)} %bitcast.21), calls=%async_computation | async-start | bytes 1048576 | tf_op jit(solution)/shard_map/all_to_all | solution.py:717
  7.5 8.5 %pair_bias.1.refs_1_.refs_0_ = bf16[256,512]{1,0:T(8,128)(2,1)} custom-call(bf16[32,512,128]{2,1,0:T(8,128)(2,1)} %pair_ref.1, bf16[128,8]{1,0:T(8,128)(2,1)} %copy.18.proj_ref, s32[1,512]{1,0:T(1,128)} %bitcast.26), custom_call_target="tpu_custom_call" | custom-call | bytes 33210000 | tf_op jit(solution)/shard_map/pair_bias/pallas_call | solution.py:109
  17.0 3.3 %collective-permute-start.2 = (bf16[256,512]{1,0:T(8,128)(2,1)}, bf16[256,512]{1,0:T(8,128)(2,1)S(1)}, u32[]{:S(2)}, u32[]{:S(2)}) collective-permute-start(bf16[256,512]{1,0:T(8,128)(2,1)} %pair_bias.1.refs_1_.refs_0_), channel_id=1, source_target_pairs={{0,8},{4,12},{8,0},{12,4},{1,9},{5,13},{9,1},{13,5},{2,10},{6,14},... | collective-permute-start | bytes 786440 | tf_op jit(solution)/shard_map/ppermute | solution.py:660
  25.8 5.2 %row_entry.1 = (bf16[4,256,256]{2,1,0:T(8,128)(2,1)}, bf16[4,512,256]{2,1,0:T(8,128)(2,1)}, bf16[4,2,512,256]{3,2,1,0:T(8,128)(2,1)}, bf16[4,256,256]{2,1,0:T(8,128)(2,1)}) custom-call(bf16[8,4,32,256]{3,2,1,0:T(8,128)(2,1)} %hold.2.x_ref, bf16[8,4,32,256]{3,2,1,0:T(8,128)(2,1)} %copy-done.13, s32[1,512]{1,0:T(1,128)} %bitcast.27, bf16[256,1024]{1,0:T(8,128)(2,1)} %w_ref.2), custom_call_target="tpu_custom_call" | custom-call | bytes 18450000 | tf_op jit(solution)/shard_map/row_entry/pallas_call | solution.py:177
  32.4 3.2 %collective-permute-start.3 = (bf16[256,512]{1,0:T(8,128)(2,1)}, bf16[256,512]{1,0:T(8,128)(2,1)S(1)}, u32[]{:S(2)}, u32[]{:S(2)}) collective-permute-start(bf16[256,512]{1,0:T(8,128)(2,1)} %get-tuple-element.24.refs_3_), channel_id=1, source_target_pairs={{0,12},{4,0},{8,4},{12,8},{1,13},{5,1},{9,5},{13,9},{2,14},{6,2},{... | collective-permute-start | bytes 786440 | tf_op jit(solution)/shard_map/ppermute | solution.py:664
  36.4 9.5 %row_attention.2.refs_4_ = bf16[8,8,16,256]{3,2,1,0:T(8,128)(2,1)} custom-call(bf16[4,256,256]{2,1,0:T(8,128)(2,1)} %get-tuple-element.19.refs_2_.q_ref, bf16[4,512,256]{2,1,0:T(8,128)(2,1)} %get-tuple-element.20.k_ref, bf16[4,2,512,256]{3,2,1,0:T(8,128)(2,1)} %get-tuple-element.21.v_ref, bf16[4,256,256]{2,1,0:T(8,128)(2,1)} %get-tuple-element.22.g_ref, ...), custom_call_target="tpu_custom_call" | custom-call | bytes 29520000 | tf_op jit(solution)/shard_map/row_attention/pallas_call | solution.py:253
  47.4 9.7 %row_attention.3._ = bf16[8,8,16,256]{3,2,1,0:T(8,128)(2,1)} custom-call(bf16[4,256,256]{2,1,0:T(8,128)(2,1)} %get-tuple-element.19.refs_2_.q_ref, bf16[4,512,256]{2,1,0:T(8,128)(2,1)} %get-tuple-element.20.k_ref, bf16[4,2,512,256]{3,2,1,0:T(8,128)(2,1)} %get-tuple-element.21.v_ref, bf16[4,256,256]{2,1,0:T(8,128)(2,1)} %get-tuple-element.22.g_ref, ...), custom_call_target="tpu_custom_call" | custom-call | bytes 29520000 | tf_op jit(solution)/shard_map/row_attention/pallas_call | solution.py:253
  57.2 8.7 %all-to-all-start.1 = ((bf16[64,16,256]{2,1,0:T(8,128)(2,1)}), bf16[64,16,256]{2,1,0:T(8,128)(2,1)S(1)}, u32[]{:S(2)}, u32[]{:S(2)}) async-start(bf16[64,16,256]{2,1,0:T(8,128)(2,1)} %bitcast.16), calls=%async_computation.1 | async-start | bytes 1048576 | tf_op jit(solution)/shard_map/all_to_all | solution.py:736
  69.0 7.6 %spread.1._.s_ref = bf16[1024,2048]{1,0:T(8,128)(2,1)} custom-call(bf16[32,64,128]{2,1,0:T(8,128)(2,1)} %bitcast.19, bf16[512,256]{1,0:T(8,128)(2,1)} %bitcast.17, s32[1,256]{1,0:T(1,128)} %bitcast.28, bf16[8,8,16,256]{3,2,1,0:T(8,128)(2,1)} %row_attention.3._), custom_call_target="tpu_custom_call" | custom-call | bytes 29520000 | tf_op jit(solution)/shard_map/spread/pallas_call | solution.py:417
  79.7 7.6 %col_attention.1 = (bf16[8,256,256]{2,1,0:T(8,128)(2,1)}, bf16[128,256]{1,0:T(8,128)(2,1)}) custom-call(bf16[64,16,256]{2,1,0:T(8,128)(2,1)} %copy-done.8, s32[1,256]{1,0:T(1,128)} %bitcast.29, s32[512]{0:T(512)} %chain_ref.3, bf16[256,1024]{1,0:T(8,128)(2,1)} %w_ref.3, bf16[256,256]{1,0:T(8,128)(2,1)} %wo_ref.5, bf16[64,256]{1,0:T(8,128)(2,1)} %bitcast.23, ...), custom_call_target="tpu_custom_call" | custom-call | bytes 29520000 | tf_op jit(solution)/shard_map/col_attention/pallas_call | solution.py:323
  92.8 6.6 %all-to-all-start.2 = ((bf16[8,256,256]{2,1,0:T(8,128)(2,1)}), bf16[8,256,256]{2,1,0:T(8,128)(2,1)S(1)}, u32[]{:S(2)}, u32[]{:S(2)}) async-start(bf16[8,256,256]{2,1,0:T(8,128)(2,1)} %get-tuple-element.25), calls=%async_computation.2 | async-start | bytes 2097152 | tf_op jit(solution)/shard_map/all_to_all | solution.py:747
  100.5 3.2 %collective-permute-start.12 = (bf16[128,256]{1,0:T(8,128)(2,1)S(1)}, bf16[128,256]{1,0:T(8,128)(2,1)S(1)}, u32[]{:S(2)}, u32[]{:S(2)}) collective-permute-start(bf16[128,256]{1,0:T(8,128)(2,1)S(1)} %collective-permute-done.10), channel_id=1, source_target_pairs={{0,12},{4,0},{8,4},{12,8},{1,13},{5,1},{9,5},{13,9},{2,14},{6,2},{... | collective-permute-start | bytes 196616 | tf_op jit(solution)/shard_map/ppermute | solution.py:664
  105.6 5.7 %collective-permute-done.13 = bf16[128,256]{1,0:T(8,128)(2,1)S(1)} collective-permute-done((bf16[128,256]{1,0:T(8,128)(2,1)S(1)}, bf16[128,256]{1,0:T(8,128)(2,1)S(1)}, u32[]{:S(2)}, u32[]{:S(2)}) %collective-permute-start.13) | collective-permute-done | bytes 65568 | tf_op jit(solution)/shard_map/ppermute | solution.py:665
  115.4 8.9 %couple.1 = (bf16[32,64,128]{2,1,0:T(8,128)(2,1)}, bf16[1024,256]{1,0:T(8,128)(2,1)}, bf16[2048,256]{1,0:T(8,128)(2,1)}) custom-call(bf16[8,256,256]{2,1,0:T(8,128)(2,1)} %copy-done.1, bf16[512,256]{1,0:T(8,128)(2,1)} %bitcast.18, s32[1,256]{1,0:T(1,128)} %bitcast.30, bf16[512,256]{1,0:T(8,128)(2,1)} %copy-done.15, bf16[512,256]{1,0:T(8,128)(2,1)} %copy-done.16, ...), custom_call_target="tpu_custom_call" | custom-call | bytes 33210000 | tf_op jit(solution)/shard_map/couple/pallas_call | solution.py:474
  124.3 6.7 %factor_grads.1 = (bf16[256,1024]{1,0:T(8,128)(2,1)}, bf16[8,128,256]{2,1,0:T(8,128)(2,1)}, bf16[8,128,256]{2,1,0:T(8,128)(2,1)}) custom-call(bf16[1024,256]{1,0:T(8,128)(2,1)} %get-tuple-element.27.a_ref, bf16[2048,256]{1,0:T(8,128)(2,1)} %get-tuple-element.28.bd_ref, bf16[1024,2048]{1,0:T(8,128)(2,1)} %spread.1._.s_ref, ...), custom_call_target="tpu_custom_call" | custom-call | bytes 36900000 | tf_op jit(solution)/shard_map/factor_grads/pallas_call | solution.py:516
  131.0 3.8 %collective-permute-start.20 = (bf16[32,64,128]{2,1,0:T(8,128)(2,1)S(1)}, bf16[32,64,128]{2,1,0:T(8,128)(2,1)S(1)}, u32[]{:S(2)}, u32[]{:S(2)}) collective-permute-start(bf16[32,64,128]{2,1,0:T(8,128)(2,1)S(1)} %copy-done.5), channel_id=1, source_target_pairs={{0,64},{64,0},{1,65},{65,1},{2,66},{66,2},{3,67},{67,3},{4,68},{68... | collective-permute-start | bytes 1572872 | tf_op jit(solution)/shard_map/ppermute | solution.py:671
  138.0 9.2 %collective-permute-done.20.refs_2_.refs_5_ = bf16[32,64,128]{2,1,0:T(8,128)(2,1)S(1)} collective-permute-done((bf16[32,64,128]{2,1,0:T(8,128)(2,1)S(1)}, bf16[32,64,128]{2,1,0:T(8,128)(2,1)S(1)}, u32[]{:S(2)}, u32[]{:S(2)}) %collective-permute-start.20) | collective-permute-done | bytes 524320 | tf_op jit(solution)/shard_map/ppermute | solution.py:671
  153.0 3.5 %all-to-all-start.3 = ((bf16[8,128,256]{2,1,0:T(8,128)(2,1)}), bf16[8,128,256]{2,1,0:T(8,128)(2,1)S(1)}, u32[]{:S(2)}, u32[]{:S(2)}) async-start(bf16[8,128,256]{2,1,0:T(8,128)(2,1)} %fold.1), calls=%async_computation.3 | async-start | bytes 1048576 | tf_op jit(solution)/shard_map/all_to_all | solution.py:754
  169.2 4.7 %all-to-all-start.4 = ((bf16[8,32,1152]{2,1,0:T(8,128)(2,1)}), bf16[8,32,1152]{2,1,0:T(8,128)(2,1)S(1)}, u32[]{:S(2)}, u32[]{:S(2)}) async-start(bf16[8,32,1152]{2,1,0:T(8,128)(2,1)} %pack_grads.1), calls=%async_computation.4 | async-start | bytes 1179648 | tf_op jit(solution)/shard_map/all_to_all | solution.py:756
  173.9 3.8 %collective-permute-start.24 = (bf16[16,64,128]{2,1,0:T(8,128)(2,1)S(1)}, bf16[16,64,128]{2,1,0:T(8,128)(2,1)S(1)}, u32[]{:S(2)}, u32[]{:S(2)}) collective-permute-start(bf16[16,64,128]{2,1,0:T(8,128)(2,1)S(1)} %collective-permute-done.21.refs_2_), channel_id=1, source_target_pairs={{0,64},{64,0},{1,65},{65,1},{2,66},{66,2},{3,67},{67,3},{4,68},{68... | collective-permute-start | bytes 786440 | tf_op jit(solution)/shard_map/ppermute | solution.py:678
  177.7 4.7 %collective-permute-done.22.refs_3_ = bf16[16,64,128]{2,1,0:T(8,128)(2,1)S(1)} collective-permute-done((bf16[16,64,128]{2,1,0:T(8,128)(2,1)S(1)}, bf16[16,64,128]{2,1,0:T(8,128)(2,1)S(1)}, u32[]{:S(2)}, u32[]{:S(2)}) %collective-permute-start.22) | collective-permute-done | bytes 262176 | tf_op jit(solution)/shard_map/ppermute | solution.py:675
  185.2 5.9 %collective-permute-done.24.refs_7_ = bf16[16,64,128]{2,1,0:T(8,128)(2,1)S(1)} collective-permute-done((bf16[16,64,128]{2,1,0:T(8,128)(2,1)S(1)}, bf16[16,64,128]{2,1,0:T(8,128)(2,1)S(1)}, u32[]{:S(2)}, u32[]{:S(2)}) %collective-permute-start.24) | collective-permute-done | bytes 262176 | tf_op jit(solution)/shard_map/ppermute | solution.py:678
  194.8 5.2 %assemble.1 = bf16[32,512,128]{2,1,0:T(8,128)(2,1)} custom-call(bf16[32,64,128]{2,1,0:T(8,128)(2,1)} %get-tuple-element.29._.refs_0_, bf16[32,64,128]{2,1,0:T(8,128)(2,1)} %copy-done.3, bf16[16,64,128]{2,1,0:T(8,128)(2,1)} %copy-done.17, bf16[16,64,128]{2,1,0:T(8,128)(2,1)} %copy-done.19, bf16[32,64,128]{2,1,0:T(8,128)(2,1)} %copy-done.2, ...), custom_call_target="tpu_custom_call" | custom-call | bytes 18450000 | tf_op jit(solution)/shard_map/assemble/pallas_call | solution.py:376
  200.9 5.0 %finish_home.1 = (bf16[32,32,256]{2,1,0:T(8,128)(2,1)}, bf16[32,32,256]{2,1,0:T(8,128)(2,1)}) custom-call(bf16[8,32,1152]{2,1,0:T(8,128)(2,1)} %copy-done.4, bf16[64,256]{1,0:T(8,128)(2,1)} %bitcast.24, bf16[8,256,256]{2,1,0:T(8,128)(2,1)} %copy-done.1, s32[8,32]{1,0:T(8,128)} %reshape_reshape.3.member_ref, s32[512]{0:T(512)} %chain_ref.3), custom_call_target="tpu_custom_call" | custom-call | bytes 22140000 | tf_op jit(solution)/shard_map/finish_home/pallas_call | solution.py:620
  (129 shorter events, 59.1 us)
Async XLA Ops:
  0.6 15.6 %all-to-all-start = ((bf16[8,4,32,256]{3,2,1,0:T(8,128)(2,1)}), bf16[8,4,32,256]{3,2,1,0:T(8,128)(2,1)S(1)}, u32[]{:S(2)}, u32[]{:S(2)}) async-start(bf16[8,4,32,256]{3,2,1,0:T(8,128)(2,1)} %bitcast.21), calls=%async_computation | async-start | bytes 1048576 | tf_op jit(solution)/shard_map/all_to_all | solution.py:717
  17.0 14.0 %collective-permute-start.2 = (bf16[256,512]{1,0:T(8,128)(2,1)}, bf16[256,512]{1,0:T(8,128)(2,1)S(1)}, u32[]{:S(2)}, u32[]{:S(2)}) collective-permute-start(bf16[256,512]{1,0:T(8,128)(2,1)} %pair_bias.1.refs_1_.refs_0_), channel_id=1, source_target_pairs={{0,8},{4,12},{8,0},{12,4},{1,9},{5,13},{9,1},{13,5},{2,10},{6,14},... | collective-permute-start | bytes 786440 | tf_op jit(solution)/shard_map/ppermute | solution.py:660
  21.8 13.9 %collective-permute-start.7 = (bf16[256,512]{1,0:T(8,128)(2,1)}, bf16[256,512]{1,0:T(8,128)(2,1)S(1)}, u32[]{:S(2)}, u32[]{:S(2)}) collective-permute-start(bf16[256,512]{1,0:T(8,128)(2,1)} %pair_bias.1.refs_1_.refs_0_), channel_id=1, source_target_pairs={{0,4},{4,8},{8,12},{12,0},{1,5},{5,9},{9,13},{13,1},{2,6},{6,10},{... | collective-permute-start | bytes 786440 | tf_op jit(solution)/shard_map/ppermute | solution.py:658
  22.4 13.3 %collective-permute-start.6 = (bf16[256,512]{1,0:T(8,128)(2,1)}, bf16[256,512]{1,0:T(8,128)(2,1)S(1)}, u32[]{:S(2)}, u32[]{:S(2)}) collective-permute-start(bf16[256,512]{1,0:T(8,128)(2,1)} %pair_bias.1.refs_1_.refs_0_), channel_id=1, source_target_pairs={{0,12},{4,0},{8,4},{12,8},{1,13},{5,1},{9,5},{13,9},{2,14},{6,2},{... | collective-permute-start | bytes 786440 | tf_op jit(solution)/shard_map/ppermute | solution.py:659
  31.8 14.1 %collective-permute-start.4 = (bf16[256,512]{1,0:T(8,128)(2,1)}, bf16[256,512]{1,0:T(8,128)(2,1)S(1)}, u32[]{:S(2)}, u32[]{:S(2)}) collective-permute-start(bf16[256,512]{1,0:T(8,128)(2,1)} %get-tuple-element.23.refs_0_), channel_id=1, source_target_pairs={{0,2},{2,0},{1,3},{3,1},{4,6},{6,4},{5,7},{7,5},{8,10},{10,8},{9,1... | collective-permute-start | bytes 786440 | tf_op jit(solution)/shard_map/ppermute | solution.py:665
  32.4 13.6 %collective-permute-start.5 = (bf16[256,512]{1,0:T(8,128)(2,1)}, bf16[256,512]{1,0:T(8,128)(2,1)S(1)}, u32[]{:S(2)}, u32[]{:S(2)}) collective-permute-start(bf16[256,512]{1,0:T(8,128)(2,1)} %get-tuple-element.24.refs_3_), channel_id=1, source_target_pairs={{0,4},{4,8},{8,12},{12,0},{1,5},{5,9},{9,13},{13,1},{2,6},{6,10},{... | collective-permute-start | bytes 786440 | tf_op jit(solution)/shard_map/ppermute | solution.py:663
  32.4 13.6 %collective-permute-start.3 = (bf16[256,512]{1,0:T(8,128)(2,1)}, bf16[256,512]{1,0:T(8,128)(2,1)S(1)}, u32[]{:S(2)}, u32[]{:S(2)}) collective-permute-start(bf16[256,512]{1,0:T(8,128)(2,1)} %get-tuple-element.24.refs_3_), channel_id=1, source_target_pairs={{0,12},{4,0},{8,4},{12,8},{1,13},{5,1},{9,5},{13,9},{2,14},{6,2},{... | collective-permute-start | bytes 786440 | tf_op jit(solution)/shard_map/ppermute | solution.py:664
  57.2 21.8 %all-to-all-start.1 = ((bf16[64,16,256]{2,1,0:T(8,128)(2,1)}), bf16[64,16,256]{2,1,0:T(8,128)(2,1)S(1)}, u32[]{:S(2)}, u32[]{:S(2)}) async-start(bf16[64,16,256]{2,1,0:T(8,128)(2,1)} %bitcast.16), calls=%async_computation.1 | async-start | bytes 1048576 | tf_op jit(solution)/shard_map/all_to_all | solution.py:736
  87.3 16.4 %collective-permute-start.11 = (bf16[128,256]{1,0:T(8,128)(2,1)}, bf16[128,256]{1,0:T(8,128)(2,1)S(1)}, u32[]{:S(2)}, u32[]{:S(2)}) collective-permute-start(bf16[128,256]{1,0:T(8,128)(2,1)} %get-tuple-element.26), channel_id=1, source_target_pairs={{0,8},{4,12},{8,0},{12,4},{1,9},{5,13},{9,1},{13,5},{2,10},{6,14},... | collective-permute-start | bytes 196616 | tf_op jit(solution)/shard_map/ppermute | solution.py:660
  88.9 11.3 %collective-permute-start.10 = (bf16[128,256]{1,0:T(8,128)(2,1)}, bf16[128,256]{1,0:T(8,128)(2,1)S(1)}, u32[]{:S(2)}, u32[]{:S(2)}) collective-permute-start(bf16[128,256]{1,0:T(8,128)(2,1)} %get-tuple-element.26), channel_id=1, source_target_pairs={{0,2},{2,0},{1,3},{3,1},{4,6},{6,4},{5,7},{7,5},{8,10},{10,8},{9,1... | collective-permute-start | bytes 196616 | tf_op jit(solution)/shard_map/ppermute | solution.py:657
  92.8 21.6 %all-to-all-start.2 = ((bf16[8,256,256]{2,1,0:T(8,128)(2,1)}), bf16[8,256,256]{2,1,0:T(8,128)(2,1)S(1)}, u32[]{:S(2)}, u32[]{:S(2)}) async-start(bf16[8,256,256]{2,1,0:T(8,128)(2,1)} %get-tuple-element.25), calls=%async_computation.2 | async-start | bytes 2097152 | tf_op jit(solution)/shard_map/all_to_all | solution.py:747
  100.3 11.2 %collective-permute-start.15 = (bf16[512,256]{1,0:T(8,128)(2,1)S(1)}, bf16[512,256]{1,0:T(8,128)(2,1)S(1)}, u32[]{:S(2)}, u32[]{:S(2)}) collective-permute-start(bf16[512,256]{1,0:T(8,128)(2,1)S(1)} %constant_dynamic-update-slice_fusion.refs_0_), channel_id=1, source_target_pairs={{0,1},{1,0},{2,3},{3,2},{4,5},{5,4},{6,7},{7,6},{8,9},{9,8},{10,11... | collective-permute-start | bytes 786440 | tf_op jit(solution)/shard_map/ppermute | solution.py:746
  100.4 11.0 %collective-permute-start.14 = (bf16[128,256]{1,0:T(8,128)(2,1)S(1)}, bf16[128,256]{1,0:T(8,128)(2,1)S(1)}, u32[]{:S(2)}, u32[]{:S(2)}) collective-permute-start(bf16[128,256]{1,0:T(8,128)(2,1)S(1)} %collective-permute-done.10), channel_id=1, source_target_pairs={{0,4},{4,8},{8,12},{12,0},{1,5},{5,9},{9,13},{13,1},{2,6},{6,10},{... | collective-permute-start | bytes 196616 | tf_op jit(solution)/shard_map/ppermute | solution.py:663
  131.0 16.2 %collective-permute-start.20 = (bf16[32,64,128]{2,1,0:T(8,128)(2,1)S(1)}, bf16[32,64,128]{2,1,0:T(8,128)(2,1)S(1)}, u32[]{:S(2)}, u32[]{:S(2)}) collective-permute-start(bf16[32,64,128]{2,1,0:T(8,128)(2,1)S(1)} %copy-done.5), channel_id=1, source_target_pairs={{0,64},{64,0},{1,65},{65,1},{2,66},{66,2},{3,67},{67,3},{4,68},{68... | collective-permute-start | bytes 1572872 | tf_op jit(solution)/shard_map/ppermute | solution.py:671
  134.8 15.1 %collective-permute-start.19 = (bf16[32,64,128]{2,1,0:T(8,128)(2,1)S(1)}, bf16[32,64,128]{2,1,0:T(8,128)(2,1)S(1)}, u32[]{:S(2)}, u32[]{:S(2)}) collective-permute-start(bf16[32,64,128]{2,1,0:T(8,128)(2,1)S(1)} %copy-done.5), channel_id=1, source_target_pairs={{0,16},{16,32},{32,48},{48,0},{1,17},{17,33},{33,49},{49,1},{2,18}... | collective-permute-start | bytes 1572872 | tf_op jit(solution)/shard_map/ppermute | solution.py:672
  135.8 14.1 %collective-permute-start.18 = (bf16[32,64,128]{2,1,0:T(8,128)(2,1)S(1)}, bf16[32,64,128]{2,1,0:T(8,128)(2,1)S(1)}, u32[]{:S(2)}, u32[]{:S(2)}) collective-permute-start(bf16[32,64,128]{2,1,0:T(8,128)(2,1)S(1)} %copy-done.5), channel_id=1, source_target_pairs={{0,48},{16,0},{32,16},{48,32},{1,49},{17,1},{33,17},{49,33},{2,50}... | collective-permute-start | bytes 1572872 | tf_op jit(solution)/shard_map/ppermute | solution.py:673
  153.0 13.2 %all-to-all-start.3 = ((bf16[8,128,256]{2,1,0:T(8,128)(2,1)}), bf16[8,128,256]{2,1,0:T(8,128)(2,1)S(1)}, u32[]{:S(2)}, u32[]{:S(2)}) async-start(bf16[8,128,256]{2,1,0:T(8,128)(2,1)} %fold.1), calls=%async_computation.3 | async-start | bytes 1048576 | tf_op jit(solution)/shard_map/all_to_all | solution.py:754
  157.5 16.4 %collective-permute-start.21 = (bf16[16,64,128]{2,1,0:T(8,128)(2,1)S(1)}, bf16[16,64,128]{2,1,0:T(8,128)(2,1)S(1)}, u32[]{:S(2)}, u32[]{:S(2)}) collective-permute-start(bf16[16,64,128]{2,1,0:T(8,128)(2,1)S(1)} %slice.8), channel_id=1, source_target_pairs={{0,16},{16,32},{32,48},{48,0},{1,17},{17,33},{33,49},{49,1},{2,18}... | collective-permute-start | bytes 786440 | tf_op jit(solution)/shard_map/ppermute | solution.py:674
  158.8 26.5 %collective-permute-start.26 = (bf16[32,64,128]{2,1,0:T(8,128)(2,1)}, bf16[32,64,128]{2,1,0:T(8,128)(2,1)S(1)}, u32[]{:S(2)}, u32[]{:S(2)}) collective-permute-start(bf16[32,64,128]{2,1,0:T(8,128)(2,1)} %copy-done.7), channel_id=1, source_target_pairs={{0,16},{16,32},{32,48},{48,0},{1,17},{17,33},{33,49},{49,1},{2,18}... | collective-permute-start | bytes 1572872 | tf_op jit(solution)/shard_map/ppermute | solution.py:676
  159.5 25.7 %collective-permute-start.23 = (bf16[32,64,128]{2,1,0:T(8,128)(2,1)}, bf16[32,64,128]{2,1,0:T(8,128)(2,1)S(1)}, u32[]{:S(2)}, u32[]{:S(2)}) collective-permute-start(bf16[32,64,128]{2,1,0:T(8,128)(2,1)} %copy-done.7), channel_id=1, source_target_pairs={{0,48},{16,0},{32,16},{48,32},{1,49},{17,1},{33,17},{49,33},{2,50}... | collective-permute-start | bytes 1572872 | tf_op jit(solution)/shard_map/ppermute | solution.py:677
  163.0 19.4 %collective-permute-start.22 = (bf16[16,64,128]{2,1,0:T(8,128)(2,1)S(1)}, bf16[16,64,128]{2,1,0:T(8,128)(2,1)S(1)}, u32[]{:S(2)}, u32[]{:S(2)}) collective-permute-start(bf16[16,64,128]{2,1,0:T(8,128)(2,1)S(1)} %slice.9), channel_id=1, source_target_pairs={{0,48},{16,0},{32,16},{48,32},{1,49},{17,1},{33,17},{49,33},{2,50}... | collective-permute-start | bytes 786440 | tf_op jit(solution)/shard_map/ppermute | solution.py:675
  169.2 30.9 %all-to-all-start.4 = ((bf16[8,32,1152]{2,1,0:T(8,128)(2,1)}), bf16[8,32,1152]{2,1,0:T(8,128)(2,1)S(1)}, u32[]{:S(2)}, u32[]{:S(2)}) async-start(bf16[8,32,1152]{2,1,0:T(8,128)(2,1)} %pack_grads.1), calls=%async_computation.4 | async-start | bytes 1179648 | tf_op jit(solution)/shard_map/all_to_all | solution.py:756
  173.9 17.3 %collective-permute-start.24 = (bf16[16,64,128]{2,1,0:T(8,128)(2,1)S(1)}, bf16[16,64,128]{2,1,0:T(8,128)(2,1)S(1)}, u32[]{:S(2)}, u32[]{:S(2)}) collective-permute-start(bf16[16,64,128]{2,1,0:T(8,128)(2,1)S(1)} %collective-permute-done.21.refs_2_), channel_id=1, source_target_pairs={{0,64},{64,0},{1,65},{65,1},{2,66},{66,2},{3,67},{67,3},{4,68},{68... | collective-permute-start | bytes 786440 | tf_op jit(solution)/shard_map/ppermute | solution.py:678
  182.3 11.7 %collective-permute-start.25 = (bf16[16,64,128]{2,1,0:T(8,128)(2,1)S(1)}, bf16[16,64,128]{2,1,0:T(8,128)(2,1)S(1)}, u32[]{:S(2)}, u32[]{:S(2)}) collective-permute-start(bf16[16,64,128]{2,1,0:T(8,128)(2,1)S(1)} %collective-permute-done.22.refs_3_), channel_id=1, source_target_pairs={{0,64},{64,0},{1,65},{65,1},{2,66},{66,2},{3,67},{67,3},{4,68},{68... | collective-permute-start | bytes 786440 | tf_op jit(solution)/shard_map/ppermute | solution.py:679
  (38 other events, 242.4 us)

commit v2 on v1

--- a/solution.py
+++ b/solution.py
@@ -15,9 +15,11 @@
 BF16 = jnp.bfloat16
 F32 = jnp.float32
 NT = (((1,), (1,)), ((), ()))
-ROW_UNROLL = 1
-COL_STEP = 64
-PAIR_UNROLL = 2
+COL_STEP = 128
+ROW_UNROLL = 4
+PAIR_UNROLL = 8
+BIAS_STEP = 8
+ASSEMBLE_STEP = 8
 
 VMEM = pl.BlockSpec(memory_space=pltpu.VMEM)
 SMEM = pl.BlockSpec(memory_space=pltpu.SMEM)
@@ -105,7 +107,7 @@
 
 def pair_bias(pair, proj, valid):
     rows, residues, depth = pair.shape
-    step = 4
+    step = BIAS_STEP
     return pl.pallas_call(
         bias_kernel,
         grid=(rows // step,),
@@ -204,48 +206,48 @@
 
 def row_kernel(steps, q_ref, k_ref, v_ref, g_ref, x_ref, wo_ref, *refs):
     count = len(steps)
-    pieces, (out_ref, bias_s) = refs[:count], refs[-2:]
+    pieces, (out_ref, bias_s, after_s) = refs[:count], refs[-3:]
     blocks, seqs, rows, depth = x_ref.shape
+    lines = count * rows
     for at, piece in enumerate(pieces):
-        bias_s[at] = piece[...]
-    for before in refs[count:-2]:
+        for head in range(H):
+            to = lines * head + rows * at
+            bias_s[to : to + rows, :] = piece[rows * head : rows * head + rows, :]
+    for before in refs[count:-3]:
         out_ref[...] = before[...]
     x_lo, y = res_index()
-
+    at_blocks = [((y + ahead) & 3) * 2 + (x_lo ^ across) for across, ahead in steps]
+    spots = [pl.ds(pl.multiple_of(at * rows, rows), rows) for at in at_blocks]
+
+    def sequence(s, carry):
+        query = jnp.concatenate([q_ref[s, spot, :] for spot in spots], 0)
+        gate = jnp.concatenate([g_ref[s, spot, :] for spot in spots], 0)
+        x = jnp.concatenate([x_ref[at, s] for at in at_blocks], 0)
+        sides = []
+        for side in range(2):
+            offset = bias_s[4 * lines * side : 4 * lines * side + 4 * lines, :].astype(F32)
+            sides.append(scores_of(query, k_ref.at[s], side) + offset)
+        output = jnp.concatenate([weigh(sides[side], v_ref[s, side]) for side in range(2)], 1)
+        gated = (gate.astype(F32) * output).astype(BF16)
+        after_s[s] = x.astype(F32) + nn(gated, wo_ref[...])
+        return carry
+
+    lax.fori_loop(0, seqs, sequence, 0, unroll=ROW_UNROLL)
     upper = lax.broadcasted_iota(jnp.int32, (rows // 8, 8, depth), 1) < 4
-
-    def block(step, carry):
-        across, ahead = jnp.int32(0), jnp.int32(0)
-        for one, (far_across, far_ahead) in enumerate(steps):
-            across = jnp.where(step == one, far_across, across)
-            ahead = jnp.where(step == one, far_ahead, ahead)
-        at = ((y + ahead) & 3) * 2 + (x_lo ^ across)
-        here = pl.ds(pl.multiple_of(at * rows, rows), rows)
-        scores = {}
-        for side in range(2):
-            offset = bias_s[step, 4 * rows * side : 4 * rows * side + 4 * rows, :].astype(F32)
-            for s in range(seqs):
-                scores[s, side] = scores_of(q_ref[s, here, :], k_ref.at[s], side) + offset
-        done = []
-        for s in range(seqs):
-            output = jnp.concatenate(
-                [weigh(scores[s, side], v_ref[s, side]) for side in range(2)], 1
+    for at, block in enumerate(at_blocks):
+        even, odd = [], []
+        for pair in range(seqs // 2):
+            first, second = (
+                after_s[one, rows * at : rows * at + rows, :].reshape(rows // 8, 8, depth)
+                for one in (2 * pair, 2 * pair + 1)
             )
-            gated = (g_ref[s, here, :].astype(F32) * output).astype(BF16)
-            after = x_ref[at, s].astype(F32) + nn(gated, wo_ref[...])
-            done.append(after.reshape(rows // 8, 8, depth))
-        even, odd = [], []
-        for first, second in zip(done[::2], done[1::2]):
             even.append(jnp.where(upper, first, pltpu.roll(second, 4, 1)))
             odd.append(jnp.where(upper, pltpu.roll(first, 4, 1), second))
         even = jnp.concatenate(even, 1).astype(BF16)
         odd = jnp.concatenate(odd, 1).astype(BF16)
         for pair in range(rows // 8):
-            out_ref[2 * pair, at] = even[pair]
-            out_ref[2 * pair + 1, at] = odd[pair]
-        return carry
-
-    lax.fori_loop(0, count, block, 0, unroll=ROW_UNROLL)
+            out_ref[2 * pair, block] = even[pair]
+            out_ref[2 * pair + 1, block] = odd[pair]
 
 
 def row_attention(steps, q, k, v, g, x, wo, bias, before=()):
@@ -255,7 +257,10 @@
         in_specs=[VMEM] * (6 + len(bias) + len(before)),
         out_specs=VMEM,
         out_shape=jax.ShapeDtypeStruct((rows // 4, blocks, 4 * seqs, depth), BF16),
-        scratch_shapes=[pltpu.VMEM((len(bias),) + bias[0].shape, BF16)],
+        scratch_shapes=[
+            pltpu.VMEM((len(bias) * bias[0].shape[0], bias[0].shape[1]), BF16),
+            pltpu.VMEM((seqs, len(bias) * rows, depth), F32),
+        ],
         compiler_params=ROOM,
         cost_estimate=lasting(8),
         name="row_attention",
@@ -372,7 +377,7 @@
 
 def assemble(pieces):
     rows, columns, depth = pieces[0].shape
-    step = 8
+    step = ASSEMBLE_STEP
     return pl.pallas_call(
         assemble_kernel,
         grid=(rows // step,),
@@ -748,7 +753,7 @@
 
     delta, a_all, bd = couple(back, w_outer, member, b_pieces)
     deltas = ring_halves(delta, "z", "x_hi")
-    ga, gb, gb_other = factor_grads(a_all, bd, spread, delta)
+    ga, gb, gb_other = factor_grads(a_all, bd, spread, deltas[5])
     gb_other = lax.ppermute(gb_other, "core", SWAP)
     gb = fold(gb, gb_other, [deltas[1], deltas[4], deltas[5]])
     gb = lax.all_to_all(gb, ("y", "x_lo"), 0, 0, tiled=True)

time: 207 us -> 202 us (0.976)
  Pallas kernels: 78.3 us -> 68.8 us
  waiting for transfers between devices: 40.5 us -> 44.8 us
    pallas_call x2, Pallas kernels: 19.2 us -> 14.5 us  [row_attention(): pl.pallas_call(functools.partial(row_kernel, steps), in_specs=[VMEM] * (6...]
    ppermute x1, waiting for transfers between devices: 4.65 us -> 0.24 us  [ring_halves(): far_high = lax.ppermute(above[half:], along, turn_by(3))]
    ppermute x2, starting transfers between devices: 6.46 us -> 2.93 us  [ring(): partner_above = lax.ppermute(partner, along, turn_by(3))]
    ppermute x2, starting transfers between devices: 5.35 us -> 2.5 us  [ring(): above = lax.ppermute(x, along, turn_by(3))]
    ppermute x1, waiting for transfers between devices: 2.67 us -> 0.01 us  [ring_halves(): below = lax.ppermute(x, along, turn_by(1))]
    ppermute x1, starting transfers between devices: 2.21 us -> 4.68 us  [ring_halves(): partner_high = lax.ppermute(far_high, across, SWAP)]
    all_to_all x1, starting transfers between devices: 4.67 us -> 7.13 us  [per_device(): lax.all_to_all(pack_grads(ga, gb, q_size), ('x_hi', 'z'), 0, 0, tiled=True)]
    pallas_call x1, Pallas kernels: 8.94 us -> 6.49 us  [couple(): pl.pallas_call(couple_kernel, in_specs=[VMEM] * 7, out_specs=[VMEM] * 3,...]
  transfers between devices with their start and end apart: 32 -> 32, of which waited for: 12 -> 15; matrix products, arithmetic and copies ran while one was open for 4% -> 4% of each run, Pallas kernels for 19% -> 20%
where the time goes in v2:
time: 202 us; the launch traced here: 201 us
  Pallas kernels  68.8 us (34%)
  starting transfers between devices  67.2 us (33%)
  waiting for transfers between devices  44.8 us (22%)
  local copies, waits for them, and re-layouts  18.9 us (9%)
    pallas_call x2, Pallas kernels, row_attention(): pl.pallas_call(functools.partial(row_kernel, steps), in_specs=[VMEM] * (6...  14.5 us
    unnamed x68, local copies, waits for them, and re-layouts  14 us
    ppermute x1, waiting for transfers between devices, ring_halves(): partner = lax.ppermute(x, across, SWAP)  10.2 us
    all_to_all x1, starting transfers between devices, per_device(): lax.all_to_all(after_row.reshape(q_size * b_size, 16, depth), ('x_hi', 'z...  10 us
    ppermute x1, waiting for transfers between devices, ring_halves(): partner_low = lax.ppermute(far_low, across, SWAP)  8.05 us
    pallas_call x1, Pallas kernels, spread_of(): pl.pallas_call(spread_kernel, in_specs=[VMEM] * 3 + [ORDER], out_specs=VM...  7.64 us
    pallas_call x1, Pallas kernels, col_attention(): pl.pallas_call(col_kernel, in_specs=[VMEM] * 2 + [SMEM] + [VMEM] * 3 + [O...  7.27 us
    all_to_all x1, starting transfers between devices, per_device(): lax.all_to_all(pack_grads(ga, gb, q_size), ('x_hi', 'z'), 0, 0, tiled=True)  7.13 us
  transfers between devices with their start and end apart: 32, of which 15 were waited for; matrix products, arithmetic and copies ran while one was open for 4% of the time, Pallas kernels for 20%

profile of v2, /device:TPU:0, one launch (start us, length us, event | category | flops | bytes accessed | tf_op | source)
XLA Modules:
  0.0 200.7 jit_solution(17774574000437470395)
XLA Ops:
  0.6 5.5 %all-to-all-start = ((bf16[8,4,32,256]{3,2,1,0:T(8,128)(2,1)}), bf16[8,4,32,256]{3,2,1,0:T(8,128)(2,1)S(1)}, u32[]{:S(2)}, u32[]{:S(2)}) async-start(bf16[8,4,32,256]{3,2,1,0:T(8,128)(2,1)} %bitcast.21), calls=%async_computation | async-start | bytes 1048576 | tf_op jit(solution)/shard_map/all_to_all | solution.py:722
  7.5 6.5 %pair_bias.1.refs_1_.refs_0_ = bf16[256,512]{1,0:T(8,128)(2,1)} custom-call(bf16[32,512,128]{2,1,0:T(8,128)(2,1)} %pair_ref.1, bf16[128,8]{1,0:T(8,128)(2,1)} %copy.18.proj_ref, s32[1,512]{1,0:T(1,128)} %bitcast.26), custom_call_target="tpu_custom_call" | custom-call | bytes 33210000 | tf_op jit(solution)/shard_map/pair_bias/pallas_call | solution.py:111
  22.7 5.2 %row_entry.1 = (bf16[4,256,256]{2,1,0:T(8,128)(2,1)}, bf16[4,512,256]{2,1,0:T(8,128)(2,1)}, bf16[4,2,512,256]{3,2,1,0:T(8,128)(2,1)}, bf16[4,256,256]{2,1,0:T(8,128)(2,1)}) custom-call(bf16[8,4,32,256]{3,2,1,0:T(8,128)(2,1)} %hold.2.x_ref, bf16[8,4,32,256]{3,2,1,0:T(8,128)(2,1)} %copy-done.13, s32[1,512]{1,0:T(1,128)} %bitcast.27, bf16[256,1024]{1,0:T(8,128)(2,1)} %w_ref.2), custom_call_target="tpu_custom_call" | custom-call | bytes 18450000 | tf_op jit(solution)/shard_map/row_entry/pallas_call | solution.py:179
  34.3 7.2 %row_attention.2.refs_4_ = bf16[8,8,16,256]{3,2,1,0:T(8,128)(2,1)} custom-call(bf16[4,256,256]{2,1,0:T(8,128)(2,1)} %get-tuple-element.19.refs_2_.q_ref, bf16[4,512,256]{2,1,0:T(8,128)(2,1)} %get-tuple-element.20.k_ref, bf16[4,2,512,256]{3,2,1,0:T(8,128)(2,1)} %get-tuple-element.21.v_ref, bf16[4,256,256]{2,1,0:T(8,128)(2,1)} %get-tuple-element.22.g_ref, ...), custom_call_target="tpu_custom_call" | custom-call | bytes 29520000 | tf_op jit(solution)/shard_map/row_attention/pallas_call | solution.py:255
  43.0 7.4 %row_attention.3._ = bf16[8,8,16,256]{3,2,1,0:T(8,128)(2,1)} custom-call(bf16[4,256,256]{2,1,0:T(8,128)(2,1)} %get-tuple-element.19.refs_2_.q_ref, bf16[4,512,256]{2,1,0:T(8,128)(2,1)} %get-tuple-element.20.k_ref, bf16[4,2,512,256]{3,2,1,0:T(8,128)(2,1)} %get-tuple-element.21.v_ref, bf16[4,256,256]{2,1,0:T(8,128)(2,1)} %get-tuple-element.22.g_ref, ...), custom_call_target="tpu_custom_call" | custom-call | bytes 29520000 | tf_op jit(solution)/shard_map/row_attention/pallas_call | solution.py:255
  50.4 10.0 %all-to-all-start.1 = ((bf16[64,16,256]{2,1,0:T(8,128)(2,1)}), bf16[64,16,256]{2,1,0:T(8,128)(2,1)S(1)}, u32[]{:S(2)}, u32[]{:S(2)}) async-start(bf16[64,16,256]{2,1,0:T(8,128)(2,1)} %bitcast.16), calls=%async_computation.1 | async-start | bytes 1048576 | tf_op jit(solution)/shard_map/all_to_all | solution.py:741
  63.5 7.6 %spread.1._.s_ref = bf16[1024,2048]{1,0:T(8,128)(2,1)} custom-call(bf16[32,64,128]{2,1,0:T(8,128)(2,1)} %bitcast.19, bf16[512,256]{1,0:T(8,128)(2,1)} %bitcast.17, s32[1,256]{1,0:T(1,128)} %bitcast.28, bf16[8,8,16,256]{3,2,1,0:T(8,128)(2,1)} %row_attention.3._), custom_call_target="tpu_custom_call" | custom-call | bytes 29520000 | tf_op jit(solution)/shard_map/spread/pallas_call | solution.py:422
  71.1 2.3 %all-to-all-done.1.y_ref = bf16[64,16,256]{2,1,0:T(8,128)(2,1)S(1)} async-done(((bf16[64,16,256]{2,1,0:T(8,128)(2,1)}), bf16[64,16,256]{2,1,0:T(8,128)(2,1)S(1)}, u32[]{:S(2)}, u32[]{:S(2)}) %all-to-all-start.1) | async-done | bytes 524320 | tf_op jit(solution)/shard_map/all_to_all | solution.py:741
  74.2 7.3 %col_attention.1 = (bf16[8,256,256]{2,1,0:T(8,128)(2,1)}, bf16[128,256]{1,0:T(8,128)(2,1)}) custom-call(bf16[64,16,256]{2,1,0:T(8,128)(2,1)} %copy-done.8, s32[1,256]{1,0:T(1,128)} %bitcast.29, s32[512]{0:T(512)} %chain_ref.3, bf16[256,1024]{1,0:T(8,128)(2,1)} %w_ref.3, bf16[256,256]{1,0:T(8,128)(2,1)} %wo_ref.5, bf16[64,256]{1,0:T(8,128)(2,1)} %bitcast.23, ...), custom_call_target="tpu_custom_call" | custom-call | bytes 29520000 | tf_op jit(solution)/shard_map/col_attention/pallas_call | solution.py:328
  85.8 6.6 %all-to-all-start.2 = ((bf16[8,256,256]{2,1,0:T(8,128)(2,1)}), bf16[8,256,256]{2,1,0:T(8,128)(2,1)S(1)}, u32[]{:S(2)}, u32[]{:S(2)}) async-start(bf16[8,256,256]{2,1,0:T(8,128)(2,1)} %get-tuple-element.25), calls=%async_computation.2 | async-start | bytes 2097152 | tf_op jit(solution)/shard_map/all_to_all | solution.py:752
  97.9 6.3 %collective-permute-done.13 = bf16[128,256]{1,0:T(8,128)(2,1)S(1)} collective-permute-done((bf16[128,256]{1,0:T(8,128)(2,1)S(1)}, bf16[128,256]{1,0:T(8,128)(2,1)S(1)}, u32[]{:S(2)}, u32[]{:S(2)}) %collective-permute-start.13) | collective-permute-done | bytes 65568 | tf_op jit(solution)/shard_map/ppermute | solution.py:670
  108.3 6.5 %couple.1 = (bf16[32,64,128]{2,1,0:T(8,128)(2,1)}, bf16[1024,256]{1,0:T(8,128)(2,1)}, bf16[2048,256]{1,0:T(8,128)(2,1)}) custom-call(bf16[8,256,256]{2,1,0:T(8,128)(2,1)} %copy-done.1, bf16[512,256]{1,0:T(8,128)(2,1)} %bitcast.18, s32[1,256]{1,0:T(1,128)} %bitcast.30, bf16[512,256]{1,0:T(8,128)(2,1)} %copy-done.15, bf16[512,256]{1,0:T(8,128)(2,1)} %copy-done.16, ...), custom_call_target="tpu_custom_call" | custom-call | bytes 33210000 | tf_op jit(solution)/shard_map/couple/pallas_call | solution.py:479
  114.8 3.7 %collective-permute-start.17 = (bf16[32,64,128]{2,1,0:T(8,128)(2,1)}, bf16[32,64,128]{2,1,0:T(8,128)(2,1)S(1)}, u32[]{:S(2)}, u32[]{:S(2)}) collective-permute-start(bf16[32,64,128]{2,1,0:T(8,128)(2,1)} %get-tuple-element.29.refs_0_), channel_id=1, source_target_pairs={{0,64},{64,0},{1,65},{65,1},{2,66},{66,2},{3,67},{67,3},{4,68},{68... | collective-permute-start | bytes 1572872 | tf_op jit(solution)/shard_map/ppermute | solution.py:676
  120.7 10.2 %collective-permute-done.17._.refs_2_.refs_5_ = bf16[32,64,128]{2,1,0:T(8,128)(2,1)S(1)} collective-permute-done((bf16[32,64,128]{2,1,0:T(8,128)(2,1)}, bf16[32,64,128]{2,1,0:T(8,128)(2,1)S(1)}, u32[]{:S(2)}, u32[]{:S(2)}) %collective-permute-start.17) | collective-permute-done | bytes 524320 | tf_op jit(solution)/shard_map/ppermute | solution.py:676
  131.7 6.6 %factor_grads.1 = (bf16[256,1024]{1,0:T(8,128)(2,1)}, bf16[8,128,256]{2,1,0:T(8,128)(2,1)}, bf16[8,128,256]{2,1,0:T(8,128)(2,1)}) custom-call(bf16[1024,256]{1,0:T(8,128)(2,1)} %get-tuple-element.27.a_ref, bf16[2048,256]{1,0:T(8,128)(2,1)} %get-tuple-element.28.bd_ref, bf16[1024,2048]{1,0:T(8,128)(2,1)} %spread.1._.s_ref, bf16[32,64,128]{2,1,0:T(8,128)(2,1)} %copy-done.2), custom_call_target="tpu_custom_call" | custom-call | bytes 36900000 | tf_op jit(solution)/shard_map/factor_grads/pallas_call | solution.py:521
  143.4 3.5 %all-to-all-start.3 = ((bf16[8,128,256]{2,1,0:T(8,128)(2,1)}), bf16[8,128,256]{2,1,0:T(8,128)(2,1)S(1)}, u32[]{:S(2)}, u32[]{:S(2)}) async-start(bf16[8,128,256]{2,1,0:T(8,128)(2,1)} %fold.1), calls=%async_computation.3 | async-start | bytes 1048576 | tf_op jit(solution)/shard_map/all_to_all | solution.py:759
  154.2 3.2 %all-to-all-done.3.gb_ref = bf16[8,128,256]{2,1,0:T(8,128)(2,1)S(1)} async-done(((bf16[8,128,256]{2,1,0:T(8,128)(2,1)}), bf16[8,128,256]{2,1,0:T(8,128)(2,1)S(1)}, u32[]{:S(2)}, u32[]{:S(2)}) %all-to-all-start.3) | async-done | bytes 524320 | tf_op jit(solution)/shard_map/all_to_all | solution.py:759
  160.5 7.1 %all-to-all-start.4 = ((bf16[8,32,1152]{2,1,0:T(8,128)(2,1)}), bf16[8,32,1152]{2,1,0:T(8,128)(2,1)S(1)}, u32[]{:S(2)}, u32[]{:S(2)}) async-start(bf16[8,32,1152]{2,1,0:T(8,128)(2,1)} %pack_grads.1), calls=%async_computation.4 | async-start | bytes 1179648 | tf_op jit(solution)/shard_map/all_to_all | solution.py:761
  167.6 3.6 %collective-permute-start.24 = (bf16[16,64,128]{2,1,0:T(8,128)(2,1)S(1)}, bf16[16,64,128]{2,1,0:T(8,128)(2,1)S(1)}, u32[]{:S(2)}, u32[]{:S(2)}) collective-permute-start(bf16[16,64,128]{2,1,0:T(8,128)(2,1)S(1)} %collective-permute-done.21.refs_2_), channel_id=1, source_target_pairs={{0,64},{64,0},{1,65},{65,1},{2,66},{66,2},{3,67},{67,3},{4,68},{68... | collective-permute-start | bytes 786440 | tf_op jit(solution)/shard_map/ppermute | solution.py:683
  171.4 4.7 %collective-permute-start.25 = (bf16[16,64,128]{2,1,0:T(8,128)(2,1)S(1)}, bf16[16,64,128]{2,1,0:T(8,128)(2,1)S(1)}, u32[]{:S(2)}, u32[]{:S(2)}) collective-permute-start(bf16[16,64,128]{2,1,0:T(8,128)(2,1)S(1)} %collective-permute-done.22.refs_3_), channel_id=1, source_target_pairs={{0,64},{64,0},{1,65},{65,1},{2,66},{66,2},{3,67},{67,3},{4,68},{68... | collective-permute-start | bytes 786440 | tf_op jit(solution)/shard_map/ppermute | solution.py:684
  176.8 8.1 %collective-permute-done.24.refs_7_ = bf16[16,64,128]{2,1,0:T(8,128)(2,1)S(1)} collective-permute-done((bf16[16,64,128]{2,1,0:T(8,128)(2,1)S(1)}, bf16[16,64,128]{2,1,0:T(8,128)(2,1)S(1)}, u32[]{:S(2)}, u32[]{:S(2)}) %collective-permute-start.24) | collective-permute-done | bytes 262176 | tf_op jit(solution)/shard_map/ppermute | solution.py:683
  184.9 3.3 %collective-permute-done.25.refs_8_ = bf16[16,64,128]{2,1,0:T(8,128)(2,1)S(1)} collective-permute-done((bf16[16,64,128]{2,1,0:T(8,128)(2,1)S(1)}, bf16[16,64,128]{2,1,0:T(8,128)(2,1)S(1)}, u32[]{:S(2)}, u32[]{:S(2)}) %collective-permute-start.25) | collective-permute-done | bytes 262176 | tf_op jit(solution)/shard_map/ppermute | solution.py:684
  189.7 5.2 %assemble.1 = bf16[32,512,128]{2,1,0:T(8,128)(2,1)} custom-call(bf16[32,64,128]{2,1,0:T(8,128)(2,1)} %get-tuple-element.29.refs_0_, bf16[32,64,128]{2,1,0:T(8,128)(2,1)} %copy-done.4, bf16[16,64,128]{2,1,0:T(8,128)(2,1)} %copy-done.17, bf16[16,64,128]{2,1,0:T(8,128)(2,1)} %copy-done.19, bf16[32,64,128]{2,1,0:T(8,128)(2,1)} %copy-done.5, ...), custom_call_target="tpu_custom_call" | custom-call | bytes 18450000 | tf_op jit(solution)/shard_map/assemble/pallas_call | solution.py:381
  195.7 5.0 %finish_home.1 = (bf16[32,32,256]{2,1,0:T(8,128)(2,1)}, bf16[32,32,256]{2,1,0:T(8,128)(2,1)}) custom-call(bf16[8,32,1152]{2,1,0:T(8,128)(2,1)} %copy-done.6, bf16[64,256]{1,0:T(8,128)(2,1)} %bitcast.24, bf16[8,256,256]{2,1,0:T(8,128)(2,1)} %copy-done.1, s32[8,32]{1,0:T(8,128)} %reshape_reshape.3.member_ref, s32[512]{0:T(512)} %chain_ref.3), custom_call_target="tpu_custom_call" | custom-call | bytes 22140000 | tf_op jit(solution)/shard_map/finish_home/pallas_call | solution.py:625
  (129 shorter events, 57.1 us)
Async XLA Ops:
  0.6 15.6 %all-to-all-start = ((bf16[8,4,32,256]{3,2,1,0:T(8,128)(2,1)}), bf16[8,4,32,256]{3,2,1,0:T(8,128)(2,1)S(1)}, u32[]{:S(2)}, u32[]{:S(2)}) async-start(bf16[8,4,32,256]{3,2,1,0:T(8,128)(2,1)} %bitcast.21), calls=%async_computation | async-start | bytes 1048576 | tf_op jit(solution)/shard_map/all_to_all | solution.py:722
  17.0 10.9 %collective-permute-start.1 = (bf16[256,512]{1,0:T(8,128)(2,1)}, bf16[256,512]{1,0:T(8,128)(2,1)S(1)}, u32[]{:S(2)}, u32[]{:S(2)}) collective-permute-start(bf16[256,512]{1,0:T(8,128)(2,1)} %pair_bias.1.refs_1_.refs_0_), channel_id=1, source_target_pairs={{0,2},{2,0},{1,3},{3,1},{4,6},{6,4},{5,7},{7,5},{8,10},{10,8},{9,1... | collective-permute-start | bytes 786440 | tf_op jit(solution)/shard_map/ppermute | solution.py:662
  17.9 10.9 %collective-permute-start.2 = (bf16[256,512]{1,0:T(8,128)(2,1)}, bf16[256,512]{1,0:T(8,128)(2,1)S(1)}, u32[]{:S(2)}, u32[]{:S(2)}) collective-permute-start(bf16[256,512]{1,0:T(8,128)(2,1)} %pair_bias.1.refs_1_.refs_0_), channel_id=1, source_target_pairs={{0,8},{4,12},{8,0},{12,4},{1,9},{5,13},{9,1},{13,5},{2,10},{6,14},... | collective-permute-start | bytes 786440 | tf_op jit(solution)/shard_map/ppermute | solution.py:665
  19.9 13.6 %collective-permute-start.6 = (bf16[256,512]{1,0:T(8,128)(2,1)}, bf16[256,512]{1,0:T(8,128)(2,1)S(1)}, u32[]{:S(2)}, u32[]{:S(2)}) collective-permute-start(bf16[256,512]{1,0:T(8,128)(2,1)} %pair_bias.1.refs_1_.refs_0_), channel_id=1, source_target_pairs={{0,12},{4,0},{8,4},{12,8},{1,13},{5,1},{9,5},{13,9},{2,14},{6,2},{... | collective-permute-start | bytes 786440 | tf_op jit(solution)/shard_map/ppermute | solution.py:664
  21.1 12.5 %collective-permute-start.7 = (bf16[256,512]{1,0:T(8,128)(2,1)}, bf16[256,512]{1,0:T(8,128)(2,1)S(1)}, u32[]{:S(2)}, u32[]{:S(2)}) collective-permute-start(bf16[256,512]{1,0:T(8,128)(2,1)} %pair_bias.1.refs_1_.refs_0_), channel_id=1, source_target_pairs={{0,4},{4,8},{8,12},{12,0},{1,5},{5,9},{9,13},{13,1},{2,6},{6,10},{... | collective-permute-start | bytes 786440 | tf_op jit(solution)/shard_map/ppermute | solution.py:663
  29.5 12.1 %collective-permute-start.3 = (bf16[256,512]{1,0:T(8,128)(2,1)}, bf16[256,512]{1,0:T(8,128)(2,1)S(1)}, u32[]{:S(2)}, u32[]{:S(2)}) collective-permute-start(bf16[256,512]{1,0:T(8,128)(2,1)} %get-tuple-element.24.refs_3_), channel_id=1, source_target_pairs={{0,12},{4,0},{8,4},{12,8},{1,13},{5,1},{9,5},{13,9},{2,14},{6,2},{... | collective-permute-start | bytes 786440 | tf_op jit(solution)/shard_map/ppermute | solution.py:669
  31.2 10.4 %collective-permute-start.4 = (bf16[256,512]{1,0:T(8,128)(2,1)}, bf16[256,512]{1,0:T(8,128)(2,1)S(1)}, u32[]{:S(2)}, u32[]{:S(2)}) collective-permute-start(bf16[256,512]{1,0:T(8,128)(2,1)} %get-tuple-element.23.refs_0_), channel_id=1, source_target_pairs={{0,2},{2,0},{1,3},{3,1},{4,6},{6,4},{5,7},{7,5},{8,10},{10,8},{9,1... | collective-permute-start | bytes 786440 | tf_op jit(solution)/shard_map/ppermute | solution.py:670
  50.4 23.0 %all-to-all-start.1 = ((bf16[64,16,256]{2,1,0:T(8,128)(2,1)}), bf16[64,16,256]{2,1,0:T(8,128)(2,1)S(1)}, u32[]{:S(2)}, u32[]{:S(2)}) async-start(bf16[64,16,256]{2,1,0:T(8,128)(2,1)} %bitcast.16), calls=%async_computation.1 | async-start | bytes 1048576 | tf_op jit(solution)/shard_map/all_to_all | solution.py:741
  81.4 11.8 %collective-permute-start.8 = (bf16[128,256]{1,0:T(8,128)(2,1)}, bf16[128,256]{1,0:T(8,128)(2,1)S(1)}, u32[]{:S(2)}, u32[]{:S(2)}) collective-permute-start(bf16[128,256]{1,0:T(8,128)(2,1)} %get-tuple-element.26), channel_id=1, source_target_pairs={{0,12},{4,0},{8,4},{12,8},{1,13},{5,1},{9,5},{13,9},{2,14},{6,2},{... | collective-permute-start | bytes 196616 | tf_op jit(solution)/shard_map/ppermute | solution.py:664
  82.7 10.5 %collective-permute-start.9 = (bf16[128,256]{1,0:T(8,128)(2,1)}, bf16[128,256]{1,0:T(8,128)(2,1)S(1)}, u32[]{:S(2)}, u32[]{:S(2)}) collective-permute-start(bf16[128,256]{1,0:T(8,128)(2,1)} %get-tuple-element.26), channel_id=1, source_target_pairs={{0,4},{4,8},{8,12},{12,0},{1,5},{5,9},{9,13},{13,1},{2,6},{6,10},{... | collective-permute-start | bytes 196616 | tf_op jit(solution)/shard_map/ppermute | solution.py:663
  84.0 11.4 %collective-permute-start.11 = (bf16[128,256]{1,0:T(8,128)(2,1)}, bf16[128,256]{1,0:T(8,128)(2,1)S(1)}, u32[]{:S(2)}, u32[]{:S(2)}) collective-permute-start(bf16[128,256]{1,0:T(8,128)(2,1)} %get-tuple-element.26), channel_id=1, source_target_pairs={{0,8},{4,12},{8,0},{12,4},{1,9},{5,13},{9,1},{13,5},{2,10},{6,14},... | collective-permute-start | bytes 196616 | tf_op jit(solution)/shard_map/ppermute | solution.py:665
  85.8 21.5 %all-to-all-start.2 = ((bf16[8,256,256]{2,1,0:T(8,128)(2,1)}), bf16[8,256,256]{2,1,0:T(8,128)(2,1)S(1)}, u32[]{:S(2)}, u32[]{:S(2)}) async-start(bf16[8,256,256]{2,1,0:T(8,128)(2,1)} %get-tuple-element.25), calls=%async_computation.2 | async-start | bytes 2097152 | tf_op jit(solution)/shard_map/all_to_all | solution.py:752
  93.3 11.1 %collective-permute-start.15 = (bf16[512,256]{1,0:T(8,128)(2,1)S(1)}, bf16[512,256]{1,0:T(8,128)(2,1)S(1)}, u32[]{:S(2)}, u32[]{:S(2)}) collective-permute-start(bf16[512,256]{1,0:T(8,128)(2,1)S(1)} %constant_dynamic-update-slice_fusion.refs_0_), channel_id=1, source_target_pairs={{0,1},{1,0},{2,3},{3,2},{4,5},{5,4},{6,7},{7,6},{8,9},{9,8},{10,11... | collective-permute-start | bytes 786440 | tf_op jit(solution)/shard_map/ppermute | solution.py:751
  114.8 16.1 %collective-permute-start.17 = (bf16[32,64,128]{2,1,0:T(8,128)(2,1)}, bf16[32,64,128]{2,1,0:T(8,128)(2,1)S(1)}, u32[]{:S(2)}, u32[]{:S(2)}) collective-permute-start(bf16[32,64,128]{2,1,0:T(8,128)(2,1)} %get-tuple-element.29.refs_0_), channel_id=1, source_target_pairs={{0,64},{64,0},{1,65},{65,1},{2,66},{66,2},{3,67},{67,3},{4,68},{68... | collective-permute-start | bytes 1572872 | tf_op jit(solution)/shard_map/ppermute | solution.py:676
  118.5 19.9 %collective-permute-start.19 = (bf16[32,64,128]{2,1,0:T(8,128)(2,1)}, bf16[32,64,128]{2,1,0:T(8,128)(2,1)S(1)}, u32[]{:S(2)}, u32[]{:S(2)}) collective-permute-start(bf16[32,64,128]{2,1,0:T(8,128)(2,1)} %get-tuple-element.29.refs_0_), channel_id=1, source_target_pairs={{0,48},{16,0},{32,16},{48,32},{1,49},{17,1},{33,17},{49,33},{2,50}... | collective-permute-start | bytes 1572872 | tf_op jit(solution)/shard_map/ppermute | solution.py:678
  120.7 17.7 %collective-permute-start.20 = (bf16[32,64,128]{2,1,0:T(8,128)(2,1)}, bf16[32,64,128]{2,1,0:T(8,128)(2,1)S(1)}, u32[]{:S(2)}, u32[]{:S(2)}) collective-permute-start(bf16[32,64,128]{2,1,0:T(8,128)(2,1)} %get-tuple-element.29.refs_0_), channel_id=1, source_target_pairs={{0,16},{16,32},{32,48},{48,0},{1,17},{17,33},{33,49},{49,1},{2,18}... | collective-permute-start | bytes 1572872 | tf_op jit(solution)/shard_map/ppermute | solution.py:677
  143.4 14.1 %all-to-all-start.3 = ((bf16[8,128,256]{2,1,0:T(8,128)(2,1)}), bf16[8,128,256]{2,1,0:T(8,128)(2,1)S(1)}, u32[]{:S(2)}, u32[]{:S(2)}) async-start(bf16[8,128,256]{2,1,0:T(8,128)(2,1)} %fold.1), calls=%async_computation.3 | async-start | bytes 1048576 | tf_op jit(solution)/shard_map/all_to_all | solution.py:759
  147.9 19.7 %collective-permute-start.21 = (bf16[16,64,128]{2,1,0:T(8,128)(2,1)S(1)}, bf16[16,64,128]{2,1,0:T(8,128)(2,1)S(1)}, u32[]{:S(2)}, u32[]{:S(2)}) collective-permute-start(bf16[16,64,128]{2,1,0:T(8,128)(2,1)S(1)} %slice.8), channel_id=1, source_target_pairs={{0,16},{16,32},{32,48},{48,0},{1,17},{17,33},{33,49},{49,1},{2,18}... | collective-permute-start | bytes 786440 | tf_op jit(solution)/shard_map/ppermute | solution.py:679
  150.4 26.5 %collective-permute-start.23 = (bf16[32,64,128]{2,1,0:T(8,128)(2,1)S(1)}, bf16[32,64,128]{2,1,0:T(8,128)(2,1)S(1)}, u32[]{:S(2)}, u32[]{:S(2)}) collective-permute-start(bf16[32,64,128]{2,1,0:T(8,128)(2,1)S(1)} %copy-done.3), channel_id=1, source_target_pairs={{0,48},{16,0},{32,16},{48,32},{1,49},{17,1},{33,17},{49,33},{2,50}... | collective-permute-start | bytes 1572872 | tf_op jit(solution)/shard_map/ppermute | solution.py:682
  152.2 19.2 %collective-permute-start.22 = (bf16[16,64,128]{2,1,0:T(8,128)(2,1)S(1)}, bf16[16,64,128]{2,1,0:T(8,128)(2,1)S(1)}, u32[]{:S(2)}, u32[]{:S(2)}) collective-permute-start(bf16[16,64,128]{2,1,0:T(8,128)(2,1)S(1)} %slice.9), channel_id=1, source_target_pairs={{0,48},{16,0},{32,16},{48,32},{1,49},{17,1},{33,17},{49,33},{2,50}... | collective-permute-start | bytes 786440 | tf_op jit(solution)/shard_map/ppermute | solution.py:680
  153.7 34.5 %collective-permute-start.26 = (bf16[32,64,128]{2,1,0:T(8,128)(2,1)S(1)}, bf16[32,64,128]{2,1,0:T(8,128)(2,1)S(1)}, u32[]{:S(2)}, u32[]{:S(2)}) collective-permute-start(bf16[32,64,128]{2,1,0:T(8,128)(2,1)S(1)} %copy-done.3), channel_id=1, source_target_pairs={{0,16},{16,32},{32,48},{48,0},{1,17},{17,33},{33,49},{49,1},{2,18}... | collective-permute-start | bytes 1572872 | tf_op jit(solution)/shard_map/ppermute | solution.py:681
  160.5 34.5 %all-to-all-start.4 = ((bf16[8,32,1152]{2,1,0:T(8,128)(2,1)}), bf16[8,32,1152]{2,1,0:T(8,128)(2,1)S(1)}, u32[]{:S(2)}, u32[]{:S(2)}) async-start(bf16[8,32,1152]{2,1,0:T(8,128)(2,1)} %pack_grads.1), calls=%async_computation.4 | async-start | bytes 1179648 | tf_op jit(solution)/shard_map/all_to_all | solution.py:761
  167.6 17.3 %collective-permute-start.24 = (bf16[16,64,128]{2,1,0:T(8,128)(2,1)S(1)}, bf16[16,64,128]{2,1,0:T(8,128)(2,1)S(1)}, u32[]{:S(2)}, u32[]{:S(2)}) collective-permute-start(bf16[16,64,128]{2,1,0:T(8,128)(2,1)S(1)} %collective-permute-done.21.refs_2_), channel_id=1, source_target_pairs={{0,64},{64,0},{1,65},{65,1},{2,66},{66,2},{3,67},{67,3},{4,68},{68... | collective-permute-start | bytes 786440 | tf_op jit(solution)/shard_map/ppermute | solution.py:683
  171.4 16.7 %collective-permute-start.25 = (bf16[16,64,128]{2,1,0:T(8,128)(2,1)S(1)}, bf16[16,64,128]{2,1,0:T(8,128)(2,1)S(1)}, u32[]{:S(2)}, u32[]{:S(2)}) collective-permute-start(bf16[16,64,128]{2,1,0:T(8,128)(2,1)S(1)} %collective-permute-done.22.refs_3_), channel_id=1, source_target_pairs={{0,64},{64,0},{1,65},{65,1},{2,66},{66,2},{3,67},{67,3},{4,68},{68... | collective-permute-start | bytes 786440 | tf_op jit(solution)/shard_map/ppermute | solution.py:684
  (38 other events, 210.7 us)

commit v3 on v2

--- a/solution.py
+++ b/solution.py
@@ -79,7 +79,7 @@
     lane = lax.broadcasted_iota(jnp.int32, (depth, depth), 1)
     centering = (jnp.where(line == lane, 1.0, 0.0) - 1.0 / depth).astype(BF16)
     live = valid_ref[...] > 0
-    proj = proj_ref[...].astype(F32).T
+    proj = proj_ref[...].astype(F32)
     blank = jnp.zeros_like(proj)
     mean = jnp.full_like(proj, 1.0 / depth)
     sides = jnp.concatenate(
@@ -113,7 +113,7 @@
         grid=(rows // step,),
         in_specs=[
             pl.BlockSpec((step, residues, depth), lambda g: (g, 0, 0)),
-            pl.BlockSpec((depth, H), lambda g: (0, 0)),
+            pl.BlockSpec((H, depth), lambda g: (0, 0)),
             pl.BlockSpec((1, residues), lambda g: (0, 0)),
         ],
         out_specs=pl.BlockSpec((rows * H, residues), lambda g: (0, 0)),
@@ -348,7 +348,7 @@
 
 
 def assemble_kernel(*refs):
-    pieces, (out_ref, d_s) = refs[:10], refs[10:]
+    pieces, (out_ref, d_s) = refs[:10], refs[11:]
     step = out_ref.shape[0]
     at = pl.program_id(0)
 
@@ -375,20 +375,20 @@
     lax.fori_loop(0, step, line, 0, unroll=2)
 
 
-def assemble(pieces):
+def assemble(pieces, after):
     rows, columns, depth = pieces[0].shape
     step = ASSEMBLE_STEP
     return pl.pallas_call(
         assemble_kernel,
         grid=(rows // step,),
-        in_specs=[VMEM] * len(pieces),
+        in_specs=[VMEM] * len(pieces) + [ORDER],
         out_specs=pl.BlockSpec((step, 8 * columns, depth), lambda g: (g, 0, 0)),
         out_shape=jax.ShapeDtypeStruct((rows, 8 * columns, depth), BF16),
         scratch_shapes=[pltpu.VMEM((8, rows, columns, depth), BF16)],
         compiler_params=ROOM,
         cost_estimate=lasting(5),
         name="assemble",
-    )(*pieces)
+    )(*pieces, after)
 
 
 def spread_kernel(g_ref, w_ref, member_ref, _, out_ref):
@@ -430,24 +430,9 @@
     )(given, w, member, after)
 
 
-def couple_kernel(both_ref, w_ref, member_ref, *refs):
-    b_pieces, (out_ref, a_ref, bd_ref, o_s, b_s) = refs[:-5], refs[-5:]
+def couple_kernel(a_ref, bd_ref, w_ref, member_ref, out_ref, o_s):
     width = FACTOR_WIDTH
     rows, columns = o_s.shape
-    core = lax.axis_index("core")
-    x_lo, y = res_index()
-    near, far = (0, 1, 3, 4), (2, 5, 6, 7)
-    for other in range(2):
-        for part, piece in zip((near, far), b_pieces[2 * other : 2 * other + 2]):
-            for at, block in enumerate(part):
-                to = ((y + block) & 3) * 2 + (x_lo ^ (block // 4))
-                to = pl.multiple_of((to * 2 + (core ^ other)) * 128, 128)
-                put(b_s, pl.ds(to, 128), piece[128 * at : 128 * at + 128, :].astype(F32))
-    count = columns // width
-    for at in range(width):
-        here = slice(at * count, at * count + count)
-        bd_ref[here, :] = take(b_s, pl.ds(at, count, stride=width)).astype(BF16)
-    a_ref[...] = both_ref[:, 128:].reshape(a_ref.shape)
     for at in range(columns // 256):
         here = slice(256 * at, 256 * at + 256)
         o_s[:, here] = nt(a_ref[...], bd_ref[here, :]).astype(BF16)
@@ -473,33 +458,41 @@
     lax.fori_loop(0, rows // (2 * width), pair, 0, unroll=PAIR_UNROLL)
 
 
-def couple(both, w, member, b_pieces):
-    seqs = both.shape[2]
-    rows, columns = both.shape[0] * 128, 4 * b_pieces[0].shape[0]
+def couple(a_all, bd, w, member):
+    rows, columns = a_all.shape[0], bd.shape[0]
     return pl.pallas_call(
         couple_kernel,
-        in_specs=[VMEM] * 7,
-        out_specs=[VMEM] * 3,
-        out_shape=[
-            jax.ShapeDtypeStruct((rows // FACTOR_WIDTH, columns // FACTOR_WIDTH, 128), BF16),
-            jax.ShapeDtypeStruct((rows, seqs), BF16),
-            jax.ShapeDtypeStruct((columns, seqs), BF16),
-        ],
-        scratch_shapes=[
-            pltpu.VMEM((rows, columns), BF16),
-            pltpu.VMEM((2, columns, seqs // 2), F32),
-        ],
-        compiler_params=ROOM,
-        cost_estimate=lasting(9),
+        in_specs=[VMEM] * 4,
+        out_specs=VMEM,
+        out_shape=jax.ShapeDtypeStruct(
+            (rows // FACTOR_WIDTH, columns // FACTOR_WIDTH, 128), BF16
+        ),
+        scratch_shapes=[pltpu.VMEM((rows, columns), BF16)],
+        compiler_params=ROOM,
+        cost_estimate=lasting(6),
         name="couple",
-    )(both, w, member, *b_pieces)
-
-
-def grads_kernel(a_ref, bd_ref, s_ref, _, ga_ref, own_ref, other_ref, turned_s):
+    )(a_all, bd, w, member)
+
+
+def grads_kernel(both_ref, s_ref, *refs):
+    b_pieces, (a_ref, bd_ref, ga_ref, own_ref, other_ref, turned_s) = refs[:4], refs[4:]
     width = FACTOR_WIDTH
     blocks = own_ref.shape[0]
     columns = turned_s.shape[1] // width
     core = lax.axis_index("core")
+    x_lo, y = res_index()
+    near, far = (0, 1, 3, 4), (2, 5, 6, 7)
+    for other in range(2):
+        for part, piece in zip((near, far), b_pieces[2 * other : 2 * other + 2]):
+            for at, block in enumerate(part):
+                to = ((y + block) & 3) * 2 + (x_lo ^ (block // 4))
+                to = pl.multiple_of((to * 2 + (core ^ other)) * 128, 128)
+                lines = piece[128 * at : 128 * at + 128, :]
+                put(turned_s, pl.ds(to, 128), lines.astype(F32))
+    for at in range(width):
+        here = slice(at * columns, at * columns + columns)
+        bd_ref[here, :] = take(turned_s, pl.ds(at, columns, stride=width)).astype(BF16)
+    a_ref[...] = both_ref[:, 128:].reshape(a_ref.shape)
     left = a_ref[...].astype(F32).T.astype(BF16)
     for at in range(columns * width // 256):
         here = slice(256 * at, 256 * at + 256)
@@ -515,35 +508,42 @@
         ga_ref[:, here] = nn(s_ref[here, :], bd_ref[...]).T.astype(BF16)
 
 
-def factor_grads(a_all, bd, spread, after):
-    seqs, columns = a_all.shape[1], spread.shape[1]
+def factor_grads(both, spread, b_pieces):
+    seqs = both.shape[2]
+    rows, columns = spread.shape
     shape = jax.ShapeDtypeStruct((columns // 256, 128, seqs), BF16)
     return pl.pallas_call(
         grads_kernel,
-        in_specs=[VMEM] * 3 + [ORDER],
-        out_specs=[VMEM] * 3,
-        out_shape=[jax.ShapeDtypeStruct((seqs, spread.shape[0]), BF16), shape, shape],
+        in_specs=[VMEM] * 6,
+        out_specs=[VMEM] * 5,
+        out_shape=[
+            jax.ShapeDtypeStruct((rows, seqs), BF16),
+            jax.ShapeDtypeStruct((columns, seqs), BF16),
+            jax.ShapeDtypeStruct((seqs, rows), BF16),
+            shape,
+            shape,
+        ],
         scratch_shapes=[pltpu.VMEM((2, columns, seqs // 2), F32)],
         compiler_params=ROOM,
-        cost_estimate=lasting(10),
+        cost_estimate=lasting(9),
         name="factor_grads",
-    )(a_all, bd, spread, after)
-
-
-def fold_kernel(own_ref, other_ref, *refs):
-    refs[-1][...] = (own_ref[...].astype(F32) + other_ref[...].astype(F32)).astype(BF16)
-
-
-def fold(own, other, after):
+    )(both, spread, *b_pieces)
+
+
+def fold_kernel(own_ref, other_ref, out_ref):
+    out_ref[...] = (own_ref[...].astype(F32) + other_ref[...].astype(F32)).astype(BF16)
+
+
+def fold(own, other):
     return pl.pallas_call(
         fold_kernel,
-        in_specs=[VMEM] * 2 + [ORDER] * len(after),
+        in_specs=[VMEM] * 2,
         out_specs=VMEM,
         out_shape=jax.ShapeDtypeStruct(own.shape, BF16),
         compiler_params=ROOM,
         cost_estimate=lasting(1),
         name="fold",
-    )(own, other, *after)
+    )(own, other)
 
 
 def pack_kernel(ga_ref, gb_ref, out_ref):
@@ -569,7 +569,7 @@
     )(ga, gb)
 
 
-def home_kernel(gf_ref, w_ref, x_ref, member_ref, chain_ref, x_out_ref, ct_ref, x_s, ct_s):
+def home_kernel(gf_ref, w_ref, x_ref, member_ref, chain_ref, x_out_ref, ct_ref, x_s, ct_s, live_s):
     width = FACTOR_WIDTH
     groups, rows, depth = x_ref.shape
     parts = 4
@@ -579,8 +579,8 @@
     x_hi, z = seq_index()
     x_lo, y = res_index()
     first = ((y * 2 + x_lo) * 2 + lax.axis_index("core")) * residues
-    member = member_ref[pl.ds(x_hi * 4 + z, 1), :]
-    member = jnp.broadcast_to(member.astype(F32), (8, member.shape[1])).T[:seqs, :1]
+    live_s[...] = jnp.broadcast_to(column_of(member_ref[...]), live_s.shape)
+    member = live_s[pl.ds(pl.multiple_of((x_hi * 4 + z) * seqs, seqs), seqs), :1]
     total = gf_ref[0, :, :wide].astype(F32)
     for at in range(1, groups):
         total = total + gf_ref[at, :, :wide].astype(F32)
@@ -627,7 +627,8 @@
         in_specs=[VMEM] * 4 + [SMEM],
         out_specs=[VMEM] * 2,
         out_shape=[jax.ShapeDtypeStruct(shape, BF16)] * 2,
-        scratch_shapes=[pltpu.VMEM((2, seqs * residues, depth // 2), F32)] * 2,
+        scratch_shapes=[pltpu.VMEM((2, seqs * residues, depth // 2), F32)] * 2
+        + [pltpu.VMEM((member.shape[1], 128), F32)],
         compiler_params=ROOM,
         cost_estimate=lasting(6),
         name="finish_home",
@@ -718,7 +719,7 @@
         pair_grad.reshape(res_here, r_size, q_size, 4, pair_width), q_at, 2, keepdims=False
     ).reshape(res_here, r_size * 4, pair_width)
 
-    bias = pair_bias(pair_rep, bias_proj, chain_row)
+    bias = pair_bias(pair_rep, bias_proj.T, chain_row)
     x_rows = lax.all_to_all(
         multiple_alignment_rep.reshape(b_size, seqs_here // b_size, res_here, depth),
         ("y", "x_lo"), 0, 0, tiled=True,
@@ -751,17 +752,17 @@
     b_pieces += [lax.ppermute(piece, "core", SWAP) for piece in b_pieces]
     back = lax.all_to_all(going, ("x_hi", "z"), 0, 0, tiled=True)
 
-    delta, a_all, bd = couple(back, w_outer, member, b_pieces)
+    a_all, bd, ga, gb, gb_other = factor_grads(back, spread, b_pieces)
+    gb_other = lax.ppermute(gb_other, "core", SWAP)
+    delta = couple(a_all, bd, w_outer, member)
     deltas = ring_halves(delta, "z", "x_hi")
-    ga, gb, gb_other = factor_grads(a_all, bd, spread, deltas[5])
-    gb_other = lax.ppermute(gb_other, "core", SWAP)
-    gb = fold(gb, gb_other, [deltas[1], deltas[4], deltas[5]])
+    gb = fold(gb, gb_other)
     gb = lax.all_to_all(gb, ("y", "x_lo"), 0, 0, tiled=True)
-    couple_delta = assemble(deltas)
     factors = lax.all_to_all(pack_grads(ga, gb, q_size), ("x_hi", "z"), 0, 0, tiled=True)
     alignment_refreshed, cotangent = finish_home(
-        factors, dyadic_t, back, member.reshape(q_size, seqs_here), chain_position_valid
+        factors, dyadic_t, back, member, chain_position_valid
     )
+    couple_delta = assemble(deltas, cotangent)
     return (alignment_refreshed, couple_delta, cotangent)
 
 

time: 202 us -> 180 us (0.89)
  waiting for transfers between devices: 44.8 us -> 27.6 us
  local copies, waits for them, and re-layouts: 18.9 us -> 15.1 us
    ppermute x1, waiting for transfers between devices: 10.2 us -> 1.22 us  [ring_halves(): partner = lax.ppermute(x, across, SWAP)]
    ppermute x1, waiting for transfers between devices: 8.05 us -> 0.01 us  [ring_halves(): partner_low = lax.ppermute(far_low, across, SWAP)]
    ppermute x1, waiting for transfers between devices: 0.24 us -> 7.3 us  [ring_halves(): far_high = lax.ppermute(above[half:], along, turn_by(3))]
    ppermute x2, starting transfers between devices: 2.93 us -> 6.3 us  [ring(): partner_above = lax.ppermute(partner, along, turn_by(3))]
    ppermute x1, waiting for transfers between devices: 3.32 us -> 0.13 us  [ring_halves(): partner_high = lax.ppermute(far_high, across, SWAP)]
    unnamed x68 -> x57, local copies, waits for them, and re-layouts: 14 us -> 11.3 us
    all_to_all x1, waiting for transfers between devices: 3.24 us -> 0.58 us  [per_device(): gb = lax.all_to_all(gb, ('y', 'x_lo'), 0, 0, tiled=True)]
    ppermute x1, waiting for transfers between devices: 0.01 us -> 2.3 us  [ring_halves(): below = lax.ppermute(x, along, turn_by(1))]
  transfers between devices with their start and end apart: 32 -> 32, of which waited for: 15 -> 12; matrix products, arithmetic and copies ran while one was open for 4% -> 3% of each run, Pallas kernels for 20% -> 23%
where the time goes in v3:
time: 180 us; the launch traced here: 179 us
  Pallas kernels  69.6 us (39%)
  starting transfers between devices  66 us (37%)
  waiting for transfers between devices  27.6 us (15%)
  local copies, waits for them, and re-layouts  15.1 us (8%)
    pallas_call x2, Pallas kernels, row_attention(): pl.pallas_call(functools.partial(row_kernel, steps), in_specs=[VMEM] * (6...  14.5 us
    unnamed x57, local copies, waits for them, and re-layouts  11.3 us
    all_to_all x1, starting transfers between devices, per_device(): lax.all_to_all(after_row.reshape(q_size * b_size, 16, depth), ('x_hi', 'z...  8.78 us
    pallas_call x1, Pallas kernels, factor_grads(): pl.pallas_call(grads_kernel, in_specs=[VMEM] * 6, out_specs=[VMEM] * 5, o...  8.29 us
    pallas_call x1, Pallas kernels, spread_of(): pl.pallas_call(spread_kernel, in_specs=[VMEM] * 3 + [ORDER], out_specs=VM...  7.64 us
    ppermute x1, waiting for transfers between devices, ring_halves(): far_high = lax.ppermute(above[half:], along, turn_by(3))  7.3 us
    pallas_call x1, Pallas kernels, col_attention(): pl.pallas_call(col_kernel, in_specs=[VMEM] * 2 + [SMEM] + [VMEM] * 3 + [O...  7.26 us
    all_to_all x1, starting transfers between devices, per_device(): back = lax.all_to_all(going, ('x_hi', 'z'), 0, 0, tiled=True)  6.6 us
  transfers between devices with their start and end apart: 32, of which 12 were waited for; matrix products, arithmetic and copies ran while one was open for 3% of the time, Pallas kernels for 23%

profile of v3, /device:TPU:0, one launch (start us, length us, event | category | flops | bytes accessed | tf_op | source)
XLA Modules:
  0.0 179.4 jit_solution(1964675148086984511)
XLA Ops:
  0.6 5.5 %all-to-all-start = ((bf16[8,4,32,256]{3,2,1,0:T(8,128)(2,1)}), bf16[8,4,32,256]{3,2,1,0:T(8,128)(2,1)S(1)}, u32[]{:S(2)}, u32[]{:S(2)}) async-start(bf16[8,4,32,256]{3,2,1,0:T(8,128)(2,1)} %bitcast.22), calls=%async_computation | async-start | bytes 1048576 | tf_op jit(solution)/shard_map/all_to_all | solution.py:723
  6.1 6.5 %pair_bias.1.refs_1_.refs_0_ = bf16[256,512]{1,0:T(8,128)(2,1)} custom-call(bf16[32,512,128]{2,1,0:T(8,128)(2,1)} %pair_ref.1, bf16[8,128]{1,0:T(8,128)(2,1)} %bitcast.33, s32[1,512]{1,0:T(1,128)} %bitcast.27), custom_call_target="tpu_custom_call" | custom-call | bytes 33210000 | tf_op jit(solution)/shard_map/pair_bias/pallas_call | solution.py:111
  12.7 3.5 %all-to-all-done.refs_0_ = bf16[8,4,32,256]{3,2,1,0:T(8,128)(2,1)S(1)} async-done(((bf16[8,4,32,256]{3,2,1,0:T(8,128)(2,1)}), bf16[8,4,32,256]{3,2,1,0:T(8,128)(2,1)S(1)}, u32[]{:S(2)}, u32[]{:S(2)}) %all-to-all-start) | async-done | bytes 524320 | tf_op jit(solution)/shard_map/all_to_all | solution.py:723
  22.5 5.2 %row_entry.1 = (bf16[4,256,256]{2,1,0:T(8,128)(2,1)}, bf16[4,512,256]{2,1,0:T(8,128)(2,1)}, bf16[4,2,512,256]{3,2,1,0:T(8,128)(2,1)}, bf16[4,256,256]{2,1,0:T(8,128)(2,1)}) custom-call(bf16[8,4,32,256]{3,2,1,0:T(8,128)(2,1)} %hold.2.x_ref, bf16[8,4,32,256]{3,2,1,0:T(8,128)(2,1)} %copy-done.13, s32[1,512]{1,0:T(1,128)} %bitcast.28, bf16[256,1024]{1,0:T(8,128)(2,1)} %w_ref.2), custom_call_target="tpu_custom_call" | custom-call | bytes 18450000 | tf_op jit(solution)/shard_map/row_entry/pallas_call | solution.py:179
  30.1 3.1 %collective-permute-start.3 = (bf16[256,512]{1,0:T(8,128)(2,1)}, bf16[256,512]{1,0:T(8,128)(2,1)S(1)}, u32[]{:S(2)}, u32[]{:S(2)}) collective-permute-start(bf16[256,512]{1,0:T(8,128)(2,1)} %get-tuple-element.23.refs_3_), channel_id=1, source_target_pairs={{0,12},{4,0},{8,4},{12,8},{1,13},{5,1},{9,5},{13,9},{2,14},{6,2},{... | collective-permute-start | bytes 786440 | tf_op jit(solution)/shard_map/ppermute | solution.py:670
  34.0 7.2 %row_attention.2.refs_4_ = bf16[8,8,16,256]{3,2,1,0:T(8,128)(2,1)} custom-call(bf16[4,256,256]{2,1,0:T(8,128)(2,1)} %get-tuple-element.18.refs_2_.q_ref, bf16[4,512,256]{2,1,0:T(8,128)(2,1)} %get-tuple-element.19.k_ref, bf16[4,2,512,256]{3,2,1,0:T(8,128)(2,1)} %get-tuple-element.20.v_ref, bf16[4,256,256]{2,1,0:T(8,128)(2,1)} %get-tuple-element.21.g_ref, ...), custom_call_target="tpu_custom_call" | custom-call | bytes 29520000 | tf_op jit(solution)/shard_map/row_attention/pallas_call | solution.py:255
  42.7 7.4 %row_attention.3._ = bf16[8,8,16,256]{3,2,1,0:T(8,128)(2,1)} custom-call(bf16[4,256,256]{2,1,0:T(8,128)(2,1)} %get-tuple-element.18.refs_2_.q_ref, bf16[4,512,256]{2,1,0:T(8,128)(2,1)} %get-tuple-element.19.k_ref, bf16[4,2,512,256]{3,2,1,0:T(8,128)(2,1)} %get-tuple-element.20.v_ref, bf16[4,256,256]{2,1,0:T(8,128)(2,1)} %get-tuple-element.21.g_ref, ...), custom_call_target="tpu_custom_call" | custom-call | bytes 29520000 | tf_op jit(solution)/shard_map/row_attention/pallas_call | solution.py:255
  50.0 8.8 %all-to-all-start.1 = ((bf16[64,16,256]{2,1,0:T(8,128)(2,1)}), bf16[64,16,256]{2,1,0:T(8,128)(2,1)S(1)}, u32[]{:S(2)}, u32[]{:S(2)}) async-start(bf16[64,16,256]{2,1,0:T(8,128)(2,1)} %bitcast.17), calls=%async_computation.1 | async-start | bytes 1048576 | tf_op jit(solution)/shard_map/all_to_all | solution.py:742
  61.9 7.6 %spread.1._.s_ref = bf16[1024,2048]{1,0:T(8,128)(2,1)} custom-call(bf16[32,64,128]{2,1,0:T(8,128)(2,1)} %bitcast.20, bf16[512,256]{1,0:T(8,128)(2,1)} %bitcast.18, s32[1,256]{1,0:T(1,128)} %bitcast.29, bf16[8,8,16,256]{3,2,1,0:T(8,128)(2,1)} %row_attention.3._), custom_call_target="tpu_custom_call" | custom-call | bytes 29520000 | tf_op jit(solution)/shard_map/spread/pallas_call | solution.py:422
  72.5 7.3 %col_attention.1 = (bf16[8,256,256]{2,1,0:T(8,128)(2,1)}, bf16[128,256]{1,0:T(8,128)(2,1)}) custom-call(bf16[64,16,256]{2,1,0:T(8,128)(2,1)} %copy-done.4, s32[1,256]{1,0:T(1,128)} %bitcast.30, s32[512]{0:T(512)} %chain_ref.3, bf16[256,1024]{1,0:T(8,128)(2,1)} %w_ref.3, bf16[256,256]{1,0:T(8,128)(2,1)} %wo_ref.5, bf16[64,256]{1,0:T(8,128)(2,1)} %bitcast.24, ...), custom_call_target="tpu_custom_call" | custom-call | bytes 29520000 | tf_op jit(solution)/shard_map/col_attention/pallas_call | solution.py:328
  82.7 2.7 %collective-permute-start.8 = (bf16[128,256]{1,0:T(8,128)(2,1)}, bf16[128,256]{1,0:T(8,128)(2,1)S(1)}, u32[]{:S(2)}, u32[]{:S(2)}) collective-permute-start(bf16[128,256]{1,0:T(8,128)(2,1)} %get-tuple-element.25), channel_id=1, source_target_pairs={{0,12},{4,0},{8,4},{12,8},{1,13},{5,1},{9,5},{13,9},{2,14},{6,2},{... | collective-permute-start | bytes 196616 | tf_op jit(solution)/shard_map/ppermute | solution.py:665
  85.3 6.6 %all-to-all-start.2 = ((bf16[8,256,256]{2,1,0:T(8,128)(2,1)}), bf16[8,256,256]{2,1,0:T(8,128)(2,1)S(1)}, u32[]{:S(2)}, u32[]{:S(2)}) async-start(bf16[8,256,256]{2,1,0:T(8,128)(2,1)} %get-tuple-element.24), calls=%async_computation.2 | async-start | bytes 2097152 | tf_op jit(solution)/shard_map/all_to_all | solution.py:753
  93.0 3.2 %collective-permute-start.12 = (bf16[128,256]{1,0:T(8,128)(2,1)S(1)}, bf16[128,256]{1,0:T(8,128)(2,1)S(1)}, u32[]{:S(2)}, u32[]{:S(2)}) collective-permute-start(bf16[128,256]{1,0:T(8,128)(2,1)S(1)} %collective-permute-done.10), channel_id=1, source_target_pairs={{0,12},{4,0},{8,4},{12,8},{1,13},{5,1},{9,5},{13,9},{2,14},{6,2},{... | collective-permute-start | bytes 196616 | tf_op jit(solution)/shard_map/ppermute | solution.py:670
  98.2 5.6 %collective-permute-done.13 = bf16[128,256]{1,0:T(8,128)(2,1)S(1)} collective-permute-done((bf16[128,256]{1,0:T(8,128)(2,1)S(1)}, bf16[128,256]{1,0:T(8,128)(2,1)S(1)}, u32[]{:S(2)}, u32[]{:S(2)}) %collective-permute-start.13) | collective-permute-done | bytes 65568 | tf_op jit(solution)/shard_map/ppermute | solution.py:671
  107.8 8.3 %factor_grads.1 = (bf16[1024,256]{1,0:T(8,128)(2,1)}, bf16[2048,256]{1,0:T(8,128)(2,1)}, bf16[256,1024]{1,0:T(8,128)(2,1)}, bf16[8,128,256]{2,1,0:T(8,128)(2,1)}, bf16[8,128,256]{2,1,0:T(8,128)(2,1)}) custom-call(bf16[8,256,256]{2,1,0:T(8,128)(2,1)} %copy-done.1, bf16[1024,2048]{1,0:T(8,128)(2,1)} %spread.1._.s_ref, bf16[512,256]{1,0:T(8,128)(2,1)} %copy-done.14, ...), custom_call_target="tpu_custom_call" | custom-call | bytes 33210000 | tf_op jit(solution)/shard_map/factor_grads/pallas_call | solution.py:515
  116.1 5.6 %couple.1.refs_0_ = bf16[32,64,128]{2,1,0:T(8,128)(2,1)} custom-call(bf16[1024,256]{1,0:T(8,128)(2,1)} %get-tuple-element.30.a_ref, bf16[2048,256]{1,0:T(8,128)(2,1)} %get-tuple-element.31.bd_ref, bf16[512,256]{1,0:T(8,128)(2,1)} %bitcast.19, s32[1,256]{1,0:T(1,128)} %bitcast.31), custom_call_target="tpu_custom_call" | custom-call | bytes 22140000 | tf_op jit(solution)/shard_map/couple/pallas_call | solution.py:463
  123.0 3.6 %collective-permute-start.22 = (bf16[32,64,128]{2,1,0:T(8,128)(2,1)}, bf16[32,64,128]{2,1,0:T(8,128)(2,1)S(1)}, u32[]{:S(2)}, u32[]{:S(2)}) collective-permute-start(bf16[32,64,128]{2,1,0:T(8,128)(2,1)} %couple.1.refs_0_), channel_id=1, source_target_pairs={{0,64},{64,0},{1,65},{65,1},{2,66},{66,2},{3,67},{67,3},{4,68},{68... | collective-permute-start | bytes 1572872 | tf_op jit(solution)/shard_map/ppermute | solution.py:677
  131.7 3.5 %all-to-all-start.3 = ((bf16[8,128,256]{2,1,0:T(8,128)(2,1)}), bf16[8,128,256]{2,1,0:T(8,128)(2,1)S(1)}, u32[]{:S(2)}, u32[]{:S(2)}) async-start(bf16[8,128,256]{2,1,0:T(8,128)(2,1)} %fold.1), calls=%async_computation.3 | async-start | bytes 1048576 | tf_op jit(solution)/shard_map/all_to_all | solution.py:760
  148.2 5.3 %all-to-all-start.4 = ((bf16[8,32,1152]{2,1,0:T(8,128)(2,1)}), bf16[8,32,1152]{2,1,0:T(8,128)(2,1)S(1)}, u32[]{:S(2)}, u32[]{:S(2)}) async-start(bf16[8,32,1152]{2,1,0:T(8,128)(2,1)} %pack_grads.1), calls=%async_computation.4 | async-start | bytes 1179648 | tf_op jit(solution)/shard_map/all_to_all | solution.py:761
  153.5 3.6 %collective-permute-start.24 = (bf16[16,64,128]{2,1,0:T(8,128)(2,1)S(1)}, bf16[16,64,128]{2,1,0:T(8,128)(2,1)}, u32[]{:S(2)}, u32[]{:S(2)}) collective-permute-start(bf16[16,64,128]{2,1,0:T(8,128)(2,1)S(1)} %collective-permute-done.20.refs_2_), channel_id=1, source_target_pairs={{0,64},{64,0},{1,65},{65,1},{2,66},{66,2},{3,67},{67,3},{4,68},{68... | collective-permute-start | bytes 786440 | tf_op jit(solution)/shard_map/ppermute | solution.py:684
  157.1 7.3 %collective-permute-done.21.refs_3_ = bf16[16,64,128]{2,1,0:T(8,128)(2,1)} collective-permute-done((bf16[16,64,128]{2,1,0:T(8,128)(2,1)}, bf16[16,64,128]{2,1,0:T(8,128)(2,1)}, u32[]{:S(2)}, u32[]{:S(2)}) %collective-permute-start.21) | collective-permute-done | bytes 262176 | tf_op jit(solution)/shard_map/ppermute | solution.py:681
  164.4 2.9 %collective-permute-start.25 = (bf16[16,64,128]{2,1,0:T(8,128)(2,1)}, bf16[16,64,128]{2,1,0:T(8,128)(2,1)}, u32[]{:S(2)}, u32[]{:S(2)}) collective-permute-start(bf16[16,64,128]{2,1,0:T(8,128)(2,1)} %collective-permute-done.21.refs_3_), channel_id=1, source_target_pairs={{0,64},{64,0},{1,65},{65,1},{2,66},{66,2},{3,67},{67,3},{4,68},{68... | collective-permute-start | bytes 786440 | tf_op jit(solution)/shard_map/ppermute | solution.py:685
  168.1 5.0 %finish_home.1 = (bf16[32,32,256]{2,1,0:T(8,128)(2,1)}, bf16[32,32,256]{2,1,0:T(8,128)(2,1)}) custom-call(bf16[8,32,1152]{2,1,0:T(8,128)(2,1)} %copy-done.2, bf16[64,256]{1,0:T(8,128)(2,1)} %bitcast.25, bf16[8,256,256]{2,1,0:T(8,128)(2,1)} %copy-done.1, s32[1,256]{1,0:T(1,128)} %bitcast.32, s32[512]{0:T(512)} %chain_ref.3), custom_call_target="tpu_custom_call" | custom-call | bytes 22140000 | tf_op jit(solution)/shard_map/finish_home/pallas_call | solution.py:625
  174.2 5.2 %assemble.1 = bf16[32,512,128]{2,1,0:T(8,128)(2,1)} custom-call(bf16[32,64,128]{2,1,0:T(8,128)(2,1)} %couple.1.refs_0_, bf16[32,64,128]{2,1,0:T(8,128)(2,1)} %copy-done.6, bf16[16,64,128]{2,1,0:T(8,128)(2,1)} %copy-done.16, bf16[16,64,128]{2,1,0:T(8,128)(2,1)} %collective-permute-done.21.refs_3_, bf16[32,64,128]{2,1,0:T(8,128)(2,1)} %copy-done.5, ...), custom_call_target="tpu_custom_call" | custom-call | bytes 18450000 | tf_op jit(solution)/shard_map/assemble/pallas_call | solution.py:381
  (117 shorter events, 47.9 us)
Async XLA Ops:
  0.6 15.6 %all-to-all-start = ((bf16[8,4,32,256]{3,2,1,0:T(8,128)(2,1)}), bf16[8,4,32,256]{3,2,1,0:T(8,128)(2,1)S(1)}, u32[]{:S(2)}, u32[]{:S(2)}) async-start(bf16[8,4,32,256]{3,2,1,0:T(8,128)(2,1)} %bitcast.22), calls=%async_computation | async-start | bytes 1048576 | tf_op jit(solution)/shard_map/all_to_all | solution.py:723
  17.0 10.9 %collective-permute-start.2 = (bf16[256,512]{1,0:T(8,128)(2,1)}, bf16[256,512]{1,0:T(8,128)(2,1)S(1)}, u32[]{:S(2)}, u32[]{:S(2)}) collective-permute-start(bf16[256,512]{1,0:T(8,128)(2,1)} %pair_bias.1.refs_1_.refs_0_), channel_id=1, source_target_pairs={{0,8},{4,12},{8,0},{12,4},{1,9},{5,13},{9,1},{13,5},{2,10},{6,14},... | collective-permute-start | bytes 786440 | tf_op jit(solution)/shard_map/ppermute | solution.py:666
  18.5 14.7 %collective-permute-start.7 = (bf16[256,512]{1,0:T(8,128)(2,1)}, bf16[256,512]{1,0:T(8,128)(2,1)S(1)}, u32[]{:S(2)}, u32[]{:S(2)}) collective-permute-start(bf16[256,512]{1,0:T(8,128)(2,1)} %pair_bias.1.refs_1_.refs_0_), channel_id=1, source_target_pairs={{0,4},{4,8},{8,12},{12,0},{1,5},{5,9},{9,13},{13,1},{2,6},{6,10},{... | collective-permute-start | bytes 786440 | tf_op jit(solution)/shard_map/ppermute | solution.py:664
  19.9 13.3 %collective-permute-start.6 = (bf16[256,512]{1,0:T(8,128)(2,1)}, bf16[256,512]{1,0:T(8,128)(2,1)S(1)}, u32[]{:S(2)}, u32[]{:S(2)}) collective-permute-start(bf16[256,512]{1,0:T(8,128)(2,1)} %pair_bias.1.refs_1_.refs_0_), channel_id=1, source_target_pairs={{0,12},{4,0},{8,4},{12,8},{1,13},{5,1},{9,5},{13,9},{2,14},{6,2},{... | collective-permute-start | bytes 786440 | tf_op jit(solution)/shard_map/ppermute | solution.py:665
  28.7 12.5 %collective-permute-start.4 = (bf16[256,512]{1,0:T(8,128)(2,1)}, bf16[256,512]{1,0:T(8,128)(2,1)S(1)}, u32[]{:S(2)}, u32[]{:S(2)}) collective-permute-start(bf16[256,512]{1,0:T(8,128)(2,1)} %get-tuple-element.22.refs_0_), channel_id=1, source_target_pairs={{0,2},{2,0},{1,3},{3,1},{4,6},{6,4},{5,7},{7,5},{8,10},{10,8},{9,1... | collective-permute-start | bytes 786440 | tf_op jit(solution)/shard_map/ppermute | solution.py:671
  29.9 11.2 %collective-permute-start.5 = (bf16[256,512]{1,0:T(8,128)(2,1)}, bf16[256,512]{1,0:T(8,128)(2,1)S(1)}, u32[]{:S(2)}, u32[]{:S(2)}) collective-permute-start(bf16[256,512]{1,0:T(8,128)(2,1)} %get-tuple-element.23.refs_3_), channel_id=1, source_target_pairs={{0,4},{4,8},{8,12},{12,0},{1,5},{5,9},{9,13},{13,1},{2,6},{6,10},{... | collective-permute-start | bytes 786440 | tf_op jit(solution)/shard_map/ppermute | solution.py:669
  30.1 11.1 %collective-permute-start.3 = (bf16[256,512]{1,0:T(8,128)(2,1)}, bf16[256,512]{1,0:T(8,128)(2,1)S(1)}, u32[]{:S(2)}, u32[]{:S(2)}) collective-permute-start(bf16[256,512]{1,0:T(8,128)(2,1)} %get-tuple-element.23.refs_3_), channel_id=1, source_target_pairs={{0,12},{4,0},{8,4},{12,8},{1,13},{5,1},{9,5},{13,9},{2,14},{6,2},{... | collective-permute-start | bytes 786440 | tf_op jit(solution)/shard_map/ppermute | solution.py:670
  50.0 21.7 %all-to-all-start.1 = ((bf16[64,16,256]{2,1,0:T(8,128)(2,1)}), bf16[64,16,256]{2,1,0:T(8,128)(2,1)S(1)}, u32[]{:S(2)}, u32[]{:S(2)}) async-start(bf16[64,16,256]{2,1,0:T(8,128)(2,1)} %bitcast.17), calls=%async_computation.1 | async-start | bytes 1048576 | tf_op jit(solution)/shard_map/all_to_all | solution.py:742
  79.8 16.5 %collective-permute-start.11 = (bf16[128,256]{1,0:T(8,128)(2,1)}, bf16[128,256]{1,0:T(8,128)(2,1)S(1)}, u32[]{:S(2)}, u32[]{:S(2)}) collective-permute-start(bf16[128,256]{1,0:T(8,128)(2,1)} %get-tuple-element.25), channel_id=1, source_target_pairs={{0,8},{4,12},{8,0},{12,4},{1,9},{5,13},{9,1},{13,5},{2,10},{6,14},... | collective-permute-start | bytes 196616 | tf_op jit(solution)/shard_map/ppermute | solution.py:666
  81.4 11.4 %collective-permute-start.10 = (bf16[128,256]{1,0:T(8,128)(2,1)}, bf16[128,256]{1,0:T(8,128)(2,1)S(1)}, u32[]{:S(2)}, u32[]{:S(2)}) collective-permute-start(bf16[128,256]{1,0:T(8,128)(2,1)} %get-tuple-element.25), channel_id=1, source_target_pairs={{0,2},{2,0},{1,3},{3,1},{4,6},{6,4},{5,7},{7,5},{8,10},{10,8},{9,1... | collective-permute-start | bytes 196616 | tf_op jit(solution)/shard_map/ppermute | solution.py:663
  85.3 21.5 %all-to-all-start.2 = ((bf16[8,256,256]{2,1,0:T(8,128)(2,1)}), bf16[8,256,256]{2,1,0:T(8,128)(2,1)S(1)}, u32[]{:S(2)}, u32[]{:S(2)}) async-start(bf16[8,256,256]{2,1,0:T(8,128)(2,1)} %get-tuple-element.24), calls=%async_computation.2 | async-start | bytes 2097152 | tf_op jit(solution)/shard_map/all_to_all | solution.py:753
  92.8 11.1 %collective-permute-start.15 = (bf16[512,256]{1,0:T(8,128)(2,1)S(1)}, bf16[512,256]{1,0:T(8,128)(2,1)S(1)}, u32[]{:S(2)}, u32[]{:S(2)}) collective-permute-start(bf16[512,256]{1,0:T(8,128)(2,1)S(1)} %constant_dynamic-update-slice_fusion.refs_0_), channel_id=1, source_target_pairs={{0,1},{1,0},{2,3},{3,2},{4,5},{5,4},{6,7},{7,6},{8,9},{9,8},{10,11... | collective-permute-start | bytes 786440 | tf_op jit(solution)/shard_map/ppermute | solution.py:752
  92.9 10.9 %collective-permute-start.14 = (bf16[128,256]{1,0:T(8,128)(2,1)S(1)}, bf16[128,256]{1,0:T(8,128)(2,1)S(1)}, u32[]{:S(2)}, u32[]{:S(2)}) collective-permute-start(bf16[128,256]{1,0:T(8,128)(2,1)S(1)} %collective-permute-done.10), channel_id=1, source_target_pairs={{0,4},{4,8},{8,12},{12,0},{1,5},{5,9},{9,13},{13,1},{2,6},{6,10},{... | collective-permute-start | bytes 196616 | tf_op jit(solution)/shard_map/ppermute | solution.py:669
  116.1 12.7 %collective-permute-start.17 = (bf16[8,128,256]{2,1,0:T(8,128)(2,1)}, bf16[8,128,256]{2,1,0:T(8,128)(2,1)S(1)}, u32[]{:S(2)}, u32[]{:S(2)}) collective-permute-start(bf16[8,128,256]{2,1,0:T(8,128)(2,1)} %get-tuple-element.28), channel_id=1, source_target_pairs={{0,1},{1,0},{2,3},{3,2},{4,5},{5,4},{6,7},{7,6},{8,9},{9,8},{10,11... | collective-permute-start | bytes 1572872 | tf_op jit(solution)/shard_map/ppermute | solution.py:756
  121.8 15.8 %collective-permute-start.19 = (bf16[32,64,128]{2,1,0:T(8,128)(2,1)}, bf16[32,64,128]{2,1,0:T(8,128)(2,1)S(1)}, u32[]{:S(2)}, u32[]{:S(2)}) collective-permute-start(bf16[32,64,128]{2,1,0:T(8,128)(2,1)} %couple.1.refs_0_), channel_id=1, source_target_pairs={{0,16},{16,32},{32,48},{48,0},{1,17},{17,33},{33,49},{49,1},{2,18}... | collective-permute-start | bytes 1572872 | tf_op jit(solution)/shard_map/ppermute | solution.py:678
  123.0 16.5 %collective-permute-start.22 = (bf16[32,64,128]{2,1,0:T(8,128)(2,1)}, bf16[32,64,128]{2,1,0:T(8,128)(2,1)S(1)}, u32[]{:S(2)}, u32[]{:S(2)}) collective-permute-start(bf16[32,64,128]{2,1,0:T(8,128)(2,1)} %couple.1.refs_0_), channel_id=1, source_target_pairs={{0,64},{64,0},{1,65},{65,1},{2,66},{66,2},{3,67},{67,3},{4,68},{68... | collective-permute-start | bytes 1572872 | tf_op jit(solution)/shard_map/ppermute | solution.py:677
  126.6 16.2 %collective-permute-start.18 = (bf16[32,64,128]{2,1,0:T(8,128)(2,1)}, bf16[32,64,128]{2,1,0:T(8,128)(2,1)S(1)}, u32[]{:S(2)}, u32[]{:S(2)}) collective-permute-start(bf16[32,64,128]{2,1,0:T(8,128)(2,1)} %couple.1.refs_0_), channel_id=1, source_target_pairs={{0,48},{16,0},{32,16},{48,32},{1,49},{17,1},{33,17},{49,33},{2,50}... | collective-permute-start | bytes 1572872 | tf_op jit(solution)/shard_map/ppermute | solution.py:679
  131.7 13.5 %all-to-all-start.3 = ((bf16[8,128,256]{2,1,0:T(8,128)(2,1)}), bf16[8,128,256]{2,1,0:T(8,128)(2,1)S(1)}, u32[]{:S(2)}, u32[]{:S(2)}) async-start(bf16[8,128,256]{2,1,0:T(8,128)(2,1)} %fold.1), calls=%async_computation.3 | async-start | bytes 1048576 | tf_op jit(solution)/shard_map/all_to_all | solution.py:760
  138.3 15.2 %collective-permute-start.20 = (bf16[16,64,128]{2,1,0:T(8,128)(2,1)}, bf16[16,64,128]{2,1,0:T(8,128)(2,1)S(1)}, u32[]{:S(2)}, u32[]{:S(2)}) collective-permute-start(bf16[16,64,128]{2,1,0:T(8,128)(2,1)} %slice.8), channel_id=1, source_target_pairs={{0,16},{16,32},{32,48},{48,0},{1,17},{17,33},{33,49},{49,1},{2,18}... | collective-permute-start | bytes 786440 | tf_op jit(solution)/shard_map/ppermute | solution.py:680
  139.5 33.6 %collective-permute-start.26 = (bf16[32,64,128]{2,1,0:T(8,128)(2,1)S(1)}, bf16[32,64,128]{2,1,0:T(8,128)(2,1)S(1)}, u32[]{:S(2)}, u32[]{:S(2)}) collective-permute-start(bf16[32,64,128]{2,1,0:T(8,128)(2,1)S(1)} %collective-permute-done.22.refs_5_), channel_id=1, source_target_pairs={{0,16},{16,32},{32,48},{48,0},{1,17},{17,33},{33,49},{49,1},{2,18}... | collective-permute-start | bytes 1572872 | tf_op jit(solution)/shard_map/ppermute | solution.py:682
  141.4 31.8 %collective-permute-start.23 = (bf16[32,64,128]{2,1,0:T(8,128)(2,1)S(1)}, bf16[32,64,128]{2,1,0:T(8,128)(2,1)S(1)}, u32[]{:S(2)}, u32[]{:S(2)}) collective-permute-start(bf16[32,64,128]{2,1,0:T(8,128)(2,1)S(1)} %collective-permute-done.22.refs_5_), channel_id=1, source_target_pairs={{0,48},{16,0},{32,16},{48,32},{1,49},{17,1},{33,17},{49,33},{2,50}... | collective-permute-start | bytes 1572872 | tf_op jit(solution)/shard_map/ppermute | solution.py:683
  143.6 20.9 %collective-permute-start.21 = (bf16[16,64,128]{2,1,0:T(8,128)(2,1)}, bf16[16,64,128]{2,1,0:T(8,128)(2,1)}, u32[]{:S(2)}, u32[]{:S(2)}) collective-permute-start(bf16[16,64,128]{2,1,0:T(8,128)(2,1)} %slice.9), channel_id=1, source_target_pairs={{0,48},{16,0},{32,16},{48,32},{1,49},{17,1},{33,17},{49,33},{2,50}... | collective-permute-start | bytes 786440 | tf_op jit(solution)/shard_map/ppermute | solution.py:681
  148.2 19.1 %all-to-all-start.4 = ((bf16[8,32,1152]{2,1,0:T(8,128)(2,1)}), bf16[8,32,1152]{2,1,0:T(8,128)(2,1)S(1)}, u32[]{:S(2)}, u32[]{:S(2)}) async-start(bf16[8,32,1152]{2,1,0:T(8,128)(2,1)} %pack_grads.1), calls=%async_computation.4 | async-start | bytes 1179648 | tf_op jit(solution)/shard_map/all_to_all | solution.py:761
  153.5 19.7 %collective-permute-start.24 = (bf16[16,64,128]{2,1,0:T(8,128)(2,1)S(1)}, bf16[16,64,128]{2,1,0:T(8,128)(2,1)}, u32[]{:S(2)}, u32[]{:S(2)}) collective-permute-start(bf16[16,64,128]{2,1,0:T(8,128)(2,1)S(1)} %collective-permute-done.20.refs_2_), channel_id=1, source_target_pairs={{0,64},{64,0},{1,65},{65,1},{2,66},{66,2},{3,67},{67,3},{4,68},{68... | collective-permute-start | bytes 786440 | tf_op jit(solution)/shard_map/ppermute | solution.py:684
  (33 other events, 230.2 us)

commit v4 on v3

--- a/solution.py
+++ b/solution.py
@@ -24,7 +24,7 @@
 VMEM = pl.BlockSpec(memory_space=pltpu.VMEM)
 SMEM = pl.BlockSpec(memory_space=pltpu.SMEM)
 ORDER = pl.BlockSpec(memory_space=pl.ANY)
-ROOM = pltpu.CompilerParams(vmem_limit_bytes=56 * 1024 * 1024)
+ROOM = pltpu.CompilerParams(vmem_limit_bytes=24 * 1024 * 1024)
 
 
 def lasting(microseconds):

time: 180 us -> 174 us (0.967)
  Pallas kernels: 69.6 us -> 46.6 us
  local copies, waits for them, and re-layouts: 15.1 us -> 27.2 us
  waiting for transfers between devices: 27.6 us -> 31.7 us
    unnamed x57 -> x67, local copies, waits for them, and re-layouts: 11.3 us -> 24 us
    pallas_call x2, Pallas kernels: 14.5 us -> 9.35 us  [row_attention(): pl.pallas_call(functools.partial(row_kernel, steps), in_specs=[VMEM] * (6...]
    pallas_call x1, Pallas kernels: 7.64 us -> 4.5 us  [spread_of(): pl.pallas_call(spread_kernel, in_specs=[VMEM] * 3 + [ORDER], out_specs=VM...]
    pallas_call x1, Pallas kernels: 5.2 us -> 2.09 us  [row_entry(): pl.pallas_call(entry_kernel, in_specs=[VMEM] * 4, out_specs=[VMEM] * 4, o...]
    pallas_call x1, Pallas kernels: 8.29 us -> 5.44 us  [factor_grads(): pl.pallas_call(grads_kernel, in_specs=[VMEM] * 6, out_specs=[VMEM] * 5, o...]
    ppermute x1, waiting for transfers between devices: 2.3 us -> 4.77 us  [ring_halves(): below = lax.ppermute(x, along, turn_by(1))]
    pallas_call x1, Pallas kernels: 5.64 us -> 3.41 us  [couple(): pl.pallas_call(couple_kernel, in_specs=[VMEM] * 4, out_specs=VMEM, out_sh...]
    all_to_all x1, waiting for transfers between devices: 3.53 us -> 1.36 us  [per_device(): lax.all_to_all(multiple_alignment_rep.reshape(b_size, seqs_here // b_size...]
  transfers between devices with their start and end apart: 32 -> 32, of which waited for: 12 -> 10; matrix products, arithmetic and copies ran while one was open for 3% -> 2% of each run, Pallas kernels for 23% -> 15%
where the time goes in v4:
time: 174 us; the launch traced here: 172 us
  starting transfers between devices  65.9 us (38%)
  Pallas kernels  46.6 us (27%)
  waiting for transfers between devices  31.7 us (18%)
  local copies, waits for them, and re-layouts  27.2 us (16%)
    unnamed x67, local copies, waits for them, and re-layouts  24 us
    pallas_call x2, Pallas kernels, row_attention(): pl.pallas_call(functools.partial(row_kernel, steps), in_specs=[VMEM] * (6...  9.35 us
    all_to_all x1, starting transfers between devices, per_device(): lax.all_to_all(after_row.reshape(q_size * b_size, 16, depth), ('x_hi', 'z...  8.64 us
    ppermute x1, waiting for transfers between devices, ring_halves(): far_high = lax.ppermute(above[half:], along, turn_by(3))  8.58 us
    pallas_call x1, Pallas kernels, col_attention(): pl.pallas_call(col_kernel, in_specs=[VMEM] * 2 + [SMEM] + [VMEM] * 3 + [O...  6.58 us
    ppermute x2, starting transfers between devices, ring(): partner_above = lax.ppermute(partner, along, turn_by(3))  6.46 us
    ppermute x2, waiting for transfers between devices, ring(): partner_far = lax.ppermute(far, across, SWAP)  6.35 us
    all_to_all x1, starting transfers between devices, per_device(): lax.all_to_all(pack_grads(ga, gb, q_size), ('x_hi', 'z'), 0, 0, tiled=True)  5.53 us
  transfers between devices with their start and end apart: 32, of which 10 were waited for; matrix products, arithmetic and copies ran while one was open for 2% of the time, Pallas kernels for 15%

profile of v4, /device:TPU:0, one launch (start us, length us, event | category | flops | bytes accessed | tf_op | source)
XLA Modules:
  0.0 172.5 jit_solution(16262278304722030213)
XLA Ops:
  0.6 5.5 %all-to-all-start = ((bf16[8,4,32,256]{3,2,1,0:T(8,128)(2,1)}), bf16[8,4,32,256]{3,2,1,0:T(8,128)(2,1)S(1)}, u32[]{:S(2)}, u32[]{:S(2)}) async-start(bf16[8,4,32,256]{3,2,1,0:T(8,128)(2,1)} %bitcast.30), calls=%async_computation | async-start | bytes 1048576 | tf_op jit(solution)/shard_map/all_to_all | solution.py:723
  9.7 4.5 %pair_bias.1.refs_1_.refs_0_ = bf16[256,512]{1,0:T(8,128)(2,1)S(1)} custom-call(bf16[32,512,128]{2,1,0:T(8,128)(2,1)S(1)} %copy-done.9, bf16[8,128]{1,0:T(8,128)(2,1)S(1)} %bitcast.28, s32[1,512]{1,0:T(1,128)S(1)} %bitcast.22), custom_call_target="tpu_custom_call" | custom-call | bytes 33210000 | tf_op jit(solution)/shard_map/pair_bias/pallas_call | solution.py:111
  31.8 3.2 %collective-permute-start.3 = (bf16[256,512]{1,0:T(8,128)(2,1)}, bf16[256,512]{1,0:T(8,128)(2,1)S(1)}, u32[]{:S(2)}, u32[]{:S(2)}) collective-permute-start(bf16[256,512]{1,0:T(8,128)(2,1)} %get-tuple-element.23.refs_3_), channel_id=1, source_target_pairs={{0,12},{4,0},{8,4},{12,8},{1,13},{5,1},{9,5},{13,9},{2,14},{6,2},{... | collective-permute-start | bytes 786440 | tf_op jit(solution)/shard_map/ppermute | solution.py:670
  40.2 4.8 %row_attention.2.refs_4_ = bf16[8,8,16,256]{3,2,1,0:T(8,128)(2,1)S(1)} custom-call(bf16[4,256,256]{2,1,0:T(8,128)(2,1)S(1)} %copy-done.8, bf16[4,512,256]{2,1,0:T(8,128)(2,1)S(1)} %copy-done.11, bf16[4,2,512,256]{3,2,1,0:T(8,128)(2,1)S(1)} %get-tuple-element.20.v_ref, bf16[4,256,256]{2,1,0:T(8,128)(2,1)S(1)} %get-tuple-element.21.g_ref, ...), custom_call_target="tpu_custom_call" | custom-call | bytes 29520000 | tf_op jit(solution)/shard_map/row_attention/pallas_call | solution.py:255
  45.1 4.5 %row_attention.3._ = bf16[8,8,16,256]{3,2,1,0:T(8,128)(2,1)} custom-call(bf16[4,256,256]{2,1,0:T(8,128)(2,1)S(1)} %copy-done.8, bf16[4,512,256]{2,1,0:T(8,128)(2,1)S(1)} %copy-done.11, bf16[4,2,512,256]{3,2,1,0:T(8,128)(2,1)S(1)} %get-tuple-element.20.v_ref, bf16[4,256,256]{2,1,0:T(8,128)(2,1)S(1)} %get-tuple-element.21.g_ref, ...), custom_call_target="tpu_custom_call" | custom-call | bytes 29520000 | tf_op jit(solution)/shard_map/row_attention/pallas_call | solution.py:255
  49.7 8.6 %all-to-all-start.1 = ((bf16[64,16,256]{2,1,0:T(8,128)(2,1)}), bf16[64,16,256]{2,1,0:T(8,128)(2,1)S(1)}, u32[]{:S(2)}, u32[]{:S(2)}) async-start(bf16[64,16,256]{2,1,0:T(8,128)(2,1)} %bitcast.3), calls=%async_computation.1 | async-start | bytes 1048576 | tf_op jit(solution)/shard_map/all_to_all | solution.py:742
  60.8 4.5 %spread.1._.s_ref = bf16[1024,2048]{1,0:T(8,128)(2,1)S(1)} custom-call(bf16[32,64,128]{2,1,0:T(8,128)(2,1)S(1)} %bitcast.19, bf16[512,256]{1,0:T(8,128)(2,1)S(1)} %bitcast.17, s32[1,256]{1,0:T(1,128)S(1)} %bitcast.24, bf16[8,8,16,256]{3,2,1,0:T(8,128)(2,1)} %row_attention.3._), custom_call_target="tpu_custom_call" | custom-call | bytes 29520000 | tf_op jit(solution)/shard_map/spread/pallas_call | solution.py:422
  67.4 3.7 %all-to-all-done.1.y_ref = bf16[64,16,256]{2,1,0:T(8,128)(2,1)S(1)} async-done(((bf16[64,16,256]{2,1,0:T(8,128)(2,1)}), bf16[64,16,256]{2,1,0:T(8,128)(2,1)S(1)}, u32[]{:S(2)}, u32[]{:S(2)}) %all-to-all-start.1) | async-done | bytes 524320 | tf_op jit(solution)/shard_map/all_to_all | solution.py:742
  73.3 6.6 %col_attention.1 = (bf16[8,256,256]{2,1,0:T(8,128)(2,1)}, bf16[128,256]{1,0:T(8,128)(2,1)S(1)}) custom-call(bf16[64,16,256]{2,1,0:T(8,128)(2,1)S(1)} %all-to-all-done.1.y_ref, s32[1,256]{1,0:T(1,128)S(1)} %bitcast.25, s32[512]{0:T(512)S(1)} %copy-done.27, bf16[256,1024]{1,0:T(8,128)(2,1)S(1)} %copy-done.23, bf16[256,256]{1,0:T(8,128)(2,1)S(1)} %copy-done.25, ...), custom_call_target="tpu_custom_call" | custom-call | bytes 29520000 | tf_op jit(solution)/shard_map/col_attention/pallas_call | solution.py:328
  82.5 2.8 %collective-permute-start.8 = (bf16[128,256]{1,0:T(8,128)(2,1)S(1)}, bf16[128,256]{1,0:T(8,128)(2,1)S(1)}, u32[]{:S(2)}, u32[]{:S(2)}) collective-permute-start(bf16[128,256]{1,0:T(8,128)(2,1)S(1)} %get-tuple-element.25), channel_id=1, source_target_pairs={{0,12},{4,0},{8,4},{12,8},{1,13},{5,1},{9,5},{13,9},{2,14},{6,2},{... | collective-permute-start | bytes 196616 | tf_op jit(solution)/shard_map/ppermute | solution.py:665
  85.3 5.2 %all-to-all-start.2 = ((bf16[8,256,256]{2,1,0:T(8,128)(2,1)}), bf16[8,256,256]{2,1,0:T(8,128)(2,1)S(1)}, u32[]{:S(2)}, u32[]{:S(2)}) async-start(bf16[8,256,256]{2,1,0:T(8,128)(2,1)} %get-tuple-element.24), calls=%async_computation.2 | async-start | bytes 2097152 | tf_op jit(solution)/shard_map/all_to_all | solution.py:753
  90.8 3.2 %collective-permute-start.12 = (bf16[128,256]{1,0:T(8,128)(2,1)S(1)}, bf16[128,256]{1,0:T(8,128)(2,1)S(1)}, u32[]{:S(2)}, u32[]{:S(2)}) collective-permute-start(bf16[128,256]{1,0:T(8,128)(2,1)S(1)} %collective-permute-done.10), channel_id=1, source_target_pairs={{0,12},{4,0},{8,4},{12,8},{1,13},{5,1},{9,5},{13,9},{2,14},{6,2},{... | collective-permute-start | bytes 196616 | tf_op jit(solution)/shard_map/ppermute | solution.py:670
  95.9 6.3 %collective-permute-done.13 = bf16[128,256]{1,0:T(8,128)(2,1)S(1)} collective-permute-done((bf16[128,256]{1,0:T(8,128)(2,1)S(1)}, bf16[128,256]{1,0:T(8,128)(2,1)S(1)}, u32[]{:S(2)}, u32[]{:S(2)}) %collective-permute-start.13) | collective-permute-done | bytes 65568 | tf_op jit(solution)/shard_map/ppermute | solution.py:671
  107.5 5.4 %factor_grads.1 = (bf16[1024,256]{1,0:T(8,128)(2,1)S(1)}, bf16[2048,256]{1,0:T(8,128)(2,1)S(1)}, bf16[256,1024]{1,0:T(8,128)(2,1)S(1)}, bf16[8,128,256]{2,1,0:T(8,128)(2,1)S(1)}, bf16[8,128,256]{2,1,0:T(8,128)(2,1)S(1)}) custom-call(bf16[8,256,256]{2,1,0:T(8,128)(2,1)S(1)} %all-to-all-done.2.both_ref.x_ref, bf16[1024,2048]{1,0:T(8,128)(2,1)S(1)} %copy-done.2, ...), custom_call_target="tpu_custom_call" | custom-call | bytes 33210000 | tf_op jit(solution)/shard_map/factor_grads/pallas_call | solution.py:515
  113.0 3.4 %couple.1.refs_0_ = bf16[32,64,128]{2,1,0:T(8,128)(2,1)S(1)} custom-call(bf16[1024,256]{1,0:T(8,128)(2,1)S(1)} %get-tuple-element.30.a_ref, bf16[2048,256]{1,0:T(8,128)(2,1)S(1)} %get-tuple-element.31.bd_ref, bf16[512,256]{1,0:T(8,128)(2,1)S(1)} %bitcast.18, s32[1,256]{1,0:T(1,128)S(1)} %bitcast.26), custom_call_target="tpu_custom_call" | custom-call | bytes 22140000 | tf_op jit(solution)/shard_map/couple/pallas_call | solution.py:463
  117.3 3.3 %collective-permute-start.22 = (bf16[32,64,128]{2,1,0:T(8,128)(2,1)S(1)}, bf16[32,64,128]{2,1,0:T(8,128)(2,1)}, u32[]{:S(2)}, u32[]{:S(2)}) collective-permute-start(bf16[32,64,128]{2,1,0:T(8,128)(2,1)S(1)} %couple.1.refs_0_), channel_id=1, source_target_pairs={{0,64},{64,0},{1,65},{65,1},{2,66},{66,2},{3,67},{67,3},{4,68},{68... | collective-permute-start | bytes 1572872 | tf_op jit(solution)/shard_map/ppermute | solution.py:677
  123.8 3.5 %all-to-all-start.3 = ((bf16[8,128,256]{2,1,0:T(8,128)(2,1)}), bf16[8,128,256]{2,1,0:T(8,128)(2,1)S(1)}, u32[]{:S(2)}, u32[]{:S(2)}) async-start(bf16[8,128,256]{2,1,0:T(8,128)(2,1)} %fold.1), calls=%async_computation.3 | async-start | bytes 1048576 | tf_op jit(solution)/shard_map/all_to_all | solution.py:760
  127.3 4.8 %collective-permute-done.19.refs_4_ = bf16[32,64,128]{2,1,0:T(8,128)(2,1)S(1)} collective-permute-done((bf16[32,64,128]{2,1,0:T(8,128)(2,1)S(1)}, bf16[32,64,128]{2,1,0:T(8,128)(2,1)S(1)}, u32[]{:S(2)}, u32[]{:S(2)}) %collective-permute-start.19) | collective-permute-done | bytes 524320 | tf_op jit(solution)/shard_map/ppermute | solution.py:678
  140.9 5.5 %all-to-all-start.4 = ((bf16[8,32,1152]{2,1,0:T(8,128)(2,1)}), bf16[8,32,1152]{2,1,0:T(8,128)(2,1)S(1)}, u32[]{:S(2)}, u32[]{:S(2)}) async-start(bf16[8,32,1152]{2,1,0:T(8,128)(2,1)} %pack_grads.1), calls=%async_computation.4 | async-start | bytes 1179648 | tf_op jit(solution)/shard_map/all_to_all | solution.py:761
  146.4 3.5 %collective-permute-start.24 = (bf16[16,64,128]{2,1,0:T(8,128)(2,1)}, bf16[16,64,128]{2,1,0:T(8,128)(2,1)}, u32[]{:S(2)}, u32[]{:S(2)}) collective-permute-start(bf16[16,64,128]{2,1,0:T(8,128)(2,1)} %collective-permute-done.20.refs_2_), channel_id=1, source_target_pairs={{0,64},{64,0},{1,65},{65,1},{2,66},{66,2},{3,67},{67,3},{4,68},{68... | collective-permute-start | bytes 786440 | tf_op jit(solution)/shard_map/ppermute | solution.py:684
  149.9 8.6 %collective-permute-done.21.refs_3_ = bf16[16,64,128]{2,1,0:T(8,128)(2,1)} collective-permute-done((bf16[16,64,128]{2,1,0:T(8,128)(2,1)}, bf16[16,64,128]{2,1,0:T(8,128)(2,1)}, u32[]{:S(2)}, u32[]{:S(2)}) %collective-permute-start.21) | collective-permute-done | bytes 262176 | tf_op jit(solution)/shard_map/ppermute | solution.py:681
  158.5 2.9 %collective-permute-start.25 = (bf16[16,64,128]{2,1,0:T(8,128)(2,1)}, bf16[16,64,128]{2,1,0:T(8,128)(2,1)}, u32[]{:S(2)}, u32[]{:S(2)}) collective-permute-start(bf16[16,64,128]{2,1,0:T(8,128)(2,1)} %collective-permute-done.21.refs_3_), channel_id=1, source_target_pairs={{0,64},{64,0},{1,65},{65,1},{2,66},{66,2},{3,67},{67,3},{4,68},{68... | collective-permute-start | bytes 786440 | tf_op jit(solution)/shard_map/ppermute | solution.py:685
  161.4 4.1 %finish_home.1 = (bf16[32,32,256]{2,1,0:T(8,128)(2,1)}, bf16[32,32,256]{2,1,0:T(8,128)(2,1)}) custom-call(bf16[8,32,1152]{2,1,0:T(8,128)(2,1)S(1)} %all-to-all-done.4.gf_ref, bf16[64,256]{1,0:T(8,128)(2,1)S(1)} %bitcast.21, bf16[8,256,256]{2,1,0:T(8,128)(2,1)S(1)} %all-to-all-done.2.both_ref.x_ref, s32[1,256]{1,0:T(1,128)S(1)} %bitcast.27, s32[512]{0:T(512)S(1)} %copy-done.27), custom_call_target="tpu_custom_call" | custom-call | bytes 22140000 | tf_op jit(solution)/shard_map/finish_home/pallas_call | solution.py:625
  167.7 4.7 %assemble.1 = bf16[32,512,128]{2,1,0:T(8,128)(2,1)} custom-call(bf16[32,64,128]{2,1,0:T(8,128)(2,1)S(1)} %couple.1.refs_0_, bf16[32,64,128]{2,1,0:T(8,128)(2,1)S(1)} %collective-permute-done.18.refs_1_, bf16[16,64,128]{2,1,0:T(8,128)(2,1)} %collective-permute-done.20.refs_2_, bf16[16,64,128]{2,1,0:T(8,128)(2,1)} %collective-permute-done.21.refs_3_, ...), custom_call_target="tpu_custom_call" | custom-call | bytes 18450000 | tf_op jit(solution)/shard_map/assemble/pallas_call | solution.py:381
  (127 shorter events, 58.0 us)
Async XLA Ops:
  0.6 15.6 %all-to-all-start = ((bf16[8,4,32,256]{3,2,1,0:T(8,128)(2,1)}), bf16[8,4,32,256]{3,2,1,0:T(8,128)(2,1)S(1)}, u32[]{:S(2)}, u32[]{:S(2)}) async-start(bf16[8,4,32,256]{3,2,1,0:T(8,128)(2,1)} %bitcast.30), calls=%async_computation | async-start | bytes 1048576 | tf_op jit(solution)/shard_map/all_to_all | solution.py:723
  17.0 12.8 %collective-permute-start.2 = (bf16[256,512]{1,0:T(8,128)(2,1)}, bf16[256,512]{1,0:T(8,128)(2,1)S(1)}, u32[]{:S(2)}, u32[]{:S(2)}) collective-permute-start(bf16[256,512]{1,0:T(8,128)(2,1)} %copy-done.12), channel_id=1, source_target_pairs={{0,8},{4,12},{8,0},{12,4},{1,9},{5,13},{9,1},{13,5},{2,10},{6,14},... | collective-permute-start | bytes 786440 | tf_op jit(solution)/shard_map/ppermute | solution.py:666
  19.2 10.7 %collective-permute-start.1 = (bf16[256,512]{1,0:T(8,128)(2,1)}, bf16[256,512]{1,0:T(8,128)(2,1)S(1)}, u32[]{:S(2)}, u32[]{:S(2)}) collective-permute-start(bf16[256,512]{1,0:T(8,128)(2,1)} %copy-done.12), channel_id=1, source_target_pairs={{0,2},{2,0},{1,3},{3,1},{4,6},{6,4},{5,7},{7,5},{8,10},{10,8},{9,1... | collective-permute-start | bytes 786440 | tf_op jit(solution)/shard_map/ppermute | solution.py:663
  20.6 14.4 %collective-permute-start.7 = (bf16[256,512]{1,0:T(8,128)(2,1)}, bf16[256,512]{1,0:T(8,128)(2,1)}, u32[]{:S(2)}, u32[]{:S(2)}) collective-permute-start(bf16[256,512]{1,0:T(8,128)(2,1)} %copy-done.12), channel_id=1, source_target_pairs={{0,4},{4,8},{8,12},{12,0},{1,5},{5,9},{9,13},{13,1},{2,6},{6,10},{... | collective-permute-start | bytes 786440 | tf_op jit(solution)/shard_map/ppermute | solution.py:664
  21.2 13.8 %collective-permute-start.6 = (bf16[256,512]{1,0:T(8,128)(2,1)}, bf16[256,512]{1,0:T(8,128)(2,1)}, u32[]{:S(2)}, u32[]{:S(2)}) collective-permute-start(bf16[256,512]{1,0:T(8,128)(2,1)} %copy-done.12), channel_id=1, source_target_pairs={{0,12},{4,0},{8,4},{12,8},{1,13},{5,1},{9,5},{13,9},{2,14},{6,2},{... | collective-permute-start | bytes 786440 | tf_op jit(solution)/shard_map/ppermute | solution.py:665
  31.2 13.8 %collective-permute-start.4 = (bf16[256,512]{1,0:T(8,128)(2,1)}, bf16[256,512]{1,0:T(8,128)(2,1)S(1)}, u32[]{:S(2)}, u32[]{:S(2)}) collective-permute-start(bf16[256,512]{1,0:T(8,128)(2,1)} %get-tuple-element.22.refs_0_), channel_id=1, source_target_pairs={{0,2},{2,0},{1,3},{3,1},{4,6},{6,4},{5,7},{7,5},{8,10},{10,8},{9,1... | collective-permute-start | bytes 786440 | tf_op jit(solution)/shard_map/ppermute | solution.py:671
  31.8 13.3 %collective-permute-start.5 = (bf16[256,512]{1,0:T(8,128)(2,1)}, bf16[256,512]{1,0:T(8,128)(2,1)S(1)}, u32[]{:S(2)}, u32[]{:S(2)}) collective-permute-start(bf16[256,512]{1,0:T(8,128)(2,1)} %get-tuple-element.23.refs_3_), channel_id=1, source_target_pairs={{0,4},{4,8},{8,12},{12,0},{1,5},{5,9},{9,13},{13,1},{2,6},{6,10},{... | collective-permute-start | bytes 786440 | tf_op jit(solution)/shard_map/ppermute | solution.py:669
  31.8 13.3 %collective-permute-start.3 = (bf16[256,512]{1,0:T(8,128)(2,1)}, bf16[256,512]{1,0:T(8,128)(2,1)S(1)}, u32[]{:S(2)}, u32[]{:S(2)}) collective-permute-start(bf16[256,512]{1,0:T(8,128)(2,1)} %get-tuple-element.23.refs_3_), channel_id=1, source_target_pairs={{0,12},{4,0},{8,4},{12,8},{1,13},{5,1},{9,5},{13,9},{2,14},{6,2},{... | collective-permute-start | bytes 786440 | tf_op jit(solution)/shard_map/ppermute | solution.py:670
  49.7 21.4 %all-to-all-start.1 = ((bf16[64,16,256]{2,1,0:T(8,128)(2,1)}), bf16[64,16,256]{2,1,0:T(8,128)(2,1)S(1)}, u32[]{:S(2)}, u32[]{:S(2)}) async-start(bf16[64,16,256]{2,1,0:T(8,128)(2,1)} %bitcast.3), calls=%async_computation.1 | async-start | bytes 1048576 | tf_op jit(solution)/shard_map/all_to_all | solution.py:742
  79.9 14.1 %collective-permute-start.11 = (bf16[128,256]{1,0:T(8,128)(2,1)S(1)}, bf16[128,256]{1,0:T(8,128)(2,1)S(1)}, u32[]{:S(2)}, u32[]{:S(2)}) collective-permute-start(bf16[128,256]{1,0:T(8,128)(2,1)S(1)} %get-tuple-element.25), channel_id=1, source_target_pairs={{0,8},{4,12},{8,0},{12,4},{1,9},{5,13},{9,1},{13,5},{2,10},{6,14},... | collective-permute-start | bytes 196616 | tf_op jit(solution)/shard_map/ppermute | solution.py:666
  85.3 20.0 %all-to-all-start.2 = ((bf16[8,256,256]{2,1,0:T(8,128)(2,1)}), bf16[8,256,256]{2,1,0:T(8,128)(2,1)S(1)}, u32[]{:S(2)}, u32[]{:S(2)}) async-start(bf16[8,256,256]{2,1,0:T(8,128)(2,1)} %get-tuple-element.24), calls=%async_computation.2 | async-start | bytes 2097152 | tf_op jit(solution)/shard_map/all_to_all | solution.py:753
  90.6 11.8 %collective-permute-start.15 = (bf16[512,256]{1,0:T(8,128)(2,1)S(1)}, bf16[512,256]{1,0:T(8,128)(2,1)S(1)}, u32[]{:S(2)}, u32[]{:S(2)}) collective-permute-start(bf16[512,256]{1,0:T(8,128)(2,1)S(1)} %constant_dynamic-update-slice_fusion.refs_0_), channel_id=1, source_target_pairs={{0,1},{1,0},{2,3},{3,2},{4,5},{5,4},{6,7},{7,6},{8,9},{9,8},{10,11... | collective-permute-start | bytes 786440 | tf_op jit(solution)/shard_map/ppermute | solution.py:752
  90.7 11.6 %collective-permute-start.14 = (bf16[128,256]{1,0:T(8,128)(2,1)S(1)}, bf16[128,256]{1,0:T(8,128)(2,1)S(1)}, u32[]{:S(2)}, u32[]{:S(2)}) collective-permute-start(bf16[128,256]{1,0:T(8,128)(2,1)S(1)} %collective-permute-done.10), channel_id=1, source_target_pairs={{0,4},{4,8},{8,12},{12,0},{1,5},{5,9},{9,13},{13,1},{2,6},{6,10},{... | collective-permute-start | bytes 196616 | tf_op jit(solution)/shard_map/ppermute | solution.py:669
  112.9 9.9 %collective-permute-start.17 = (bf16[8,128,256]{2,1,0:T(8,128)(2,1)S(1)}, bf16[8,128,256]{2,1,0:T(8,128)(2,1)S(1)}, u32[]{:S(2)}, u32[]{:S(2)}) collective-permute-start(bf16[8,128,256]{2,1,0:T(8,128)(2,1)S(1)} %get-tuple-element.28), channel_id=1, source_target_pairs={{0,1},{1,0},{2,3},{3,2},{4,5},{5,4},{6,7},{7,6},{8,9},{9,8},{10,11... | collective-permute-start | bytes 1572872 | tf_op jit(solution)/shard_map/ppermute | solution.py:756
  116.4 15.6 %collective-permute-start.19 = (bf16[32,64,128]{2,1,0:T(8,128)(2,1)S(1)}, bf16[32,64,128]{2,1,0:T(8,128)(2,1)S(1)}, u32[]{:S(2)}, u32[]{:S(2)}) collective-permute-start(bf16[32,64,128]{2,1,0:T(8,128)(2,1)S(1)} %couple.1.refs_0_), channel_id=1, source_target_pairs={{0,16},{16,32},{32,48},{48,0},{1,17},{17,33},{33,49},{49,1},{2,18}... | collective-permute-start | bytes 1572872 | tf_op jit(solution)/shard_map/ppermute | solution.py:678
  117.3 16.4 %collective-permute-start.22 = (bf16[32,64,128]{2,1,0:T(8,128)(2,1)S(1)}, bf16[32,64,128]{2,1,0:T(8,128)(2,1)}, u32[]{:S(2)}, u32[]{:S(2)}) collective-permute-start(bf16[32,64,128]{2,1,0:T(8,128)(2,1)S(1)} %couple.1.refs_0_), channel_id=1, source_target_pairs={{0,64},{64,0},{1,65},{65,1},{2,66},{66,2},{3,67},{67,3},{4,68},{68... | collective-permute-start | bytes 1572872 | tf_op jit(solution)/shard_map/ppermute | solution.py:677
  120.6 16.3 %collective-permute-start.18 = (bf16[32,64,128]{2,1,0:T(8,128)(2,1)S(1)}, bf16[32,64,128]{2,1,0:T(8,128)(2,1)S(1)}, u32[]{:S(2)}, u32[]{:S(2)}) collective-permute-start(bf16[32,64,128]{2,1,0:T(8,128)(2,1)S(1)} %couple.1.refs_0_), channel_id=1, source_target_pairs={{0,48},{16,0},{32,16},{48,32},{1,49},{17,1},{33,17},{49,33},{2,50}... | collective-permute-start | bytes 1572872 | tf_op jit(solution)/shard_map/ppermute | solution.py:679
  123.8 15.1 %all-to-all-start.3 = ((bf16[8,128,256]{2,1,0:T(8,128)(2,1)}), bf16[8,128,256]{2,1,0:T(8,128)(2,1)S(1)}, u32[]{:S(2)}, u32[]{:S(2)}) async-start(bf16[8,128,256]{2,1,0:T(8,128)(2,1)} %fold.1), calls=%async_computation.3 | async-start | bytes 1048576 | tf_op jit(solution)/shard_map/all_to_all | solution.py:760
  132.1 14.3 %collective-permute-start.20 = (bf16[16,64,128]{2,1,0:T(8,128)(2,1)S(1)}, bf16[16,64,128]{2,1,0:T(8,128)(2,1)}, u32[]{:S(2)}, u32[]{:S(2)}) collective-permute-start(bf16[16,64,128]{2,1,0:T(8,128)(2,1)S(1)} %slice.8), channel_id=1, source_target_pairs={{0,16},{16,32},{32,48},{48,0},{1,17},{17,33},{33,49},{49,1},{2,18}... | collective-permute-start | bytes 786440 | tf_op jit(solution)/shard_map/ppermute | solution.py:680
  133.6 31.9 %collective-permute-start.26 = (bf16[32,64,128]{2,1,0:T(8,128)(2,1)}, bf16[32,64,128]{2,1,0:T(8,128)(2,1)}, u32[]{:S(2)}, u32[]{:S(2)}) collective-permute-start(bf16[32,64,128]{2,1,0:T(8,128)(2,1)} %collective-permute-done.22.refs_5_), channel_id=1, source_target_pairs={{0,16},{16,32},{32,48},{48,0},{1,17},{17,33},{33,49},{49,1},{2,18}... | collective-permute-start | bytes 1572872 | tf_op jit(solution)/shard_map/ppermute | solution.py:682
  135.3 30.3 %collective-permute-start.23 = (bf16[32,64,128]{2,1,0:T(8,128)(2,1)}, bf16[32,64,128]{2,1,0:T(8,128)(2,1)}, u32[]{:S(2)}, u32[]{:S(2)}) collective-permute-start(bf16[32,64,128]{2,1,0:T(8,128)(2,1)} %collective-permute-done.22.refs_5_), channel_id=1, source_target_pairs={{0,48},{16,0},{32,16},{48,32},{1,49},{17,1},{33,17},{49,33},{2,50}... | collective-permute-start | bytes 1572872 | tf_op jit(solution)/shard_map/ppermute | solution.py:683
  137.6 20.9 %collective-permute-start.21 = (bf16[16,64,128]{2,1,0:T(8,128)(2,1)}, bf16[16,64,128]{2,1,0:T(8,128)(2,1)}, u32[]{:S(2)}, u32[]{:S(2)}) collective-permute-start(bf16[16,64,128]{2,1,0:T(8,128)(2,1)} %slice.9), channel_id=1, source_target_pairs={{0,48},{16,0},{32,16},{48,32},{1,49},{17,1},{33,17},{49,33},{2,50}... | collective-permute-start | bytes 786440 | tf_op jit(solution)/shard_map/ppermute | solution.py:681
  140.9 20.6 %all-to-all-start.4 = ((bf16[8,32,1152]{2,1,0:T(8,128)(2,1)}), bf16[8,32,1152]{2,1,0:T(8,128)(2,1)S(1)}, u32[]{:S(2)}, u32[]{:S(2)}) async-start(bf16[8,32,1152]{2,1,0:T(8,128)(2,1)} %pack_grads.1), calls=%async_computation.4 | async-start | bytes 1179648 | tf_op jit(solution)/shard_map/all_to_all | solution.py:761
  146.4 19.2 %collective-permute-start.24 = (bf16[16,64,128]{2,1,0:T(8,128)(2,1)}, bf16[16,64,128]{2,1,0:T(8,128)(2,1)}, u32[]{:S(2)}, u32[]{:S(2)}) collective-permute-start(bf16[16,64,128]{2,1,0:T(8,128)(2,1)} %collective-permute-done.20.refs_2_), channel_id=1, source_target_pairs={{0,64},{64,0},{1,65},{65,1},{2,66},{66,2},{3,67},{67,3},{4,68},{68... | collective-permute-start | bytes 786440 | tf_op jit(solution)/shard_map/ppermute | solution.py:684
  (38 other events, 236.7 us)

commit v5 on v4

--- a/solution.py
+++ b/solution.py
@@ -24,6 +24,7 @@
 VMEM = pl.BlockSpec(memory_space=pltpu.VMEM)
 SMEM = pl.BlockSpec(memory_space=pltpu.SMEM)
 ORDER = pl.BlockSpec(memory_space=pl.ANY)
+TOKEN = jax.ShapeDtypeStruct((8, 128), jnp.float32)
 ROOM = pltpu.CompilerParams(vmem_limit_bytes=24 * 1024 * 1024)
 
 
@@ -72,7 +73,8 @@
     return 1.0 / jnp.sum(member.astype(F32), keepdims=True)
 
 
-def bias_kernel(pair_ref, proj_ref, valid_ref, out_ref, turn_s):
+def bias_kernel(pair_ref, proj_ref, valid_ref, out_ref, token_ref, turn_s):
+    token_ref[...] = jnp.zeros_like(token_ref)
     at = pl.program_id(0)
     rows, residues, depth = pair_ref.shape
     line = lax.broadcasted_iota(jnp.int32, (depth, depth), 0)
@@ -116,10 +118,13 @@
             pl.BlockSpec((H, depth), lambda g: (0, 0)),
             pl.BlockSpec((1, residues), lambda g: (0, 0)),
         ],
-        out_specs=pl.BlockSpec((rows * H, residues), lambda g: (0, 0)),
-        out_shape=jax.ShapeDtypeStruct((rows * H, residues), BF16),
+        out_specs=[
+            pl.BlockSpec((rows * H, residues), lambda g: (0, 0)),
+            pl.BlockSpec(TOKEN.shape, lambda g: (0, 0)),
+        ],
+        out_shape=[jax.ShapeDtypeStruct((rows * H, residues), BF16), TOKEN],
         scratch_shapes=[pltpu.VMEM((residues // 128, rows * H, 128), F32)],
-        compiler_params=ROOM,
+        compiler_params=pltpu.CompilerParams(vmem_limit_bytes=56 * 1024 * 1024),
         cost_estimate=lasting(9),
         name="pair_bias",
     )(pair, proj, valid)
@@ -146,7 +151,8 @@
     return summed / total
 
 
-def entry_kernel(x_ref, other_ref, valid_ref, w_ref, q_ref, k_ref, v_ref, g_ref, live_s):
+def entry_kernel(x_ref, other_ref, valid_ref, w_ref, q_ref, k_ref, v_ref, g_ref, token_ref, live_s):
+    token_ref[...] = jnp.zeros_like(token_ref)
     blocks, seqs, rows, depth = x_ref.shape
     core = lax.axis_index("core")
     v_ref[:, :, :, 128:] = jnp.ones(v_ref.shape[:3] + (128,), BF16)
@@ -179,8 +185,8 @@
     return pl.pallas_call(
         entry_kernel,
         in_specs=[VMEM] * 4,
-        out_specs=[VMEM] * 4,
-        out_shape=[here, full, sides, here],
+        out_specs=[VMEM] * 5,
+        out_shape=[here, full, sides, here, TOKEN],
         scratch_shapes=[pltpu.VMEM((2 * blocks * rows, 128), F32)],
         compiler_params=ROOM,
         cost_estimate=lasting(5),
@@ -391,7 +397,8 @@
     )(*pieces, after)
 
 
-def spread_kernel(g_ref, w_ref, member_ref, _, out_ref):
+def spread_kernel(g_ref, w_ref, member_ref, _, out_ref, token_ref):
+    token_ref[...] = jnp.zeros_like(token_ref)
     width = FACTOR_WIDTH
     scale = scale_of(member_ref[...])
     blank = jnp.zeros((64, 128), BF16)
@@ -422,8 +429,11 @@
     return pl.pallas_call(
         spread_kernel,
         in_specs=[VMEM] * 3 + [ORDER],
-        out_specs=VMEM,
-        out_shape=jax.ShapeDtypeStruct((rows * FACTOR_WIDTH, columns * FACTOR_WIDTH), BF16),
+        out_specs=[VMEM] * 2,
+        out_shape=[
+            jax.ShapeDtypeStruct((rows * FACTOR_WIDTH, columns * FACTOR_WIDTH), BF16),
+            TOKEN,
+        ],
         compiler_params=ROOM,
         cost_estimate=lasting(8),
         name="spread",
@@ -474,8 +484,10 @@
     )(a_all, bd, w, member)
 
 
-def grads_kernel(both_ref, s_ref, *refs):
-    b_pieces, (a_ref, bd_ref, ga_ref, own_ref, other_ref, turned_s) = refs[:4], refs[4:]
+def grads_kernel(both_ref, spread_ref, *refs):
+    b_pieces, (a_ref, bd_ref, ga_ref, own_ref, other_ref, turned_s, s_ref, done) = refs[:4], refs[4:]
+    fetch = pltpu.make_async_copy(spread_ref, s_ref, done)
+    fetch.start()
     width = FACTOR_WIDTH
     blocks = own_ref.shape[0]
     columns = turned_s.shape[1] // width
@@ -494,6 +506,7 @@
         bd_ref[here, :] = take(turned_s, pl.ds(at, columns, stride=width)).astype(BF16)
     a_ref[...] = both_ref[:, 128:].reshape(a_ref.shape)
     left = a_ref[...].astype(F32).T.astype(BF16)
+    fetch.wait()
     for at in range(columns * width // 256):
         here = slice(256 * at, 256 * at + 256)
         put(turned_s, here, nn(left, s_ref[:, here]).T)
@@ -514,7 +527,7 @@
     shape = jax.ShapeDtypeStruct((columns // 256, 128, seqs), BF16)
     return pl.pallas_call(
         grads_kernel,
-        in_specs=[VMEM] * 6,
+        in_specs=[VMEM, pl.BlockSpec(memory_space=pl.ANY)] + [VMEM] * 4,
         out_specs=[VMEM] * 5,
         out_shape=[
             jax.ShapeDtypeStruct((rows, seqs), BF16),
@@ -523,7 +536,11 @@
             shape,
             shape,
         ],
-        scratch_shapes=[pltpu.VMEM((2, columns, seqs // 2), F32)],
+        scratch_shapes=[
+            pltpu.VMEM((2, columns, seqs // 2), F32),
+            pltpu.VMEM((rows, columns), BF16),
+            pltpu.SemaphoreType.DMA(()),
+        ],
         compiler_params=ROOM,
         cost_estimate=lasting(9),
         name="factor_grads",
@@ -569,7 +586,8 @@
     )(ga, gb)
 
 
-def home_kernel(gf_ref, w_ref, x_ref, member_ref, chain_ref, x_out_ref, ct_ref, x_s, ct_s, live_s):
+def home_kernel(gf_ref, w_ref, x_ref, member_ref, chain_ref, x_out_ref, ct_ref, token_ref, x_s, ct_s, live_s):
+    token_ref[...] = jnp.zeros_like(token_ref)
     width = FACTOR_WIDTH
     groups, rows, depth = x_ref.shape
     parts = 4
@@ -625,8 +643,8 @@
     return pl.pallas_call(
         home_kernel,
         in_specs=[VMEM] * 4 + [SMEM],
-        out_specs=[VMEM] * 2,
-        out_shape=[jax.ShapeDtypeStruct(shape, BF16)] * 2,
+        out_specs=[VMEM] * 3,
+        out_shape=[jax.ShapeDtypeStruct(shape, BF16)] * 2 + [TOKEN],
         scratch_shapes=[pltpu.VMEM((2, seqs * residues, depth // 2), F32)] * 2
         + [pltpu.VMEM((member.shape[1], 128), F32)],
         compiler_params=ROOM,
@@ -719,15 +737,15 @@
         pair_grad.reshape(res_here, r_size, q_size, 4, pair_width), q_at, 2, keepdims=False
     ).reshape(res_here, r_size * 4, pair_width)
 
-    bias = pair_bias(pair_rep, bias_proj.T, chain_row)
+    bias, bias_token = pair_bias(pair_rep, bias_proj.T, chain_row)
     x_rows = lax.all_to_all(
         multiple_alignment_rep.reshape(b_size, seqs_here // b_size, res_here, depth),
         ("y", "x_lo"), 0, 0, tiled=True,
     )
-    (x_rows,) = hold([x_rows], bias)
+    (x_rows,) = hold([x_rows], bias_token)
     x_other = lax.ppermute(x_rows, "core", SWAP)
-    q, k, v, g = row_entry(x_rows, x_other, chain_row, horizontal_entry_matrices)
-    bias_pieces = ring(bias, "y", "x_lo", after=q)
+    q, k, v, g, entry_token = row_entry(x_rows, x_other, chain_row, horizontal_entry_matrices)
+    bias_pieces = ring(bias, "y", "x_lo", after=entry_token)
     near, far = (0, 1, 3, 4), (2, 5, 6, 7)
     after_row = ()
     for part in (near, far):
@@ -738,14 +756,14 @@
         after_row = [after_row]
     (after_row,) = after_row
 
-    spread = spread_of(grad_here, w_outer, member, after_row)
+    spread, spread_token = spread_of(grad_here, w_outer, member, after_row)
     columns = lax.all_to_all(
         after_row.reshape(q_size * b_size, 16, depth),
         ("x_hi", "z", "y", "x_lo"), 0, 0, tiled=True,
     )
     going, factor_b = col_attention(
         columns, member, chain_position_valid,
-        vertical_entry_matrices, vertical_exit_matrix, dyadic_t, q_size, spread,
+        vertical_entry_matrices, vertical_exit_matrix, dyadic_t, q_size, spread_token,
     )
     b_ring = ring(factor_b, "y", "x_lo")
     b_pieces = [jnp.concatenate([b_ring[at] for at in part], 0) for part in (near, far)]
@@ -759,10 +777,10 @@
     gb = fold(gb, gb_other)
     gb = lax.all_to_all(gb, ("y", "x_lo"), 0, 0, tiled=True)
     factors = lax.all_to_all(pack_grads(ga, gb, q_size), ("x_hi", "z"), 0, 0, tiled=True)
-    alignment_refreshed, cotangent = finish_home(
+    alignment_refreshed, cotangent, home_token = finish_home(
         factors, dyadic_t, back, member, chain_position_valid
     )
-    couple_delta = assemble(deltas, cotangent)
+    couple_delta = assemble(deltas, home_token)
     return (alignment_refreshed, couple_delta, cotangent)
 
 

time: 174 us -> 172 us (0.989)
  local copies, waits for them, and re-layouts: 27.2 us -> 22.1 us
  Pallas kernels: 46.6 us -> 50.2 us
  waiting for transfers between devices: 31.7 us -> 34.2 us
  starting transfers between devices: 65.9 us -> 63.7 us
    unnamed x67 -> x61, local copies, waits for them, and re-layouts: 24 us -> 19.9 us
    all_to_all x1, waiting for transfers between devices: 1.36 us -> 3.52 us  [per_device(): lax.all_to_all(multiple_alignment_rep.reshape(b_size, seqs_here // b_size...]
    pallas_call x1, Pallas kernels: 4.46 us -> 6.56 us  [pair_bias(): pl.pallas_call(bias_kernel, grid=(rows // step,), in_specs=[pl.BlockSpec(...]
  transfers between devices with their start and end apart: 32 -> 32, of which waited for: 10 -> 10; matrix products, arithmetic and copies ran while one was open for 2% -> 1% of each run, Pallas kernels for 15% -> 16%
where the time goes in v5:
time: 172 us; the launch traced here: 171 us
  starting transfers between devices  63.7 us (37%)
  Pallas kernels  50.2 us (29%)
  waiting for transfers between devices  34.2 us (20%)
  local copies, waits for them, and re-layouts  22.1 us (13%)
    unnamed x61, local copies, waits for them, and re-layouts  19.9 us
    pallas_call x2, Pallas kernels, row_attention(): pl.pallas_call(functools.partial(row_kernel, steps), in_specs=[VMEM] * (6...  9.55 us
    ppermute x1, waiting for transfers between devices, ring_halves(): far_high = lax.ppermute(above[half:], along, turn_by(3))  8.61 us
    all_to_all x1, starting transfers between devices, per_device(): lax.all_to_all(after_row.reshape(q_size * b_size, 16, depth), ('x_hi', 'z...  8.5 us
    pallas_call x1, Pallas kernels, factor_grads(): pl.pallas_call(grads_kernel, in_specs=[VMEM, pl.BlockSpec(memory_space=pl...  6.66 us
    pallas_call x1, Pallas kernels, col_attention(): pl.pallas_call(col_kernel, in_specs=[VMEM] * 2 + [SMEM] + [VMEM] * 3 + [O...  6.63 us
    pallas_call x1, Pallas kernels, pair_bias(): pl.pallas_call(bias_kernel, grid=(rows // step,), in_specs=[pl.BlockSpec(...  6.56 us
    ppermute x2, starting transfers between devices, ring(): partner_above = lax.ppermute(partner, along, turn_by(3))  6.46 us
  transfers between devices with their start and end apart: 32, of which 10 were waited for; matrix products, arithmetic and copies ran while one was open for 1% of the time, Pallas kernels for 16%

profile of v5, /device:TPU:0, one launch (start us, length us, event | category | flops | bytes accessed | tf_op | source)
XLA Modules:
  0.0 171.2 jit_solution(5249934358173579317)
XLA Ops:
  0.7 5.6 %all-to-all-start = ((bf16[8,4,32,256]{3,2,1,0:T(8,128)(2,1)}), bf16[8,4,32,256]{3,2,1,0:T(8,128)(2,1)S(1)}, u32[]{:S(2)}, u32[]{:S(2)}) async-start(bf16[8,4,32,256]{3,2,1,0:T(8,128)(2,1)} %bitcast.29), calls=%async_computation | async-start | bytes 1048576 | tf_op jit(solution)/shard_map/all_to_all | solution.py:741
  6.3 6.6 %pair_bias.1 = (bf16[256,512]{1,0:T(8,128)(2,1)}, f32[8,128]{1,0:T(8,128)}) custom-call(bf16[32,512,128]{2,1,0:T(8,128)(2,1)} %pair_ref.1, bf16[8,128]{1,0:T(8,128)(2,1)} %bitcast.32, s32[1,512]{1,0:T(1,128)} %bitcast.22), custom_call_target="tpu_custom_call" | custom-call | bytes 33210000 | tf_op jit(solution)/shard_map/pair_bias/pallas_call | solution.py:113
  12.8 3.5 %all-to-all-done.refs_0_ = bf16[8,4,32,256]{3,2,1,0:T(8,128)(2,1)S(1)} async-done(((bf16[8,4,32,256]{3,2,1,0:T(8,128)(2,1)}), bf16[8,4,32,256]{3,2,1,0:T(8,128)(2,1)S(1)}, u32[]{:S(2)}, u32[]{:S(2)}) %all-to-all-start) | async-done | bytes 524320 | tf_op jit(solution)/shard_map/all_to_all | solution.py:741
  31.2 3.2 %collective-permute-start.3 = (bf16[256,512]{1,0:T(8,128)(2,1)}, bf16[256,512]{1,0:T(8,128)(2,1)S(1)}, u32[]{:S(2)}, u32[]{:S(2)}) collective-permute-start(bf16[256,512]{1,0:T(8,128)(2,1)} %get-tuple-element.32.refs_3_), channel_id=1, source_target_pairs={{0,12},{4,0},{8,4},{12,8},{1,13},{5,1},{9,5},{13,9},{2,14},{6,2},{... | collective-permute-start | bytes 786440 | tf_op jit(solution)/shard_map/ppermute | solution.py:688
  39.7 4.9 %row_attention.2.refs_4_ = bf16[8,8,16,256]{3,2,1,0:T(8,128)(2,1)S(1)} custom-call(bf16[4,256,256]{2,1,0:T(8,128)(2,1)S(1)} %get-tuple-element.25.q_ref, bf16[4,512,256]{2,1,0:T(8,128)(2,1)S(1)} %copy-done.7, bf16[4,2,512,256]{3,2,1,0:T(8,128)(2,1)S(1)} %get-tuple-element.27.v_ref, bf16[4,256,256]{2,1,0:T(8,128)(2,1)S(1)} %copy-done.9, ...), custom_call_target="tpu_custom_call" | custom-call | bytes 29520000 | tf_op jit(solution)/shard_map/row_attention/pallas_call | solution.py:261
  44.7 4.6 %row_attention.3._ = bf16[8,8,16,256]{3,2,1,0:T(8,128)(2,1)} custom-call(bf16[4,256,256]{2,1,0:T(8,128)(2,1)S(1)} %get-tuple-element.25.q_ref, bf16[4,512,256]{2,1,0:T(8,128)(2,1)S(1)} %copy-done.7, bf16[4,2,512,256]{3,2,1,0:T(8,128)(2,1)S(1)} %get-tuple-element.27.v_ref, bf16[4,256,256]{2,1,0:T(8,128)(2,1)S(1)} %copy-done.9, ...), custom_call_target="tpu_custom_call" | custom-call | bytes 29520000 | tf_op jit(solution)/shard_map/row_attention/pallas_call | solution.py:261
  49.3 8.5 %all-to-all-start.1 = ((bf16[64,16,256]{2,1,0:T(8,128)(2,1)}), bf16[64,16,256]{2,1,0:T(8,128)(2,1)S(1)}, u32[]{:S(2)}, u32[]{:S(2)}) async-start(bf16[64,16,256]{2,1,0:T(8,128)(2,1)} %bitcast.3), calls=%async_computation.1 | async-start | bytes 1048576 | tf_op jit(solution)/shard_map/all_to_all | solution.py:760
  59.4 4.5 %spread.1 = (bf16[1024,2048]{1,0:T(8,128)(2,1)S(1)}, f32[8,128]{1,0:T(8,128)S(1)}) custom-call(bf16[32,64,128]{2,1,0:T(8,128)(2,1)S(1)} %bitcast.19, bf16[512,256]{1,0:T(8,128)(2,1)S(1)} %bitcast.17, s32[1,256]{1,0:T(1,128)S(1)} %bitcast.24, bf16[8,8,16,256]{3,2,1,0:T(8,128)(2,1)} %row_attention.3._), custom_call_target="tpu_custom_call" | custom-call | bytes 29520000 | tf_op jit(solution)/shard_map/spread/pallas_call | solution.py:429
  65.9 4.1 %all-to-all-done.1.y_ref = bf16[64,16,256]{2,1,0:T(8,128)(2,1)S(1)} async-done(((bf16[64,16,256]{2,1,0:T(8,128)(2,1)}), bf16[64,16,256]{2,1,0:T(8,128)(2,1)S(1)}, u32[]{:S(2)}, u32[]{:S(2)}) %all-to-all-start.1) | async-done | bytes 524320 | tf_op jit(solution)/shard_map/all_to_all | solution.py:760
  72.7 6.6 %col_attention.1 = (bf16[8,256,256]{2,1,0:T(8,128)(2,1)}, bf16[128,256]{1,0:T(8,128)(2,1)S(1)}) custom-call(bf16[64,16,256]{2,1,0:T(8,128)(2,1)S(1)} %all-to-all-done.1.y_ref, s32[1,256]{1,0:T(1,128)S(1)} %bitcast.25, s32[512]{0:T(512)S(1)} %copy-done.23, bf16[256,1024]{1,0:T(8,128)(2,1)S(1)} %copy-done.18, bf16[256,256]{1,0:T(8,128)(2,1)S(1)} %copy-done.22, ...), custom_call_target="tpu_custom_call" | custom-call | bytes 29520000 | tf_op jit(solution)/shard_map/col_attention/pallas_call | solution.py:334
  84.8 4.9 %all-to-all-start.2 = ((bf16[8,256,256]{2,1,0:T(8,128)(2,1)}), bf16[8,256,256]{2,1,0:T(8,128)(2,1)S(1)}, u32[]{:S(2)}, u32[]{:S(2)}) async-start(bf16[8,256,256]{2,1,0:T(8,128)(2,1)} %get-tuple-element.34), calls=%async_computation.2 | async-start | bytes 2097152 | tf_op jit(solution)/shard_map/all_to_all | solution.py:771
  89.9 3.2 %collective-permute-start.12 = (bf16[128,256]{1,0:T(8,128)(2,1)S(1)}, bf16[128,256]{1,0:T(8,128)(2,1)S(1)}, u32[]{:S(2)}, u32[]{:S(2)}) collective-permute-start(bf16[128,256]{1,0:T(8,128)(2,1)S(1)} %collective-permute-done.10), channel_id=1, source_target_pairs={{0,12},{4,0},{8,4},{12,8},{1,13},{5,1},{9,5},{13,9},{2,14},{6,2},{... | collective-permute-start | bytes 196616 | tf_op jit(solution)/shard_map/ppermute | solution.py:688
  95.0 5.7 %collective-permute-done.13 = bf16[128,256]{1,0:T(8,128)(2,1)S(1)} collective-permute-done((bf16[128,256]{1,0:T(8,128)(2,1)S(1)}, bf16[128,256]{1,0:T(8,128)(2,1)S(1)}, u32[]{:S(2)}, u32[]{:S(2)}) %collective-permute-start.13) | collective-permute-done | bytes 65568 | tf_op jit(solution)/shard_map/ppermute | solution.py:689
  106.3 6.7 %factor_grads.1 = (bf16[1024,256]{1,0:T(8,128)(2,1)S(1)}, bf16[2048,256]{1,0:T(8,128)(2,1)S(1)}, bf16[256,1024]{1,0:T(8,128)(2,1)S(1)}, bf16[8,128,256]{2,1,0:T(8,128)(2,1)S(1)}, bf16[8,128,256]{2,1,0:T(8,128)(2,1)S(1)}) custom-call(bf16[8,256,256]{2,1,0:T(8,128)(2,1)S(1)} %all-to-all-done.2.both_ref.x_ref, bf16[1024,2048]{1,0:T(8,128)(2,1)S(1)} %copy-done.5, ...), custom_call_target="tpu_custom_call" | custom-call | bytes 33210000 | tf_op jit(solution)/shard_map/factor_grads/pallas_call | solution.py:528
  113.1 3.4 %couple.1.refs_0_ = bf16[32,64,128]{2,1,0:T(8,128)(2,1)S(1)} custom-call(bf16[1024,256]{1,0:T(8,128)(2,1)S(1)} %get-tuple-element.41.a_ref, bf16[2048,256]{1,0:T(8,128)(2,1)S(1)} %get-tuple-element.42.bd_ref, bf16[512,256]{1,0:T(8,128)(2,1)S(1)} %bitcast.18, s32[1,256]{1,0:T(1,128)S(1)} %bitcast.26), custom_call_target="tpu_custom_call" | custom-call | bytes 22140000 | tf_op jit(solution)/shard_map/couple/pallas_call | solution.py:473
  117.0 3.5 %collective-permute-start.22 = (bf16[32,64,128]{2,1,0:T(8,128)(2,1)S(1)}, bf16[32,64,128]{2,1,0:T(8,128)(2,1)}, u32[]{:S(2)}, u32[]{:S(2)}) collective-permute-start(bf16[32,64,128]{2,1,0:T(8,128)(2,1)S(1)} %couple.1.refs_0_), channel_id=1, source_target_pairs={{0,64},{64,0},{1,65},{65,1},{2,66},{66,2},{3,67},{67,3},{4,68},{68... | collective-permute-start | bytes 1572872 | tf_op jit(solution)/shard_map/ppermute | solution.py:695
  123.4 3.5 %all-to-all-start.3 = ((bf16[8,128,256]{2,1,0:T(8,128)(2,1)}), bf16[8,128,256]{2,1,0:T(8,128)(2,1)S(1)}, u32[]{:S(2)}, u32[]{:S(2)}) async-start(bf16[8,128,256]{2,1,0:T(8,128)(2,1)} %fold.1), calls=%async_computation.3 | async-start | bytes 1048576 | tf_op jit(solution)/shard_map/all_to_all | solution.py:778
  126.9 5.2 %collective-permute-done.19.refs_4_ = bf16[32,64,128]{2,1,0:T(8,128)(2,1)S(1)} collective-permute-done((bf16[32,64,128]{2,1,0:T(8,128)(2,1)S(1)}, bf16[32,64,128]{2,1,0:T(8,128)(2,1)S(1)}, u32[]{:S(2)}, u32[]{:S(2)}) %collective-permute-start.19) | collective-permute-done | bytes 524320 | tf_op jit(solution)/shard_map/ppermute | solution.py:696
  140.9 5.2 %all-to-all-start.4 = ((bf16[8,32,1152]{2,1,0:T(8,128)(2,1)}), bf16[8,32,1152]{2,1,0:T(8,128)(2,1)S(1)}, u32[]{:S(2)}, u32[]{:S(2)}) async-start(bf16[8,32,1152]{2,1,0:T(8,128)(2,1)} %pack_grads.1), calls=%async_computation.4 | async-start | bytes 1179648 | tf_op jit(solution)/shard_map/all_to_all | solution.py:779
  146.2 3.5 %collective-permute-start.24 = (bf16[16,64,128]{2,1,0:T(8,128)(2,1)}, bf16[16,64,128]{2,1,0:T(8,128)(2,1)}, u32[]{:S(2)}, u32[]{:S(2)}) collective-permute-start(bf16[16,64,128]{2,1,0:T(8,128)(2,1)} %collective-permute-done.20.refs_2_), channel_id=1, source_target_pairs={{0,64},{64,0},{1,65},{65,1},{2,66},{66,2},{3,67},{67,3},{4,68},{68... | collective-permute-start | bytes 786440 | tf_op jit(solution)/shard_map/ppermute | solution.py:702
  149.7 8.6 %collective-permute-done.21.refs_3_ = bf16[16,64,128]{2,1,0:T(8,128)(2,1)} collective-permute-done((bf16[16,64,128]{2,1,0:T(8,128)(2,1)}, bf16[16,64,128]{2,1,0:T(8,128)(2,1)}, u32[]{:S(2)}, u32[]{:S(2)}) %collective-permute-start.21) | collective-permute-done | bytes 262176 | tf_op jit(solution)/shard_map/ppermute | solution.py:699
  158.3 2.9 %collective-permute-start.25 = (bf16[16,64,128]{2,1,0:T(8,128)(2,1)}, bf16[16,64,128]{2,1,0:T(8,128)(2,1)}, u32[]{:S(2)}, u32[]{:S(2)}) collective-permute-start(bf16[16,64,128]{2,1,0:T(8,128)(2,1)} %collective-permute-done.21.refs_3_), channel_id=1, source_target_pairs={{0,64},{64,0},{1,65},{65,1},{2,66},{66,2},{3,67},{67,3},{4,68},{68... | collective-permute-start | bytes 786440 | tf_op jit(solution)/shard_map/ppermute | solution.py:703
  161.2 4.2 %finish_home.1 = (bf16[32,32,256]{2,1,0:T(8,128)(2,1)}, bf16[32,32,256]{2,1,0:T(8,128)(2,1)}, f32[8,128]{1,0:T(8,128)S(1)}) custom-call(bf16[8,32,1152]{2,1,0:T(8,128)(2,1)S(1)} %all-to-all-done.4.gf_ref, bf16[64,256]{1,0:T(8,128)(2,1)S(1)} %bitcast.21, bf16[8,256,256]{2,1,0:T(8,128)(2,1)S(1)} %all-to-all-done.2.both_ref.x_ref, s32[1,256]{1,0:T(1,128)S(1)} %bitcast.27, ...), custom_call_target="tpu_custom_call" | custom-call | bytes 22140000 | tf_op jit(solution)/shard_map/finish_home/pallas_call | solution.py:643
  166.5 4.7 %assemble.1 = bf16[32,512,128]{2,1,0:T(8,128)(2,1)} custom-call(bf16[32,64,128]{2,1,0:T(8,128)(2,1)S(1)} %couple.1.refs_0_, bf16[32,64,128]{2,1,0:T(8,128)(2,1)S(1)} %collective-permute-done.18.refs_1_, bf16[16,64,128]{2,1,0:T(8,128)(2,1)} %collective-permute-done.20.refs_2_, bf16[16,64,128]{2,1,0:T(8,128)(2,1)} %collective-permute-done.21.refs_3_, ...), custom_call_target="tpu_custom_call" | custom-call | bytes 18450000 | tf_op jit(solution)/shard_map/assemble/pallas_call | solution.py:387
  (121 shorter events, 52.7 us)
Async XLA Ops:
  0.7 15.7 %all-to-all-start = ((bf16[8,4,32,256]{3,2,1,0:T(8,128)(2,1)}), bf16[8,4,32,256]{3,2,1,0:T(8,128)(2,1)S(1)}, u32[]{:S(2)}, u32[]{:S(2)}) async-start(bf16[8,4,32,256]{3,2,1,0:T(8,128)(2,1)} %bitcast.29), calls=%async_computation | async-start | bytes 1048576 | tf_op jit(solution)/shard_map/all_to_all | solution.py:741
  17.2 11.3 %collective-permute-start.2 = (bf16[256,512]{1,0:T(8,128)(2,1)}, bf16[256,512]{1,0:T(8,128)(2,1)S(1)}, u32[]{:S(2)}, u32[]{:S(2)}) collective-permute-start(bf16[256,512]{1,0:T(8,128)(2,1)} %get-tuple-element.29.refs_0_), channel_id=1, source_target_pairs={{0,8},{4,12},{8,0},{12,4},{1,9},{5,13},{9,1},{13,5},{2,10},{6,14},... | collective-permute-start | bytes 786440 | tf_op jit(solution)/shard_map/ppermute | solution.py:684
  18.0 10.4 %collective-permute-start.1 = (bf16[256,512]{1,0:T(8,128)(2,1)}, bf16[256,512]{1,0:T(8,128)(2,1)S(1)}, u32[]{:S(2)}, u32[]{:S(2)}) collective-permute-start(bf16[256,512]{1,0:T(8,128)(2,1)} %get-tuple-element.29.refs_0_), channel_id=1, source_target_pairs={{0,2},{2,0},{1,3},{3,1},{4,6},{6,4},{5,7},{7,5},{8,10},{10,8},{9,1... | collective-permute-start | bytes 786440 | tf_op jit(solution)/shard_map/ppermute | solution.py:681
  18.6 15.8 %collective-permute-start.7 = (bf16[256,512]{1,0:T(8,128)(2,1)}, bf16[256,512]{1,0:T(8,128)(2,1)}, u32[]{:S(2)}, u32[]{:S(2)}) collective-permute-start(bf16[256,512]{1,0:T(8,128)(2,1)} %get-tuple-element.29.refs_0_), channel_id=1, source_target_pairs={{0,4},{4,8},{8,12},{12,0},{1,5},{5,9},{9,13},{13,1},{2,6},{6,10},{... | collective-permute-start | bytes 786440 | tf_op jit(solution)/shard_map/ppermute | solution.py:682
  20.0 14.4 %collective-permute-start.6 = (bf16[256,512]{1,0:T(8,128)(2,1)}, bf16[256,512]{1,0:T(8,128)(2,1)}, u32[]{:S(2)}, u32[]{:S(2)}) collective-permute-start(bf16[256,512]{1,0:T(8,128)(2,1)} %get-tuple-element.29.refs_0_), channel_id=1, source_target_pairs={{0,12},{4,0},{8,4},{12,8},{1,13},{5,1},{9,5},{13,9},{2,14},{6,2},{... | collective-permute-start | bytes 786440 | tf_op jit(solution)/shard_map/ppermute | solution.py:683
  29.8 14.8 %collective-permute-start.4 = (bf16[256,512]{1,0:T(8,128)(2,1)}, bf16[256,512]{1,0:T(8,128)(2,1)S(1)}, u32[]{:S(2)}, u32[]{:S(2)}) collective-permute-start(bf16[256,512]{1,0:T(8,128)(2,1)} %get-tuple-element.31.refs_0_), channel_id=1, source_target_pairs={{0,2},{2,0},{1,3},{3,1},{4,6},{6,4},{5,7},{7,5},{8,10},{10,8},{9,1... | collective-permute-start | bytes 786440 | tf_op jit(solution)/shard_map/ppermute | solution.py:689
  31.2 13.4 %collective-permute-start.5 = (bf16[256,512]{1,0:T(8,128)(2,1)}, bf16[256,512]{1,0:T(8,128)(2,1)S(1)}, u32[]{:S(2)}, u32[]{:S(2)}) collective-permute-start(bf16[256,512]{1,0:T(8,128)(2,1)} %get-tuple-element.32.refs_3_), channel_id=1, source_target_pairs={{0,4},{4,8},{8,12},{12,0},{1,5},{5,9},{9,13},{13,1},{2,6},{6,10},{... | collective-permute-start | bytes 786440 | tf_op jit(solution)/shard_map/ppermute | solution.py:687
  31.2 13.4 %collective-permute-start.3 = (bf16[256,512]{1,0:T(8,128)(2,1)}, bf16[256,512]{1,0:T(8,128)(2,1)S(1)}, u32[]{:S(2)}, u32[]{:S(2)}) collective-permute-start(bf16[256,512]{1,0:T(8,128)(2,1)} %get-tuple-element.32.refs_3_), channel_id=1, source_target_pairs={{0,12},{4,0},{8,4},{12,8},{1,13},{5,1},{9,5},{13,9},{2,14},{6,2},{... | collective-permute-start | bytes 786440 | tf_op jit(solution)/shard_map/ppermute | solution.py:688
  49.3 20.7 %all-to-all-start.1 = ((bf16[64,16,256]{2,1,0:T(8,128)(2,1)}), bf16[64,16,256]{2,1,0:T(8,128)(2,1)S(1)}, u32[]{:S(2)}, u32[]{:S(2)}) async-start(bf16[64,16,256]{2,1,0:T(8,128)(2,1)} %bitcast.3), calls=%async_computation.1 | async-start | bytes 1048576 | tf_op jit(solution)/shard_map/all_to_all | solution.py:760
  79.3 13.8 %collective-permute-start.11 = (bf16[128,256]{1,0:T(8,128)(2,1)S(1)}, bf16[128,256]{1,0:T(8,128)(2,1)S(1)}, u32[]{:S(2)}, u32[]{:S(2)}) collective-permute-start(bf16[128,256]{1,0:T(8,128)(2,1)S(1)} %get-tuple-element.36), channel_id=1, source_target_pairs={{0,8},{4,12},{8,0},{12,4},{1,9},{5,13},{9,1},{13,5},{2,10},{6,14},... | collective-permute-start | bytes 196616 | tf_op jit(solution)/shard_map/ppermute | solution.py:684
  84.8 19.3 %all-to-all-start.2 = ((bf16[8,256,256]{2,1,0:T(8,128)(2,1)}), bf16[8,256,256]{2,1,0:T(8,128)(2,1)S(1)}, u32[]{:S(2)}, u32[]{:S(2)}) async-start(bf16[8,256,256]{2,1,0:T(8,128)(2,1)} %get-tuple-element.34), calls=%async_computation.2 | async-start | bytes 2097152 | tf_op jit(solution)/shard_map/all_to_all | solution.py:771
  89.7 11.2 %collective-permute-start.15 = (bf16[512,256]{1,0:T(8,128)(2,1)S(1)}, bf16[512,256]{1,0:T(8,128)(2,1)S(1)}, u32[]{:S(2)}, u32[]{:S(2)}) collective-permute-start(bf16[512,256]{1,0:T(8,128)(2,1)S(1)} %constant_dynamic-update-slice_fusion.refs_0_), channel_id=1, source_target_pairs={{0,1},{1,0},{2,3},{3,2},{4,5},{5,4},{6,7},{7,6},{8,9},{9,8},{10,11... | collective-permute-start | bytes 786440 | tf_op jit(solution)/shard_map/ppermute | solution.py:770
  89.8 11.0 %collective-permute-start.14 = (bf16[128,256]{1,0:T(8,128)(2,1)S(1)}, bf16[128,256]{1,0:T(8,128)(2,1)S(1)}, u32[]{:S(2)}, u32[]{:S(2)}) collective-permute-start(bf16[128,256]{1,0:T(8,128)(2,1)S(1)} %collective-permute-done.10), channel_id=1, source_target_pairs={{0,4},{4,8},{8,12},{12,0},{1,5},{5,9},{9,13},{13,1},{2,6},{6,10},{... | collective-permute-start | bytes 196616 | tf_op jit(solution)/shard_map/ppermute | solution.py:687
  112.9 9.6 %collective-permute-start.17 = (bf16[8,128,256]{2,1,0:T(8,128)(2,1)S(1)}, bf16[8,128,256]{2,1,0:T(8,128)(2,1)S(1)}, u32[]{:S(2)}, u32[]{:S(2)}) collective-permute-start(bf16[8,128,256]{2,1,0:T(8,128)(2,1)S(1)} %get-tuple-element.39), channel_id=1, source_target_pairs={{0,1},{1,0},{2,3},{3,2},{4,5},{5,4},{6,7},{7,6},{8,9},{9,8},{10,11... | collective-permute-start | bytes 1572872 | tf_op jit(solution)/shard_map/ppermute | solution.py:774
  116.5 15.6 %collective-permute-start.19 = (bf16[32,64,128]{2,1,0:T(8,128)(2,1)S(1)}, bf16[32,64,128]{2,1,0:T(8,128)(2,1)S(1)}, u32[]{:S(2)}, u32[]{:S(2)}) collective-permute-start(bf16[32,64,128]{2,1,0:T(8,128)(2,1)S(1)} %couple.1.refs_0_), channel_id=1, source_target_pairs={{0,16},{16,32},{32,48},{48,0},{1,17},{17,33},{33,49},{49,1},{2,18}... | collective-permute-start | bytes 1572872 | tf_op jit(solution)/shard_map/ppermute | solution.py:696
  117.0 16.4 %collective-permute-start.22 = (bf16[32,64,128]{2,1,0:T(8,128)(2,1)S(1)}, bf16[32,64,128]{2,1,0:T(8,128)(2,1)}, u32[]{:S(2)}, u32[]{:S(2)}) collective-permute-start(bf16[32,64,128]{2,1,0:T(8,128)(2,1)S(1)} %couple.1.refs_0_), channel_id=1, source_target_pairs={{0,64},{64,0},{1,65},{65,1},{2,66},{66,2},{3,67},{67,3},{4,68},{68... | collective-permute-start | bytes 1572872 | tf_op jit(solution)/shard_map/ppermute | solution.py:695
  120.5 16.1 %collective-permute-start.18 = (bf16[32,64,128]{2,1,0:T(8,128)(2,1)S(1)}, bf16[32,64,128]{2,1,0:T(8,128)(2,1)S(1)}, u32[]{:S(2)}, u32[]{:S(2)}) collective-permute-start(bf16[32,64,128]{2,1,0:T(8,128)(2,1)S(1)} %couple.1.refs_0_), channel_id=1, source_target_pairs={{0,48},{16,0},{32,16},{48,32},{1,49},{17,1},{33,17},{49,33},{2,50}... | collective-permute-start | bytes 1572872 | tf_op jit(solution)/shard_map/ppermute | solution.py:697
  123.4 15.5 %all-to-all-start.3 = ((bf16[8,128,256]{2,1,0:T(8,128)(2,1)}), bf16[8,128,256]{2,1,0:T(8,128)(2,1)S(1)}, u32[]{:S(2)}, u32[]{:S(2)}) async-start(bf16[8,128,256]{2,1,0:T(8,128)(2,1)} %fold.1), calls=%async_computation.3 | async-start | bytes 1048576 | tf_op jit(solution)/shard_map/all_to_all | solution.py:778
  132.1 14.0 %collective-permute-start.20 = (bf16[16,64,128]{2,1,0:T(8,128)(2,1)S(1)}, bf16[16,64,128]{2,1,0:T(8,128)(2,1)}, u32[]{:S(2)}, u32[]{:S(2)}) collective-permute-start(bf16[16,64,128]{2,1,0:T(8,128)(2,1)S(1)} %slice.8), channel_id=1, source_target_pairs={{0,16},{16,32},{32,48},{48,0},{1,17},{17,33},{33,49},{49,1},{2,18}... | collective-permute-start | bytes 786440 | tf_op jit(solution)/shard_map/ppermute | solution.py:698
  133.4 32.0 %collective-permute-start.26 = (bf16[32,64,128]{2,1,0:T(8,128)(2,1)}, bf16[32,64,128]{2,1,0:T(8,128)(2,1)}, u32[]{:S(2)}, u32[]{:S(2)}) collective-permute-start(bf16[32,64,128]{2,1,0:T(8,128)(2,1)} %collective-permute-done.22.refs_5_), channel_id=1, source_target_pairs={{0,16},{16,32},{32,48},{48,0},{1,17},{17,33},{33,49},{49,1},{2,18}... | collective-permute-start | bytes 1572872 | tf_op jit(solution)/shard_map/ppermute | solution.py:700
  135.1 30.3 %collective-permute-start.23 = (bf16[32,64,128]{2,1,0:T(8,128)(2,1)}, bf16[32,64,128]{2,1,0:T(8,128)(2,1)}, u32[]{:S(2)}, u32[]{:S(2)}) collective-permute-start(bf16[32,64,128]{2,1,0:T(8,128)(2,1)} %collective-permute-done.22.refs_5_), channel_id=1, source_target_pairs={{0,48},{16,0},{32,16},{48,32},{1,49},{17,1},{33,17},{49,33},{2,50}... | collective-permute-start | bytes 1572872 | tf_op jit(solution)/shard_map/ppermute | solution.py:701
  137.3 21.0 %collective-permute-start.21 = (bf16[16,64,128]{2,1,0:T(8,128)(2,1)}, bf16[16,64,128]{2,1,0:T(8,128)(2,1)}, u32[]{:S(2)}, u32[]{:S(2)}) collective-permute-start(bf16[16,64,128]{2,1,0:T(8,128)(2,1)} %slice.9), channel_id=1, source_target_pairs={{0,48},{16,0},{32,16},{48,32},{1,49},{17,1},{33,17},{49,33},{2,50}... | collective-permute-start | bytes 786440 | tf_op jit(solution)/shard_map/ppermute | solution.py:699
  140.9 20.3 %all-to-all-start.4 = ((bf16[8,32,1152]{2,1,0:T(8,128)(2,1)}), bf16[8,32,1152]{2,1,0:T(8,128)(2,1)S(1)}, u32[]{:S(2)}, u32[]{:S(2)}) async-start(bf16[8,32,1152]{2,1,0:T(8,128)(2,1)} %pack_grads.1), calls=%async_computation.4 | async-start | bytes 1179648 | tf_op jit(solution)/shard_map/all_to_all | solution.py:779
  146.2 19.2 %collective-permute-start.24 = (bf16[16,64,128]{2,1,0:T(8,128)(2,1)}, bf16[16,64,128]{2,1,0:T(8,128)(2,1)}, u32[]{:S(2)}, u32[]{:S(2)}) collective-permute-start(bf16[16,64,128]{2,1,0:T(8,128)(2,1)} %collective-permute-done.20.refs_2_), channel_id=1, source_target_pairs={{0,64},{64,0},{1,65},{65,1},{2,66},{66,2},{3,67},{67,3},{4,68},{68... | collective-permute-start | bytes 786440 | tf_op jit(solution)/shard_map/ppermute | solution.py:702
  (35 other events, 232.8 us)

commit v6 on v5

--- a/solution.py
+++ b/solution.py
@@ -484,10 +484,8 @@
     )(a_all, bd, w, member)
 
 
-def grads_kernel(both_ref, spread_ref, *refs):
-    b_pieces, (a_ref, bd_ref, ga_ref, own_ref, other_ref, turned_s, s_ref, done) = refs[:4], refs[4:]
-    fetch = pltpu.make_async_copy(spread_ref, s_ref, done)
-    fetch.start()
+def grads_kernel(both_ref, s_ref, *refs):
+    b_pieces, (a_ref, bd_ref, ga_ref, own_ref, other_ref, turned_s) = refs[:4], refs[4:]
     width = FACTOR_WIDTH
     blocks = own_ref.shape[0]
     columns = turned_s.shape[1] // width
@@ -506,7 +504,6 @@
         bd_ref[here, :] = take(turned_s, pl.ds(at, columns, stride=width)).astype(BF16)
     a_ref[...] = both_ref[:, 128:].reshape(a_ref.shape)
     left = a_ref[...].astype(F32).T.astype(BF16)
-    fetch.wait()
     for at in range(columns * width // 256):
         here = slice(256 * at, 256 * at + 256)
         put(turned_s, here, nn(left, s_ref[:, here]).T)
@@ -527,7 +524,7 @@
     shape = jax.ShapeDtypeStruct((columns // 256, 128, seqs), BF16)
     return pl.pallas_call(
         grads_kernel,
-        in_specs=[VMEM, pl.BlockSpec(memory_space=pl.ANY)] + [VMEM] * 4,
+        in_specs=[VMEM] * 6,
         out_specs=[VMEM] * 5,
         out_shape=[
             jax.ShapeDtypeStruct((rows, seqs), BF16),
@@ -536,11 +533,7 @@
             shape,
             shape,
         ],
-        scratch_shapes=[
-            pltpu.VMEM((2, columns, seqs // 2), F32),
-            pltpu.VMEM((rows, columns), BF16),
-            pltpu.SemaphoreType.DMA(()),
-        ],
+        scratch_shapes=[pltpu.VMEM((2, columns, seqs // 2), F32)],
         compiler_params=ROOM,
         cost_estimate=lasting(9),
         name="factor_grads",

time: 172 us -> 171 us (level)
  no operation moved by 1% of the time
where the time goes in v6:
time: 171 us; the launch traced here: 170 us
  starting transfers between devices  64 us (37%)
  Pallas kernels  49.1 us (29%)
  waiting for transfers between devices  33.9 us (20%)
  local copies, waits for them, and re-layouts  22.1 us (13%)
    unnamed x61, local copies, waits for them, and re-layouts  19.9 us
    pallas_call x2, Pallas kernels, row_attention(): pl.pallas_call(functools.partial(row_kernel, steps), in_specs=[VMEM] * (6...  9.55 us
    ppermute x1, waiting for transfers between devices, ring_halves(): far_high = lax.ppermute(above[half:], along, turn_by(3))  8.6 us
    all_to_all x1, starting transfers between devices, per_device(): lax.all_to_all(after_row.reshape(q_size * b_size, 16, depth), ('x_hi', 'z...  8.5 us
    pallas_call x1, Pallas kernels, col_attention(): pl.pallas_call(col_kernel, in_specs=[VMEM] * 2 + [SMEM] + [VMEM] * 3 + [O...  6.63 us
    pallas_call x1, Pallas kernels, pair_bias(): pl.pallas_call(bias_kernel, grid=(rows // step,), in_specs=[pl.BlockSpec(...  6.56 us
    ppermute x2, starting transfers between devices, ring(): partner_above = lax.ppermute(partner, along, turn_by(3))  6.46 us
    ppermute x2, waiting for transfers between devices, ring(): partner_far = lax.ppermute(far, across, SWAP)  5.73 us
  transfers between devices with their start and end apart: 32, of which 10 were waited for; matrix products, arithmetic and copies ran while one was open for 1% of the time, Pallas kernels for 16%

profile of v6, /device:TPU:0, one launch (start us, length us, event | category | flops | bytes accessed | tf_op | source)
XLA Modules:
  0.0 170.1 jit_solution(13815537080559237471)
XLA Ops:
  0.7 5.6 %all-to-all-start = ((bf16[8,4,32,256]{3,2,1,0:T(8,128)(2,1)}), bf16[8,4,32,256]{3,2,1,0:T(8,128)(2,1)S(1)}, u32[]{:S(2)}, u32[]{:S(2)}) async-start(bf16[8,4,32,256]{3,2,1,0:T(8,128)(2,1)} %bitcast.29), calls=%async_computation | async-start | bytes 1048576 | tf_op jit(solution)/shard_map/all_to_all | solution.py:734
  6.3 6.6 %pair_bias.1 = (bf16[256,512]{1,0:T(8,128)(2,1)}, f32[8,128]{1,0:T(8,128)}) custom-call(bf16[32,512,128]{2,1,0:T(8,128)(2,1)} %pair_ref.1, bf16[8,128]{1,0:T(8,128)(2,1)} %bitcast.32, s32[1,512]{1,0:T(1,128)} %bitcast.22), custom_call_target="tpu_custom_call" | custom-call | bytes 33210000 | tf_op jit(solution)/shard_map/pair_bias/pallas_call | solution.py:113
  12.8 3.5 %all-to-all-done.refs_0_ = bf16[8,4,32,256]{3,2,1,0:T(8,128)(2,1)S(1)} async-done(((bf16[8,4,32,256]{3,2,1,0:T(8,128)(2,1)}), bf16[8,4,32,256]{3,2,1,0:T(8,128)(2,1)S(1)}, u32[]{:S(2)}, u32[]{:S(2)}) %all-to-all-start) | async-done | bytes 524320 | tf_op jit(solution)/shard_map/all_to_all | solution.py:734
  31.2 3.2 %collective-permute-start.3 = (bf16[256,512]{1,0:T(8,128)(2,1)}, bf16[256,512]{1,0:T(8,128)(2,1)S(1)}, u32[]{:S(2)}, u32[]{:S(2)}) collective-permute-start(bf16[256,512]{1,0:T(8,128)(2,1)} %get-tuple-element.32.refs_3_), channel_id=1, source_target_pairs={{0,12},{4,0},{8,4},{12,8},{1,13},{5,1},{9,5},{13,9},{2,14},{6,2},{... | collective-permute-start | bytes 786440 | tf_op jit(solution)/shard_map/ppermute | solution.py:681
  39.7 4.9 %row_attention.2.refs_4_ = bf16[8,8,16,256]{3,2,1,0:T(8,128)(2,1)S(1)} custom-call(bf16[4,256,256]{2,1,0:T(8,128)(2,1)S(1)} %get-tuple-element.25.q_ref, bf16[4,512,256]{2,1,0:T(8,128)(2,1)S(1)} %copy-done.7, bf16[4,2,512,256]{3,2,1,0:T(8,128)(2,1)S(1)} %get-tuple-element.27.v_ref, bf16[4,256,256]{2,1,0:T(8,128)(2,1)S(1)} %copy-done.9, ...), custom_call_target="tpu_custom_call" | custom-call | bytes 29520000 | tf_op jit(solution)/shard_map/row_attention/pallas_call | solution.py:261
  44.7 4.6 %row_attention.3._ = bf16[8,8,16,256]{3,2,1,0:T(8,128)(2,1)} custom-call(bf16[4,256,256]{2,1,0:T(8,128)(2,1)S(1)} %get-tuple-element.25.q_ref, bf16[4,512,256]{2,1,0:T(8,128)(2,1)S(1)} %copy-done.7, bf16[4,2,512,256]{3,2,1,0:T(8,128)(2,1)S(1)} %get-tuple-element.27.v_ref, bf16[4,256,256]{2,1,0:T(8,128)(2,1)S(1)} %copy-done.9, ...), custom_call_target="tpu_custom_call" | custom-call | bytes 29520000 | tf_op jit(solution)/shard_map/row_attention/pallas_call | solution.py:261
  49.3 8.5 %all-to-all-start.1 = ((bf16[64,16,256]{2,1,0:T(8,128)(2,1)}), bf16[64,16,256]{2,1,0:T(8,128)(2,1)S(1)}, u32[]{:S(2)}, u32[]{:S(2)}) async-start(bf16[64,16,256]{2,1,0:T(8,128)(2,1)} %bitcast.3), calls=%async_computation.1 | async-start | bytes 1048576 | tf_op jit(solution)/shard_map/all_to_all | solution.py:753
  59.4 4.5 %spread.1 = (bf16[1024,2048]{1,0:T(8,128)(2,1)S(1)}, f32[8,128]{1,0:T(8,128)S(1)}) custom-call(bf16[32,64,128]{2,1,0:T(8,128)(2,1)S(1)} %bitcast.19, bf16[512,256]{1,0:T(8,128)(2,1)S(1)} %bitcast.17, s32[1,256]{1,0:T(1,128)S(1)} %bitcast.24, bf16[8,8,16,256]{3,2,1,0:T(8,128)(2,1)} %row_attention.3._), custom_call_target="tpu_custom_call" | custom-call | bytes 29520000 | tf_op jit(solution)/shard_map/spread/pallas_call | solution.py:429
  65.9 4.1 %all-to-all-done.1.y_ref = bf16[64,16,256]{2,1,0:T(8,128)(2,1)S(1)} async-done(((bf16[64,16,256]{2,1,0:T(8,128)(2,1)}), bf16[64,16,256]{2,1,0:T(8,128)(2,1)S(1)}, u32[]{:S(2)}, u32[]{:S(2)}) %all-to-all-start.1) | async-done | bytes 524320 | tf_op jit(solution)/shard_map/all_to_all | solution.py:753
  72.7 6.6 %col_attention.1 = (bf16[8,256,256]{2,1,0:T(8,128)(2,1)}, bf16[128,256]{1,0:T(8,128)(2,1)S(1)}) custom-call(bf16[64,16,256]{2,1,0:T(8,128)(2,1)S(1)} %all-to-all-done.1.y_ref, s32[1,256]{1,0:T(1,128)S(1)} %bitcast.25, s32[512]{0:T(512)S(1)} %copy-done.23, bf16[256,1024]{1,0:T(8,128)(2,1)S(1)} %copy-done.18, bf16[256,256]{1,0:T(8,128)(2,1)S(1)} %copy-done.22, ...), custom_call_target="tpu_custom_call" | custom-call | bytes 29520000 | tf_op jit(solution)/shard_map/col_attention/pallas_call | solution.py:334
  84.8 4.9 %all-to-all-start.2 = ((bf16[8,256,256]{2,1,0:T(8,128)(2,1)}), bf16[8,256,256]{2,1,0:T(8,128)(2,1)S(1)}, u32[]{:S(2)}, u32[]{:S(2)}) async-start(bf16[8,256,256]{2,1,0:T(8,128)(2,1)} %get-tuple-element.34), calls=%async_computation.2 | async-start | bytes 2097152 | tf_op jit(solution)/shard_map/all_to_all | solution.py:764
  89.9 3.2 %collective-permute-start.12 = (bf16[128,256]{1,0:T(8,128)(2,1)S(1)}, bf16[128,256]{1,0:T(8,128)(2,1)S(1)}, u32[]{:S(2)}, u32[]{:S(2)}) collective-permute-start(bf16[128,256]{1,0:T(8,128)(2,1)S(1)} %collective-permute-done.10), channel_id=1, source_target_pairs={{0,12},{4,0},{8,4},{12,8},{1,13},{5,1},{9,5},{13,9},{2,14},{6,2},{... | collective-permute-start | bytes 196616 | tf_op jit(solution)/shard_map/ppermute | solution.py:681
  95.0 5.7 %collective-permute-done.13 = bf16[128,256]{1,0:T(8,128)(2,1)S(1)} collective-permute-done((bf16[128,256]{1,0:T(8,128)(2,1)S(1)}, bf16[128,256]{1,0:T(8,128)(2,1)S(1)}, u32[]{:S(2)}, u32[]{:S(2)}) %collective-permute-start.13) | collective-permute-done | bytes 65568 | tf_op jit(solution)/shard_map/ppermute | solution.py:682
  106.3 5.6 %factor_grads.1 = (bf16[1024,256]{1,0:T(8,128)(2,1)S(1)}, bf16[2048,256]{1,0:T(8,128)(2,1)S(1)}, bf16[256,1024]{1,0:T(8,128)(2,1)S(1)}, bf16[8,128,256]{2,1,0:T(8,128)(2,1)S(1)}, bf16[8,128,256]{2,1,0:T(8,128)(2,1)S(1)}) custom-call(bf16[8,256,256]{2,1,0:T(8,128)(2,1)S(1)} %all-to-all-done.2.both_ref.x_ref, bf16[1024,2048]{1,0:T(8,128)(2,1)S(1)} %copy-done.5, ...), custom_call_target="tpu_custom_call" | custom-call | bytes 33210000 | tf_op jit(solution)/shard_map/factor_grads/pallas_call | solution.py:525
  112.0 3.4 %couple.1.refs_0_ = bf16[32,64,128]{2,1,0:T(8,128)(2,1)S(1)} custom-call(bf16[1024,256]{1,0:T(8,128)(2,1)S(1)} %get-tuple-element.41.a_ref, bf16[2048,256]{1,0:T(8,128)(2,1)S(1)} %get-tuple-element.42.bd_ref, bf16[512,256]{1,0:T(8,128)(2,1)S(1)} %bitcast.18, s32[1,256]{1,0:T(1,128)S(1)} %bitcast.26), custom_call_target="tpu_custom_call" | custom-call | bytes 22140000 | tf_op jit(solution)/shard_map/couple/pallas_call | solution.py:473
  115.9 3.5 %collective-permute-start.22 = (bf16[32,64,128]{2,1,0:T(8,128)(2,1)S(1)}, bf16[32,64,128]{2,1,0:T(8,128)(2,1)}, u32[]{:S(2)}, u32[]{:S(2)}) collective-permute-start(bf16[32,64,128]{2,1,0:T(8,128)(2,1)S(1)} %couple.1.refs_0_), channel_id=1, source_target_pairs={{0,64},{64,0},{1,65},{65,1},{2,66},{66,2},{3,67},{67,3},{4,68},{68... | collective-permute-start | bytes 1572872 | tf_op jit(solution)/shard_map/ppermute | solution.py:688
  122.4 3.5 %all-to-all-start.3 = ((bf16[8,128,256]{2,1,0:T(8,128)(2,1)}), bf16[8,128,256]{2,1,0:T(8,128)(2,1)S(1)}, u32[]{:S(2)}, u32[]{:S(2)}) async-start(bf16[8,128,256]{2,1,0:T(8,128)(2,1)} %fold.1), calls=%async_computation.3 | async-start | bytes 1048576 | tf_op jit(solution)/shard_map/all_to_all | solution.py:771
  125.9 5.1 %collective-permute-done.19.refs_4_ = bf16[32,64,128]{2,1,0:T(8,128)(2,1)S(1)} collective-permute-done((bf16[32,64,128]{2,1,0:T(8,128)(2,1)S(1)}, bf16[32,64,128]{2,1,0:T(8,128)(2,1)S(1)}, u32[]{:S(2)}, u32[]{:S(2)}) %collective-permute-start.19) | collective-permute-done | bytes 524320 | tf_op jit(solution)/shard_map/ppermute | solution.py:689
  139.8 5.3 %all-to-all-start.4 = ((bf16[8,32,1152]{2,1,0:T(8,128)(2,1)}), bf16[8,32,1152]{2,1,0:T(8,128)(2,1)S(1)}, u32[]{:S(2)}, u32[]{:S(2)}) async-start(bf16[8,32,1152]{2,1,0:T(8,128)(2,1)} %pack_grads.1), calls=%async_computation.4 | async-start | bytes 1179648 | tf_op jit(solution)/shard_map/all_to_all | solution.py:772
  145.1 3.5 %collective-permute-start.24 = (bf16[16,64,128]{2,1,0:T(8,128)(2,1)}, bf16[16,64,128]{2,1,0:T(8,128)(2,1)}, u32[]{:S(2)}, u32[]{:S(2)}) collective-permute-start(bf16[16,64,128]{2,1,0:T(8,128)(2,1)} %collective-permute-done.20.refs_2_), channel_id=1, source_target_pairs={{0,64},{64,0},{1,65},{65,1},{2,66},{66,2},{3,67},{67,3},{4,68},{68... | collective-permute-start | bytes 786440 | tf_op jit(solution)/shard_map/ppermute | solution.py:695
  148.6 8.6 %collective-permute-done.21.refs_3_ = bf16[16,64,128]{2,1,0:T(8,128)(2,1)} collective-permute-done((bf16[16,64,128]{2,1,0:T(8,128)(2,1)}, bf16[16,64,128]{2,1,0:T(8,128)(2,1)}, u32[]{:S(2)}, u32[]{:S(2)}) %collective-permute-start.21) | collective-permute-done | bytes 262176 | tf_op jit(solution)/shard_map/ppermute | solution.py:692
  157.2 2.9 %collective-permute-start.25 = (bf16[16,64,128]{2,1,0:T(8,128)(2,1)}, bf16[16,64,128]{2,1,0:T(8,128)(2,1)}, u32[]{:S(2)}, u32[]{:S(2)}) collective-permute-start(bf16[16,64,128]{2,1,0:T(8,128)(2,1)} %collective-permute-done.21.refs_3_), channel_id=1, source_target_pairs={{0,64},{64,0},{1,65},{65,1},{2,66},{66,2},{3,67},{67,3},{4,68},{68... | collective-permute-start | bytes 786440 | tf_op jit(solution)/shard_map/ppermute | solution.py:696
  160.1 4.2 %finish_home.1 = (bf16[32,32,256]{2,1,0:T(8,128)(2,1)}, bf16[32,32,256]{2,1,0:T(8,128)(2,1)}, f32[8,128]{1,0:T(8,128)S(1)}) custom-call(bf16[8,32,1152]{2,1,0:T(8,128)(2,1)S(1)} %all-to-all-done.4.gf_ref, bf16[64,256]{1,0:T(8,128)(2,1)S(1)} %bitcast.21, bf16[8,256,256]{2,1,0:T(8,128)(2,1)S(1)} %all-to-all-done.2.both_ref.x_ref, s32[1,256]{1,0:T(1,128)S(1)} %bitcast.27, ...), custom_call_target="tpu_custom_call" | custom-call | bytes 22140000 | tf_op jit(solution)/shard_map/finish_home/pallas_call | solution.py:636
  165.4 4.7 %assemble.1 = bf16[32,512,128]{2,1,0:T(8,128)(2,1)} custom-call(bf16[32,64,128]{2,1,0:T(8,128)(2,1)S(1)} %couple.1.refs_0_, bf16[32,64,128]{2,1,0:T(8,128)(2,1)S(1)} %collective-permute-done.18.refs_1_, bf16[16,64,128]{2,1,0:T(8,128)(2,1)} %collective-permute-done.20.refs_2_, bf16[16,64,128]{2,1,0:T(8,128)(2,1)} %collective-permute-done.21.refs_3_, ...), custom_call_target="tpu_custom_call" | custom-call | bytes 18450000 | tf_op jit(solution)/shard_map/assemble/pallas_call | solution.py:387
  (121 shorter events, 52.7 us)
Async XLA Ops:
  0.7 15.7 %all-to-all-start = ((bf16[8,4,32,256]{3,2,1,0:T(8,128)(2,1)}), bf16[8,4,32,256]{3,2,1,0:T(8,128)(2,1)S(1)}, u32[]{:S(2)}, u32[]{:S(2)}) async-start(bf16[8,4,32,256]{3,2,1,0:T(8,128)(2,1)} %bitcast.29), calls=%async_computation | async-start | bytes 1048576 | tf_op jit(solution)/shard_map/all_to_all | solution.py:734
  17.2 11.3 %collective-permute-start.2 = (bf16[256,512]{1,0:T(8,128)(2,1)}, bf16[256,512]{1,0:T(8,128)(2,1)S(1)}, u32[]{:S(2)}, u32[]{:S(2)}) collective-permute-start(bf16[256,512]{1,0:T(8,128)(2,1)} %get-tuple-element.29.refs_0_), channel_id=1, source_target_pairs={{0,8},{4,12},{8,0},{12,4},{1,9},{5,13},{9,1},{13,5},{2,10},{6,14},... | collective-permute-start | bytes 786440 | tf_op jit(solution)/shard_map/ppermute | solution.py:677
  18.0 10.4 %collective-permute-start.1 = (bf16[256,512]{1,0:T(8,128)(2,1)}, bf16[256,512]{1,0:T(8,128)(2,1)S(1)}, u32[]{:S(2)}, u32[]{:S(2)}) collective-permute-start(bf16[256,512]{1,0:T(8,128)(2,1)} %get-tuple-element.29.refs_0_), channel_id=1, source_target_pairs={{0,2},{2,0},{1,3},{3,1},{4,6},{6,4},{5,7},{7,5},{8,10},{10,8},{9,1... | collective-permute-start | bytes 786440 | tf_op jit(solution)/shard_map/ppermute | solution.py:674
  18.6 15.8 %collective-permute-start.7 = (bf16[256,512]{1,0:T(8,128)(2,1)}, bf16[256,512]{1,0:T(8,128)(2,1)}, u32[]{:S(2)}, u32[]{:S(2)}) collective-permute-start(bf16[256,512]{1,0:T(8,128)(2,1)} %get-tuple-element.29.refs_0_), channel_id=1, source_target_pairs={{0,4},{4,8},{8,12},{12,0},{1,5},{5,9},{9,13},{13,1},{2,6},{6,10},{... | collective-permute-start | bytes 786440 | tf_op jit(solution)/shard_map/ppermute | solution.py:675
  20.0 14.4 %collective-permute-start.6 = (bf16[256,512]{1,0:T(8,128)(2,1)}, bf16[256,512]{1,0:T(8,128)(2,1)}, u32[]{:S(2)}, u32[]{:S(2)}) collective-permute-start(bf16[256,512]{1,0:T(8,128)(2,1)} %get-tuple-element.29.refs_0_), channel_id=1, source_target_pairs={{0,12},{4,0},{8,4},{12,8},{1,13},{5,1},{9,5},{13,9},{2,14},{6,2},{... | collective-permute-start | bytes 786440 | tf_op jit(solution)/shard_map/ppermute | solution.py:676
  29.8 14.8 %collective-permute-start.4 = (bf16[256,512]{1,0:T(8,128)(2,1)}, bf16[256,512]{1,0:T(8,128)(2,1)S(1)}, u32[]{:S(2)}, u32[]{:S(2)}) collective-permute-start(bf16[256,512]{1,0:T(8,128)(2,1)} %get-tuple-element.31.refs_0_), channel_id=1, source_target_pairs={{0,2},{2,0},{1,3},{3,1},{4,6},{6,4},{5,7},{7,5},{8,10},{10,8},{9,1... | collective-permute-start | bytes 786440 | tf_op jit(solution)/shard_map/ppermute | solution.py:682
  31.2 13.4 %collective-permute-start.5 = (bf16[256,512]{1,0:T(8,128)(2,1)}, bf16[256,512]{1,0:T(8,128)(2,1)S(1)}, u32[]{:S(2)}, u32[]{:S(2)}) collective-permute-start(bf16[256,512]{1,0:T(8,128)(2,1)} %get-tuple-element.32.refs_3_), channel_id=1, source_target_pairs={{0,4},{4,8},{8,12},{12,0},{1,5},{5,9},{9,13},{13,1},{2,6},{6,10},{... | collective-permute-start | bytes 786440 | tf_op jit(solution)/shard_map/ppermute | solution.py:680
  31.2 13.4 %collective-permute-start.3 = (bf16[256,512]{1,0:T(8,128)(2,1)}, bf16[256,512]{1,0:T(8,128)(2,1)S(1)}, u32[]{:S(2)}, u32[]{:S(2)}) collective-permute-start(bf16[256,512]{1,0:T(8,128)(2,1)} %get-tuple-element.32.refs_3_), channel_id=1, source_target_pairs={{0,12},{4,0},{8,4},{12,8},{1,13},{5,1},{9,5},{13,9},{2,14},{6,2},{... | collective-permute-start | bytes 786440 | tf_op jit(solution)/shard_map/ppermute | solution.py:681
  49.3 20.7 %all-to-all-start.1 = ((bf16[64,16,256]{2,1,0:T(8,128)(2,1)}), bf16[64,16,256]{2,1,0:T(8,128)(2,1)S(1)}, u32[]{:S(2)}, u32[]{:S(2)}) async-start(bf16[64,16,256]{2,1,0:T(8,128)(2,1)} %bitcast.3), calls=%async_computation.1 | async-start | bytes 1048576 | tf_op jit(solution)/shard_map/all_to_all | solution.py:753
  79.3 13.8 %collective-permute-start.11 = (bf16[128,256]{1,0:T(8,128)(2,1)S(1)}, bf16[128,256]{1,0:T(8,128)(2,1)S(1)}, u32[]{:S(2)}, u32[]{:S(2)}) collective-permute-start(bf16[128,256]{1,0:T(8,128)(2,1)S(1)} %get-tuple-element.36), channel_id=1, source_target_pairs={{0,8},{4,12},{8,0},{12,4},{1,9},{5,13},{9,1},{13,5},{2,10},{6,14},... | collective-permute-start | bytes 196616 | tf_op jit(solution)/shard_map/ppermute | solution.py:677
  84.8 19.3 %all-to-all-start.2 = ((bf16[8,256,256]{2,1,0:T(8,128)(2,1)}), bf16[8,256,256]{2,1,0:T(8,128)(2,1)S(1)}, u32[]{:S(2)}, u32[]{:S(2)}) async-start(bf16[8,256,256]{2,1,0:T(8,128)(2,1)} %get-tuple-element.34), calls=%async_computation.2 | async-start | bytes 2097152 | tf_op jit(solution)/shard_map/all_to_all | solution.py:764
  89.7 11.2 %collective-permute-start.15 = (bf16[512,256]{1,0:T(8,128)(2,1)S(1)}, bf16[512,256]{1,0:T(8,128)(2,1)S(1)}, u32[]{:S(2)}, u32[]{:S(2)}) collective-permute-start(bf16[512,256]{1,0:T(8,128)(2,1)S(1)} %constant_dynamic-update-slice_fusion.refs_0_), channel_id=1, source_target_pairs={{0,1},{1,0},{2,3},{3,2},{4,5},{5,4},{6,7},{7,6},{8,9},{9,8},{10,11... | collective-permute-start | bytes 786440 | tf_op jit(solution)/shard_map/ppermute | solution.py:763
  89.8 11.0 %collective-permute-start.14 = (bf16[128,256]{1,0:T(8,128)(2,1)S(1)}, bf16[128,256]{1,0:T(8,128)(2,1)S(1)}, u32[]{:S(2)}, u32[]{:S(2)}) collective-permute-start(bf16[128,256]{1,0:T(8,128)(2,1)S(1)} %collective-permute-done.10), channel_id=1, source_target_pairs={{0,4},{4,8},{8,12},{12,0},{1,5},{5,9},{9,13},{13,1},{2,6},{6,10},{... | collective-permute-start | bytes 196616 | tf_op jit(solution)/shard_map/ppermute | solution.py:680
  111.9 9.6 %collective-permute-start.17 = (bf16[8,128,256]{2,1,0:T(8,128)(2,1)S(1)}, bf16[8,128,256]{2,1,0:T(8,128)(2,1)S(1)}, u32[]{:S(2)}, u32[]{:S(2)}) collective-permute-start(bf16[8,128,256]{2,1,0:T(8,128)(2,1)S(1)} %get-tuple-element.39), channel_id=1, source_target_pairs={{0,1},{1,0},{2,3},{3,2},{4,5},{5,4},{6,7},{7,6},{8,9},{9,8},{10,11... | collective-permute-start | bytes 1572872 | tf_op jit(solution)/shard_map/ppermute | solution.py:767
  115.4 15.6 %collective-permute-start.19 = (bf16[32,64,128]{2,1,0:T(8,128)(2,1)S(1)}, bf16[32,64,128]{2,1,0:T(8,128)(2,1)S(1)}, u32[]{:S(2)}, u32[]{:S(2)}) collective-permute-start(bf16[32,64,128]{2,1,0:T(8,128)(2,1)S(1)} %couple.1.refs_0_), channel_id=1, source_target_pairs={{0,16},{16,32},{32,48},{48,0},{1,17},{17,33},{33,49},{49,1},{2,18}... | collective-permute-start | bytes 1572872 | tf_op jit(solution)/shard_map/ppermute | solution.py:689
  115.9 16.4 %collective-permute-start.22 = (bf16[32,64,128]{2,1,0:T(8,128)(2,1)S(1)}, bf16[32,64,128]{2,1,0:T(8,128)(2,1)}, u32[]{:S(2)}, u32[]{:S(2)}) collective-permute-start(bf16[32,64,128]{2,1,0:T(8,128)(2,1)S(1)} %couple.1.refs_0_), channel_id=1, source_target_pairs={{0,64},{64,0},{1,65},{65,1},{2,66},{66,2},{3,67},{67,3},{4,68},{68... | collective-permute-start | bytes 1572872 | tf_op jit(solution)/shard_map/ppermute | solution.py:688
  119.5 16.1 %collective-permute-start.18 = (bf16[32,64,128]{2,1,0:T(8,128)(2,1)S(1)}, bf16[32,64,128]{2,1,0:T(8,128)(2,1)S(1)}, u32[]{:S(2)}, u32[]{:S(2)}) collective-permute-start(bf16[32,64,128]{2,1,0:T(8,128)(2,1)S(1)} %couple.1.refs_0_), channel_id=1, source_target_pairs={{0,48},{16,0},{32,16},{48,32},{1,49},{17,1},{33,17},{49,33},{2,50}... | collective-permute-start | bytes 1572872 | tf_op jit(solution)/shard_map/ppermute | solution.py:690
  122.4 15.5 %all-to-all-start.3 = ((bf16[8,128,256]{2,1,0:T(8,128)(2,1)}), bf16[8,128,256]{2,1,0:T(8,128)(2,1)S(1)}, u32[]{:S(2)}, u32[]{:S(2)}) async-start(bf16[8,128,256]{2,1,0:T(8,128)(2,1)} %fold.1), calls=%async_computation.3 | async-start | bytes 1048576 | tf_op jit(solution)/shard_map/all_to_all | solution.py:771
  131.0 14.1 %collective-permute-start.20 = (bf16[16,64,128]{2,1,0:T(8,128)(2,1)S(1)}, bf16[16,64,128]{2,1,0:T(8,128)(2,1)}, u32[]{:S(2)}, u32[]{:S(2)}) collective-permute-start(bf16[16,64,128]{2,1,0:T(8,128)(2,1)S(1)} %slice.8), channel_id=1, source_target_pairs={{0,16},{16,32},{32,48},{48,0},{1,17},{17,33},{33,49},{49,1},{2,18}... | collective-permute-start | bytes 786440 | tf_op jit(solution)/shard_map/ppermute | solution.py:691
  132.3 32.0 %collective-permute-start.26 = (bf16[32,64,128]{2,1,0:T(8,128)(2,1)}, bf16[32,64,128]{2,1,0:T(8,128)(2,1)}, u32[]{:S(2)}, u32[]{:S(2)}) collective-permute-start(bf16[32,64,128]{2,1,0:T(8,128)(2,1)} %collective-permute-done.22.refs_5_), channel_id=1, source_target_pairs={{0,16},{16,32},{32,48},{48,0},{1,17},{17,33},{33,49},{49,1},{2,18}... | collective-permute-start | bytes 1572872 | tf_op jit(solution)/shard_map/ppermute | solution.py:693
  134.0 30.3 %collective-permute-start.23 = (bf16[32,64,128]{2,1,0:T(8,128)(2,1)}, bf16[32,64,128]{2,1,0:T(8,128)(2,1)}, u32[]{:S(2)}, u32[]{:S(2)}) collective-permute-start(bf16[32,64,128]{2,1,0:T(8,128)(2,1)} %collective-permute-done.22.refs_5_), channel_id=1, source_target_pairs={{0,48},{16,0},{32,16},{48,32},{1,49},{17,1},{33,17},{49,33},{2,50}... | collective-permute-start | bytes 1572872 | tf_op jit(solution)/shard_map/ppermute | solution.py:694
  136.2 21.0 %collective-permute-start.21 = (bf16[16,64,128]{2,1,0:T(8,128)(2,1)}, bf16[16,64,128]{2,1,0:T(8,128)(2,1)}, u32[]{:S(2)}, u32[]{:S(2)}) collective-permute-start(bf16[16,64,128]{2,1,0:T(8,128)(2,1)} %slice.9), channel_id=1, source_target_pairs={{0,48},{16,0},{32,16},{48,32},{1,49},{17,1},{33,17},{49,33},{2,50}... | collective-permute-start | bytes 786440 | tf_op jit(solution)/shard_map/ppermute | solution.py:692
  139.8 20.3 %all-to-all-start.4 = ((bf16[8,32,1152]{2,1,0:T(8,128)(2,1)}), bf16[8,32,1152]{2,1,0:T(8,128)(2,1)S(1)}, u32[]{:S(2)}, u32[]{:S(2)}) async-start(bf16[8,32,1152]{2,1,0:T(8,128)(2,1)} %pack_grads.1), calls=%async_computation.4 | async-start | bytes 1179648 | tf_op jit(solution)/shard_map/all_to_all | solution.py:772
  145.1 19.2 %collective-permute-start.24 = (bf16[16,64,128]{2,1,0:T(8,128)(2,1)}, bf16[16,64,128]{2,1,0:T(8,128)(2,1)}, u32[]{:S(2)}, u32[]{:S(2)}) collective-permute-start(bf16[16,64,128]{2,1,0:T(8,128)(2,1)} %collective-permute-done.20.refs_2_), channel_id=1, source_target_pairs={{0,64},{64,0},{1,65},{65,1},{2,66},{66,2},{3,67},{67,3},{4,68},{68... | collective-permute-start | bytes 786440 | tf_op jit(solution)/shard_map/ppermute | solution.py:695
  (35 other events, 232.7 us)
